TPU v7x, 512 devices: a whole 4x4x16 slice. The times are simulated.
512 devices in a mesh: arow: 16 (over z), acol: 16 (over y_lo, x, core), occ: 2 (over y_hi).
Axes of the slice: x: 4, y: 4 (y_hi: 2, y_lo: 2; y = y_hi * 2 + y_lo), z: 16, core: 2. Of those that a mesh axis runs over, the one named last changes fastest.
Arguments:
- factors: bfloat16 [16, 4096, 3072], P('occ', ('arow', 'acol')), may hold values from -0.5 to 0.5
- occ_energies: float32 [300], replicated, may hold values from -1.2 to -0.3
- virt_energies: float32 [3072], replicated, may hold values from 0.1 to 4
- freq_grid: float32 [32], replicated, may hold values from 0.05 to 20
- occ_index: int32 [16], P('occ'), may hold values from 0 to 299
- virt_index: int32 [3072], replicated, may hold values from 0 to 3071
- freq_index: int32 [1], replicated, may hold values from 0 to 31
Outputs:
- response: float32 [4096, 4096], P('arow', 'acol')
All inputs are finite; a program needn't handle non-finite values.
Results may differ from a plain program's by a relative error of at most 0.00085.
Values may be sent and summed in bfloat16 or wider, within the bound.
No kernel may reach another device: no remote copies, remote signals or barrier semaphores. Data moves between devices by JAX's collectives and lax.ppermute only.
A program may use at most 64 MiB of HBM per device.

v0:
```python
import jax
import jax.numpy as jnp
from jax import lax
from jax.sharding import PartitionSpec as P


def lookup(table, indices):
    positions = jnp.arange(table.shape[0], dtype=jnp.int32)
    hits = indices[:, None] == positions[None, :]
    return jnp.sum(jnp.where(hits, table[None, :], jnp.float32(0.0)), axis=1)


def body(factors, occ_energies, virt_energies, freq_grid, occ_index, virt_index, freq_index):
    regrouped = lax.all_to_all(factors, "acol", split_axis=2, concat_axis=1, tiled=True)
    virt_count = regrouped.shape[2]
    column = lax.axis_index("acol")
    own_virtual = lax.dynamic_slice_in_dim(virt_index, column * virt_count, virt_count)
    virt_level = lookup(virt_energies, own_virtual)
    occ_level = lookup(occ_energies, occ_index)
    frequency = lookup(freq_grid, freq_index)[0]
    excitation = virt_level[None, :] - occ_level[:, None]
    weight = -4.0 * excitation / (excitation * excitation + frequency * frequency)
    scaled = (regrouped.astype(jnp.float32) * weight[:, None, :]).astype(jnp.bfloat16)
    partial_rows = jnp.einsum(
        "wpa,wqa->pq",
        scaled,
        lax.all_gather(regrouped, "arow", axis=1, tiled=True),
        preferred_element_type=jnp.float32,
    )
    block = lax.psum_scatter(partial_rows, "acol", scatter_dimension=1, tiled=True)
    return lax.psum(block, "occ")


def solution(mesh):
    return jax.shard_map(
        body,
        mesh=mesh,
        in_specs=(P("occ", ("arow", "acol"), None), P(), P(), P(), P("occ"), P(), P()),
        out_specs=P("arow", "acol"),
        check_vma=False,
    )
```

profile of v0, /device:TPU:1, one launch (start us, length us, event | category | flops | bytes accessed | tf_op | source)
XLA Modules:
  0.0 363.5 jit_solution(11091246879435447341)
XLA Ops:
  6.5 0.0 all-gather.2.cloned.1.call-start
  6.5 6.4 %copy.16 = bf16[8,16,3072]{1,0,2:T(8,128)(2,1)} copy(bf16[8,16,3072]{2,1,0:T(8,128)(2,1)} %param.7) | data formatting | bytes 1572864 | tf_op args[0]
  13.0 8.9 %reshape.40 = bf16[16,2,12288]{2,1,0:T(2,128)(2,1)S(1)} reshape(bf16[3072,8,16]{2,1,0:T(8,128)(2,1)} %bitcast.12) | data formatting | bytes 1572864
  21.9 22.2 %all_to_all.18 = bf16[16,2,12288]{2,1,0:T(2,128)(2,1)S(1)} all-to-all(bf16[16,2,12288]{2,1,0:T(2,128)(2,1)S(1)} %reshape.40), channel_id=1, replica_groups=mesh['arow'=16,'acol'=16,'occ'=2] {'acol'}, dimensions={0} | all-to-all | bytes 1572864 | tf_op jit(solution)/shard_map/all_to_all | solution.py:14
  44.1 5.6 %reshape.41 = bf16[3072,8,16]{2,1,0:T(8,128)(2,1)} reshape(bf16[16,2,12288]{2,1,0:T(2,128)(2,1)S(1)} %all_to_all.18) | data formatting | bytes 1572864
  49.7 0.0 copy-start.3
  49.7 0.0 copy-start.1
  49.7 0.0 copy-start.2
  49.7 0.0 copy-start
  49.7 6.5 %copy.17 = bf16[8,16,16,192]{3,1,2,0:T(8,128)(2,1)S(1)} copy(bf16[8,16,16,192]{1,0,3,2:T(8,128)(2,1)} %bitcast.11) | data formatting | bytes 1572864 | tf_op jit(solution)/shard_map/all_to_all | solution.py:14
  56.2 1.3 copy.18
  57.5 0.0 all-gather.2.cloned.1.call-update
  57.6 0.0 reduce-scatter.2.cloned.1.call-start
  58.3 0.0 copy-done.3
  58.3 0.7 fusion.3
  60.3 0.8 dynamic_slice.3
  61.1 0.0 copy-done.1
  61.1 0.0 copy-done.2
  61.1 0.2 select_reduce_fusion.1
  61.3 0.0 copy-done
  61.3 0.4 select_reduce_fusion
  61.7 0.1 fusion.1
  61.8 157.7 %all-gather.2.cloned.1.call-done = bf16[8,4096,192]{1,2,0:T(8,128)(2,1)} async-done(((bf16[8,256,192]{1,2,0:T(8,128)(2,1)}), bf16[8,4096,192]{1,2,0:T(8,128)(2,1)}) %all-gather.2.cloned.1.call-update) | async-done | bytes 12582928 | tf_op jit(solution)/shard_map/all_gather | solution.py:27
  219.5 9.6 %convolution_bitcast_fusion = f32[256,4096]{1,0:T(8,128)} fusion(bf16[8,4096,192]{1,2,0:T(8,128)(2,1)} %all-gather.2.cloned.1.call-done, bf16[8,256,192]{2,1,0:T(8,128)(2,1)S(1)} %bitcast.14, f32[8,192]{1,0:T(8,128)S(1)} %fusion.1), kind=kOutput, calls=%fused_computation | convolution fusion | flops 3222405120 | bytes 17569792 | tf_op jit(solution)/shard_map/wpa,wqa->pq/dot_general | solution.py:24
  229.1 0.0 reduce-scatter.2.cloned.1.call-update
  229.1 0.0 all-reduce.2.cloned.1.call-start
  229.2 75.4 %reduce-scatter.2.cloned.1.call-done = f32[256,256]{1,0:T(8,128)} async-done(((f32[256,4096]{1,0:T(8,128)}), f32[256,256]{1,0:T(8,128)}) %reduce-scatter.2.cloned.1.call-update) | async-done | bytes 262160 | tf_op jit(solution)/shard_map/reduce_scatter | solution.py:30
  304.6 0.0 all-reduce.2.cloned.1.call-update
  304.6 50.7 %all-reduce.2.cloned.1.call-done = f32[256,256]{1,0:T(8,128)} async-done(((f32[256,256]{1,0:T(8,128)}), f32[256,256]{1,0:T(8,128)}) %all-reduce.2.cloned.1.call-update) | async-done | bytes 262160 | tf_op jit(solution)/shard_map/psum | solution.py:31
  355.3 1.7 copy.23
Async XLA Ops:
  6.5 212.9 %all-gather.2.cloned.1.call-start = ((), (), s32[]{:S(2)}) async-start(), calls=%async_computation.2 | async-start | bytes 13369344 | tf_op jit(solution)/shard_map/all_gather | solution.py:27
  49.7 8.5 %copy-start.3 = (f32[32]{0:T(128)S(1)}, f32[32]{0:T(128)}, u32[]{:S(2)}) copy-start(f32[32]{0:T(128)} %param.10) | copy-start | bytes 388
  49.7 11.3 %copy-start.1 = (f32[300]{0:T(512)S(1)}, f32[300]{0:T(512)}, u32[]{:S(2)}) copy-start(f32[300]{0:T(512)} %param.8) | copy-start | bytes 3604
  49.7 11.3 %copy-start.2 = (s32[8]{0:T(128)S(1)}, s32[8]{0:T(128)}, u32[]{:S(2)}) copy-start(s32[8]{0:T(128)} %param.11) | copy-start | bytes 100
  49.7 11.5 %copy-start = (f32[3072]{0:T(1024)S(1)}, f32[3072]{0:T(1024)}, u32[]{:S(2)}) copy-start(f32[3072]{0:T(1024)} %param.9) | copy-start | bytes 36868
  57.6 247.0 %reduce-scatter.2.cloned.1.call-start = ((), (), s32[]{:S(2)}) async-start(), calls=%async_computation.3 | async-start | bytes 4456448 | tf_op jit(solution)/shard_map/reduce_scatter | solution.py:30
  229.1 126.1 %all-reduce.2.cloned.1.call-start = ((), (), s32[]{:S(2)}) async-start(), calls=%async_computation.4 | async-start | bytes 524288 | tf_op jit(solution)/shard_map/psum | solution.py:31
Sparse Core Ops, SparseCore 0:
  57.7 161.7 all-gather.1
  229.2 75.2 reduce-scatter.1
  307.4 47.7 all-reduce.1
where the time goes:
time: 364 us; the launch traced here: 363 us
  waiting for transfers between devices  284 us (78%)
  local copies, waits for them, and re-layouts  31.3 us (9%)
  blocking collectives  22.2 us (6%)
  between operations  15.1 us (4%)
  matrix products  9.62 us (3%)
    all_gather x1, waiting for transfers between devices, body(): lax.all_gather(regrouped, 'arow', axis=1, tiled=True)  158 us
    reduce_scatter x1, waiting for transfers between devices, body(): lax.psum_scatter(partial_rows, 'acol', scatter_dimension=1, tiled=True)  75.4 us
    psum x1, waiting for transfers between devices, body(): return lax.psum(block, 'occ')  50.7 us
    unnamed x12, local copies, waits for them, and re-layouts  22.7 us
    all_to_all x1, blocking collectives, body(): lax.all_to_all(factors, 'acol', split_axis=2, concat_axis=1, tiled=True)  22.2 us
    dot_general x1, matrix products, body(): jnp.einsum('wpa,wqa->pq', scaled, lax.all_gather(regrouped, 'arow', axis=...  9.62 us
    all_to_all x2, local copies, waits for them, and re-layouts, body(): lax.all_to_all(factors, 'acol', split_axis=2, concat_axis=1, tiled=True)  7.8 us
  transfers between devices with their start and end apart: 3, of which 3 were waited for; matrix products, arithmetic and copies ran while one was open for 1% of the time, Pallas kernels for 0%

commit v1 on v0

v1 whole, which is shorter than its diff:
```python
import functools

import jax
import jax.numpy as jnp
from jax import lax
from jax.experimental import pallas as pl
from jax.experimental.pallas import tpu as pltpu
from jax.sharding import Mesh
from jax.sharding import PartitionSpec as P

AXES = ("z", "ylo", "x", "core", "yhi")
Y_RING = ("ylo", "core", "yhi")
VMEM_LIMIT = 56 * 1024 * 1024


def lookup(table, indices):
    positions = jnp.arange(table.shape[0], dtype=jnp.int32)
    hits = indices[:, None] == positions[None, :]
    return jnp.sum(jnp.where(hits, table[None, :], jnp.float32(0.0)), axis=1)


def pack_kernel(src, dst):
    half = src.shape[2] // 2
    dst[0] = src[0, :, :half]
    dst[1] = src[0, :, half:]


def pack(factors):
    orbitals, rows, virt = factors.shape
    return pl.pallas_call(
        pack_kernel,
        grid=(orbitals,),
        in_specs=[pl.BlockSpec((1, rows, virt), lambda w: (w, 0, 0))],
        out_specs=pl.BlockSpec((2, rows, virt // 2), lambda w: (w, 0, 0)),
        out_shape=jax.ShapeDtypeStruct((2 * orbitals, rows, virt // 2), factors.dtype),
    )(factors)


def product_kernel(place, weight, p0, p1, p2, p3, q00, q01, q10, q11, out, left, right):
    step = pl.program_id(0)
    x, ylo, yhi = place[0], place[1], place[2]
    rows, depth = p0.shape
    planes = rows // 16

    @pl.when(step == 0)
    def _():
        for shift, block in enumerate((p0, p1, p2, p3)):
            at = lax.rem(x + 4 - shift, 4)

            def scale(r, carry, block=block, at=at):
                chunk = block[pl.ds(pl.multiple_of(r * 16, 16), 16), :]
                left[r, at] = (chunk.astype(jnp.float32) * weight[...]).astype(jnp.bfloat16)
                return carry

            lax.fori_loop(0, planes, scale, 0)
        for bits, block in (((0, 0), q00), ((0, 1), q01), ((1, 0), q10), ((1, 1), q11)):
            at = (ylo ^ bits[1]) * 2 + (yhi ^ bits[0])

            def move(r, carry, block=block, at=at):
                right[r, at] = block[pl.ds(pl.multiple_of(r * 16, 16), 16), :]
                return carry

            lax.fori_loop(0, planes, move, 0)

    columns = right[pl.ds(step * 4, 4)].reshape(256, depth)
    low = lax.broadcasted_iota(jnp.int32, (32, 128), 1) < 64

    def tile(m, carry):
        block = left[pl.ds(m * 4, 4)].reshape(256, depth)
        total = lax.dot_general(
            block, columns, (((1,), (1,)), ((), ())), preferred_element_type=jnp.float32
        )
        for r in range(4):
            for pair in range(2):
                lanes = slice(pair * 128, pair * 128 + 128)
                first = total[r * 64 : r * 64 + 32, lanes]
                second = total[r * 64 + 32 : r * 64 + 64, lanes]
                out[m * 4 + r, 2 * pair] = jnp.where(low, first, pltpu.roll(second, 64, 1))
                out[m * 4 + r, 2 * pair + 1] = jnp.where(low, pltpu.roll(first, 64, 1), second)
        return carry

    lax.fori_loop(0, 4, tile, 0)


def product(place, weight, p_blocks, q_blocks):
    rows, depth = p_blocks[0].shape
    whole = pl.BlockSpec(memory_space=pltpu.VMEM)
    return pl.pallas_call(
        product_kernel,
        grid=(4,),
        in_specs=[pl.BlockSpec(memory_space=pltpu.SMEM)] + [whole] * 9,
        out_specs=pl.BlockSpec((16, 4, 32, 128), lambda n: (0, n, 0, 0)),
        out_shape=jax.ShapeDtypeStruct((16, 16, 32, 128), jnp.float32),
        scratch_shapes=[pltpu.VMEM((16, 4, 16, depth), jnp.bfloat16)] * 2,
        compiler_params=pltpu.CompilerParams(vmem_limit_bytes=VMEM_LIMIT),
        cost_estimate=pl.CostEstimate(
            flops=2 * 1024 * 1024 * depth, bytes_accessed=10 * 1024 * 1024, transcendentals=0
        ),
    )(place, weight, *p_blocks, *q_blocks)


def collect_kernel(parts, out):
    lane = lax.broadcasted_iota(jnp.int32, (32, 128), 1) // 32
    for ylo in range(2):
        sums = [parts[ylo * 8 + x * 2] + parts[ylo * 8 + x * 2 + 1] for x in range(4)]
        for high in range(2):
            for column in range(2):
                start = high * 64 + column * 32
                total = jnp.zeros((32, 128), jnp.float32)
                for x in range(4):
                    shift = (x * 32 - start) % 128
                    moved = pltpu.roll(sums[x], shift, 1) if shift else sums[x]
                    total = jnp.where(lane == x, moved, total)
                lanes = slice(column * 128, column * 128 + 128)
                out[ylo * 4 + high * 2, :, lanes] = total[:16]
                out[ylo * 4 + high * 2 + 1, :, lanes] = total[16:]


def collect(parts):
    return pl.pallas_call(
        collect_kernel, out_shape=jax.ShapeDtypeStruct((8, 16, 256), jnp.float32)
    )(parts)


def merge_kernel(place, mine, other, out):
    yhi = place[2]
    for group in range(8):
        a, b = mine[group], other[group]
        out[pl.ds(group * 32, 16), :] = jnp.where(yhi == 0, a, b)
        out[pl.ds(group * 32 + 16, 16), :] = jnp.where(yhi == 0, b, a)


def merge(place, mine, other):
    whole = pl.BlockSpec(memory_space=pltpu.VMEM)
    return pl.pallas_call(
        merge_kernel,
        in_specs=[pl.BlockSpec(memory_space=pltpu.SMEM), whole, whole],
        out_specs=whole,
        out_shape=jax.ShapeDtypeStruct((256, 256), jnp.float32),
    )(place, mine, other)


def ring_permutation(s, t):
    index = lambda ylo, core, yhi: (ylo * 2 + core) * 2 + yhi
    return [
        (index(ylo, core, yhi), index(ylo ^ t, yhi, core ^ s))
        for ylo in range(2)
        for core in range(2)
        for yhi in range(2)
    ]


def body(factors, occ_energies, virt_energies, freq_grid, occ_index, virt_index, freq_index):
    z, ylo, x, core, yhi = (lax.axis_index(a) for a in AXES)
    place = jnp.stack([x, ylo, yhi]).astype(jnp.int32)
    own_index = lax.ppermute(occ_index, Y_RING, ring_permutation(0, 0))
    planes = lax.all_to_all(pack(factors), "z", split_axis=0, concat_axis=0, tiled=True)
    depth = planes.shape[2]
    rows = planes.reshape(-1, depth)

    own_virtual = lax.dynamic_slice_in_dim(virt_index, (z % 2) * depth, depth)
    own_occupied = lax.dynamic_slice_in_dim(own_index, z // 2, 1)
    excitation = lookup(virt_energies, own_virtual) - lookup(occ_energies, own_occupied)
    frequency = lookup(freq_grid, freq_index)[0]
    weight = -4.0 * excitation / (excitation * excitation + frequency * frequency)

    q_blocks = [
        lax.ppermute(rows, Y_RING, ring_permutation(s, t)) for s, t in ((0, 0), (0, 1), (1, 0), (1, 1))
    ]
    own = q_blocks[0]
    p_blocks = [own] + [
        lax.ppermute(own, "x", [(i, (i + shift) % 4) for i in range(4)]) for shift in (1, 2, 3)
    ]
    partial = product(place, weight[None, :], p_blocks, q_blocks)
    plane = lax.psum_scatter(partial, "z", scatter_dimension=0, tiled=True)[0]
    parts = lax.all_to_all(plane, ("ylo", "x", "core"), split_axis=0, concat_axis=0, tiled=True)
    mine = collect(parts)
    other = lax.ppermute(mine, "yhi", [(0, 1), (1, 0)])
    return merge(place, mine, other)


def solution(mesh):
    fine = Mesh(mesh.devices.reshape(16, 2, 4, 2, 2), AXES)
    columns = ("ylo", "x", "core")
    return jax.shard_map(
        body,
        mesh=fine,
        in_specs=(P("yhi", ("z",) + columns, None), P(), P(), P(), P("yhi"), P(), P()),
        out_specs=P("z", columns),
        check_vma=False,
    )
```

time: 364 us -> 253 us (0.70)
  waiting for transfers between devices: 284 us -> 90.6 us
  blocking collectives: 22.2 us -> 74.1 us
  starting transfers between devices: 0.09 us -> 38.9 us
  local copies, waits for them, and re-layouts: 31.3 us -> 3.53 us
  Pallas kernels: 0 us -> 21.4 us
  matrix products: 9.62 us -> 0 us
  other arithmetic: 1.37 us -> 7.71 us
    all_gather x1 -> x0, waiting for transfers between devices: 158 us -> none  [body(): lax.all_gather(regrouped, 'arow', axis=1, tiled=True)]
    all_to_all x1 -> x2, blocking collectives: 22.2 us -> 74.1 us  [the longest x1 50.7 us: body(): lax.all_to_all(pack(factors), 'z', split_axis=0, concat_axis=0, tiled=True)]
    psum x1 -> x0, waiting for transfers between devices: 50.7 us -> none  [body(): return lax.psum(block, 'occ')]
    ppermute x0 -> x9, starting transfers between devices: none -> 38.9 us  [the longest x4 20.9 us: body(): lax.ppermute(rows, Y_RING, ring_permutation(s, t))]
    ppermute x0 -> x9, waiting for transfers between devices: none -> 30.8 us  [the longest x3 22.4 us: body(): lax.ppermute(own, 'x', [(i, (i + shift) % 4) for i in range(4)])]
    pallas_call x0 -> x4, Pallas kernels: none -> 21.4 us  [the longest x1 12.9 us: product(): pl.pallas_call(product_kernel, grid=(4,), in_specs=[pl.BlockSpec(memory_s...]
    unnamed x12 -> x16, local copies, waits for them, and re-layouts: 22.7 us -> 1.56 us
    reduce_scatter x1, waiting for transfers between devices: 75.4 us -> 59.7 us  [body(): plane = lax.psum_scatter(partial, 'z', scatter_dimension=0, tiled=True)[0]]
  transfers between devices with their start and end apart: 3 -> 10, of which waited for: 3 -> 6; matrix products, arithmetic and copies ran while one was open for 1% -> 4% of each run, Pallas kernels for 0% -> 0%
where the time goes in v1:
time: 253 us; the launch traced here: 252 us
  waiting for transfers between devices  90.6 us (36%)
  blocking collectives  74.1 us (29%)
  starting transfers between devices  38.9 us (15%)
  Pallas kernels  21.4 us (8%)
  between operations  15.5 us (6%)
  other arithmetic  7.71 us (3%)
  local copies, waits for them, and re-layouts  3.53 us (1%)
    reduce_scatter x1, waiting for transfers between devices, body(): plane = lax.psum_scatter(partial, 'z', scatter_dimension=0, tiled=True)[0]  59.7 us
    all_to_all x1, blocking collectives, body(): lax.all_to_all(pack(factors), 'z', split_axis=0, concat_axis=0, tiled=True)  50.7 us
    all_to_all x1, blocking collectives, body(): lax.all_to_all(plane, ('ylo', 'x', 'core'), split_axis=0, concat_axis=0,...  23.4 us
    ppermute x3, waiting for transfers between devices, body(): lax.ppermute(own, 'x', [(i, (i + shift) % 4) for i in range(4)])  22.4 us
    ppermute x4, starting transfers between devices, body(): lax.ppermute(rows, Y_RING, ring_permutation(s, t))  20.9 us
    pallas_call x1, Pallas kernels, product(): pl.pallas_call(product_kernel, grid=(4,), in_specs=[pl.BlockSpec(memory_s...  12.9 us
    ppermute x3, starting transfers between devices, body(): lax.ppermute(own, 'x', [(i, (i + shift) % 4) for i in range(4)])  11.8 us
    reduce_sum x3, other arithmetic, lookup(): return jnp.sum(jnp.where(hits, table[None, :], jnp.float32(0.0)), axis=1)  6.52 us
  transfers between devices with their start and end apart: 10, of which 6 were waited for; matrix products, arithmetic and copies ran while one was open for 4% of the time, Pallas kernels for 0%

profile of v1, /device:TPU:1, one launch (start us, length us, event | category | flops | bytes accessed | tf_op | source)
XLA Modules:
  0.0 251.6 jit_solution(7322218283826114512)
XLA Ops:
  6.5 5.0 %shard_map.73 = bf16[16,16,1536]{2,1,0:T(8,128)(2,1)} custom-call(bf16[8,16,3072]{2,1,0:T(8,128)(2,1)} %src.1), custom_call_target="tpu_custom_call" | custom-call | tf_op jit(solution)/shard_map/pallas_call | solution.py:30
  11.6 50.7 %all_to_all.10 = bf16[16,16,1536]{2,1,0:T(8,128)(2,1)S(1)} all-to-all(bf16[16,16,1536]{2,1,0:T(8,128)(2,1)} %shard_map.73), channel_id=1, replica_groups=mesh['z'=16,'ylo'=2,'x'=4,'core'=2,'yhi'=2] {'z'}, dimensions={0} | all-to-all | bytes 1572864 | tf_op jit(solution)/shard_map/all_to_all | solution.py:157
  62.2 12.1 %collective-permute-start.1 = (bf16[256,1536]{1,0:T(8,128)(2,1)S(1)}, bf16[256,1536]{1,0:T(8,128)(2,1)S(1)}, u32[]{:S(2)}, u32[]{:S(2)}) collective-permute-start(bf16[256,1536]{1,0:T(8,128)(2,1)S(1)} %bitcast.8), channel_id=1, source_target_pairs={{0,0},{1,2},{2,1},{3,3},{16,16},{17,18},{18,17},{19,19},{4,4},{5,6... | collective-permute-start | bytes 2359304 | tf_op jit(solution)/shard_map/ppermute | solution.py:168
  74.3 1.9 collective-permute-start.7
  76.2 1.9 collective-permute-start
  78.8 1.3 fusion
  81.4 0.8 dynamic_slice.6
  82.2 0.6 pad_add_fusion.place
  82.8 1.9 collective-permute-start.6
  84.8 5.0 %collective-permute-start.5 = (bf16[256,1536]{1,0:T(8,128)(2,1)S(1)}, bf16[256,1536]{1,0:T(8,128)(2,1)S(1)}, u32[]{:S(2)}, u32[]{:S(2)}) collective-permute-start(bf16[256,1536]{1,0:T(8,128)(2,1)S(1)} %bitcast.11), channel_id=1, source_target_pairs={{0,16},{1,18},{2,17},{3,19},{16,0},{17,2},{18,1},{19,3},{4,20},{5,... | collective-permute-start | bytes 2359304 | tf_op jit(solution)/shard_map/ppermute | solution.py:168
  89.7 4.4 %collective-permute-start.4 = (bf16[256,1536]{1,0:T(8,128)(2,1)S(1)}, bf16[256,1536]{1,0:T(8,128)(2,1)S(1)}, u32[]{:S(2)}, u32[]{:S(2)}) collective-permute-start(bf16[256,1536]{1,0:T(8,128)(2,1)S(1)} %collective-permute-done.1.p0.q00), channel_id=1, source_target_pairs={{0,12},{4,0},{8,4},{12,8},{1,13},{5,1},{9,5},{13,9},{2,14},{6,2},{... | collective-permute-start | bytes 2359304 | tf_op jit(solution)/shard_map/ppermute | solution.py:172
  94.1 2.0 collective-permute-done
  96.2 4.6 %collective-permute-start.3 = (bf16[256,1536]{1,0:T(8,128)(2,1)S(1)}, bf16[256,1536]{1,0:T(8,128)(2,1)S(1)}, u32[]{:S(2)}, u32[]{:S(2)}) collective-permute-start(bf16[256,1536]{1,0:T(8,128)(2,1)S(1)} %collective-permute-done.1.p0.q00), channel_id=1, source_target_pairs={{0,8},{4,12},{8,0},{12,4},{1,9},{5,13},{9,1},{13,5},{2,10},{6,14},... | collective-permute-start | bytes 2359304 | tf_op jit(solution)/shard_map/ppermute | solution.py:172
  100.8 2.8 %collective-permute-done.7.q11 = bf16[256,1536]{1,0:T(8,128)(2,1)S(1)} collective-permute-done((bf16[256,1536]{1,0:T(8,128)(2,1)S(1)}, bf16[256,1536]{1,0:T(8,128)(2,1)S(1)}, u32[]{:S(2)}, u32[]{:S(2)}) %collective-permute-start.7) | collective-permute-done | bytes 786464 | tf_op jit(solution)/shard_map/ppermute | solution.py:168
  103.6 2.8 %collective-permute-start.2 = (bf16[256,1536]{1,0:T(8,128)(2,1)S(1)}, bf16[256,1536]{1,0:T(8,128)(2,1)S(1)}, u32[]{:S(2)}, u32[]{:S(2)}) collective-permute-start(bf16[256,1536]{1,0:T(8,128)(2,1)S(1)} %collective-permute-done.1.p0.q00), channel_id=1, source_target_pairs={{0,4},{4,8},{8,12},{12,0},{1,5},{5,9},{9,13},{13,1},{2,6},{6,10},{... | collective-permute-start | bytes 2359304 | tf_op jit(solution)/shard_map/ppermute | solution.py:172
  106.5 3.3 %select_reduce_fusion = f32[1536]{0:T(1024)S(1)} fusion(f32[3072]{0:T(1024)} %param.9, s32[1536]{0:T(1024)S(1)} %dynamic_slice.6), kind=kLoop, calls=%fused_computation | loop fusion | flops 14154240 | bytes 24576 | tf_op jit(solution)/shard_map/reduce_sum | solution.py:19
  109.7 0.6 dynamic_slice.7
  110.3 1.9 select_reduce_fusion.1
  112.2 0.6 add_divide_fusion
  112.8 0.6 div.25.weight
  113.5 5.7 %collective-permute-done.3.p2 = bf16[256,1536]{1,0:T(8,128)(2,1)S(1)} collective-permute-done((bf16[256,1536]{1,0:T(8,128)(2,1)S(1)}, bf16[256,1536]{1,0:T(8,128)(2,1)S(1)}, u32[]{:S(2)}, u32[]{:S(2)}) %collective-permute-start.3) | collective-permute-done | bytes 786464 | tf_op jit(solution)/shard_map/ppermute | solution.py:172
  119.1 16.8 %collective-permute-done.2.p1 = bf16[256,1536]{1,0:T(8,128)(2,1)S(1)} collective-permute-done((bf16[256,1536]{1,0:T(8,128)(2,1)S(1)}, bf16[256,1536]{1,0:T(8,128)(2,1)S(1)}, u32[]{:S(2)}, u32[]{:S(2)}) %collective-permute-start.2) | collective-permute-done | bytes 786464 | tf_op jit(solution)/shard_map/ppermute | solution.py:172
  135.9 0.9 copy-done.7
  136.8 12.9 %shard_map.74 = f32[16,16,32,128]{3,2,1,0:T(8,128)} custom-call(s32[3]{0:T(128)} %pad_add_fusion.place, f32[1,1536]{1,0:T(1,128)} %div.25.weight, bf16[256,1536]{1,0:T(8,128)(2,1)} %copy-done.1, bf16[256,1536]{1,0:T(8,128)(2,1)} %copy-done.7, bf16[256,1536]{1,0:T(8,128)(2,1)} %copy-done.6, bf16[256,1536]{1,0:T(8,128)(2,1)} %copy-done.5, ...), custom_call_target="tpu_custom_call" | custom-call | flops 3221225472 | bytes 10485760 | tf_op jit(solution)/shard_map/pallas_call | solution.py:88
  149.7 0.0 reduce-scatter.2.cloned.1.call-update
  149.7 59.7 %reduce-scatter.2.cloned.1.call-done = f32[1,16,32,128]{3,2,1,0:T(8,128)} async-done(((f32[16,16,32,128]{3,2,1,0:T(8,128)}), f32[1,16,32,128]{3,2,1,0:T(8,128)}) %reduce-scatter.2.cloned.1.call-update) | async-done | bytes 262160 | tf_op jit(solution)/shard_map/reduce_scatter | solution.py:175
  209.4 23.4 %all_to_all.11.parts = f32[16,32,128]{2,1,0:T(8,128)} all-to-all(f32[16,32,128]{2,1,0:T(8,128)} %bitcast.12), channel_id=1, replica_groups=mesh['z'=16,'ylo'=2,'x'=4,'core'=2,'yhi'=2] {'ylo','x','core'}, dimensions={0} | all-to-all | bytes 524288 | tf_op jit(solution)/shard_map/all_to_all | solution.py:176
  232.9 1.8 shard_map.75.mine
  234.6 4.2 %collective-permute-start.8 = (f32[8,16,256]{2,1,0:T(8,128)}, f32[8,16,256]{2,1,0:T(8,128)S(1)}, u32[]{:S(2)}, u32[]{:S(2)}) collective-permute-start(f32[8,16,256]{2,1,0:T(8,128)} %shard_map.75.mine), channel_id=1, source_target_pairs={{0,1},{1,0},{2,3},{3,2},{4,5},{5,4},{6,7},{7,6},{8,9},{9,8},{10,11... | collective-permute-start | bytes 393224 | tf_op jit(solution)/shard_map/ppermute | solution.py:178
  238.9 3.6 %collective-permute-done.8.other = f32[8,16,256]{2,1,0:T(8,128)S(1)} collective-permute-done((f32[8,16,256]{2,1,0:T(8,128)}, f32[8,16,256]{2,1,0:T(8,128)S(1)}, u32[]{:S(2)}, u32[]{:S(2)}) %collective-permute-start.8) | collective-permute-done | bytes 131104 | tf_op jit(solution)/shard_map/ppermute | solution.py:178
  242.4 0.6 copy-done
  243.1 1.7 shard_map.76
  (19 shorter events, 0.0 us)
Async XLA Ops:
  6.5 202.9 %reduce-scatter.2.cloned.1.call-start = ((), (), s32[]{:S(2)}) async-start(), calls=%async_computation.3 | async-start | bytes 4456448 | tf_op jit(solution)/shard_map/reduce_scatter | solution.py:175
  62.2 27.5 %collective-permute-start.1 = (bf16[256,1536]{1,0:T(8,128)(2,1)S(1)}, bf16[256,1536]{1,0:T(8,128)(2,1)S(1)}, u32[]{:S(2)}, u32[]{:S(2)}) collective-permute-start(bf16[256,1536]{1,0:T(8,128)(2,1)S(1)} %bitcast.8), channel_id=1, source_target_pairs={{0,0},{1,2},{2,1},{3,3},{16,16},{17,18},{18,17},{19,19},{4,4},{5,6... | collective-permute-start | bytes 2359304 | tf_op jit(solution)/shard_map/ppermute | solution.py:168
  74.3 29.3 %collective-permute-start.7 = (bf16[256,1536]{1,0:T(8,128)(2,1)S(1)}, bf16[256,1536]{1,0:T(8,128)(2,1)S(1)}, u32[]{:S(2)}, u32[]{:S(2)}) collective-permute-start(bf16[256,1536]{1,0:T(8,128)(2,1)S(1)} %bitcast.9), channel_id=1, source_target_pairs={{0,17},{1,19},{2,16},{3,18},{16,1},{17,3},{18,0},{19,2},{4,21},{5,... | collective-permute-start | bytes 2359304 | tf_op jit(solution)/shard_map/ppermute | solution.py:168
  76.2 19.9 %collective-permute-start = (s32[8]{0:T(128)}, s32[8]{0:T(128)S(1)}, u32[]{:S(2)}, u32[]{:S(2)}) collective-permute-start(s32[8]{0:T(128)} %param.11), channel_id=1, source_target_pairs={{0,0},{1,2},{2,1},{3,3},{16,16},{17,18},{18,17},{19,19},{4,4},{5,6... | collective-permute-start | bytes 104 | tf_op jit(solution)/shard_map/ppermute | solution.py:156
  82.8 30.6 %collective-permute-start.6 = (bf16[256,1536]{1,0:T(8,128)(2,1)S(1)}, bf16[256,1536]{1,0:T(8,128)(2,1)S(1)}, u32[]{:S(2)}, u32[]{:S(2)}) collective-permute-start(bf16[256,1536]{1,0:T(8,128)(2,1)S(1)} %bitcast.10), channel_id=1, source_target_pairs={{0,1},{1,3},{2,0},{3,2},{16,17},{17,19},{18,16},{19,18},{4,5},{5,7... | collective-permute-start | bytes 2359304 | tf_op jit(solution)/shard_map/ppermute | solution.py:168
  84.8 28.7 %collective-permute-start.5 = (bf16[256,1536]{1,0:T(8,128)(2,1)S(1)}, bf16[256,1536]{1,0:T(8,128)(2,1)S(1)}, u32[]{:S(2)}, u32[]{:S(2)}) collective-permute-start(bf16[256,1536]{1,0:T(8,128)(2,1)S(1)} %bitcast.11), channel_id=1, source_target_pairs={{0,16},{1,18},{2,17},{3,19},{16,0},{17,2},{18,1},{19,3},{4,20},{5,... | collective-permute-start | bytes 2359304 | tf_op jit(solution)/shard_map/ppermute | solution.py:168
  89.7 46.2 %copy-start.1 = (bf16[256,1536]{1,0:T(8,128)(2,1)}, bf16[256,1536]{1,0:T(8,128)(2,1)S(1)}, u32[]{:S(2)}) copy-start(bf16[256,1536]{1,0:T(8,128)(2,1)S(1)} %collective-permute-done.1.p0.q00) | copy-start | bytes 2359300
  89.7 23.7 %collective-permute-start.4 = (bf16[256,1536]{1,0:T(8,128)(2,1)S(1)}, bf16[256,1536]{1,0:T(8,128)(2,1)S(1)}, u32[]{:S(2)}, u32[]{:S(2)}) collective-permute-start(bf16[256,1536]{1,0:T(8,128)(2,1)S(1)} %collective-permute-done.1.p0.q00), channel_id=1, source_target_pairs={{0,12},{4,0},{8,4},{12,8},{1,13},{5,1},{9,5},{13,9},{2,14},{6,2},{... | collective-permute-start | bytes 2359304 | tf_op jit(solution)/shard_map/ppermute | solution.py:172
  96.2 23.0 %collective-permute-start.3 = (bf16[256,1536]{1,0:T(8,128)(2,1)S(1)}, bf16[256,1536]{1,0:T(8,128)(2,1)S(1)}, u32[]{:S(2)}, u32[]{:S(2)}) collective-permute-start(bf16[256,1536]{1,0:T(8,128)(2,1)S(1)} %collective-permute-done.1.p0.q00), channel_id=1, source_target_pairs={{0,8},{4,12},{8,0},{12,4},{1,9},{5,13},{9,1},{13,5},{2,10},{6,14},... | collective-permute-start | bytes 2359304 | tf_op jit(solution)/shard_map/ppermute | solution.py:172
  103.6 32.3 %copy-start.2 = (bf16[256,1536]{1,0:T(8,128)(2,1)}, bf16[256,1536]{1,0:T(8,128)(2,1)S(1)}, u32[]{:S(2)}) copy-start(bf16[256,1536]{1,0:T(8,128)(2,1)S(1)} %collective-permute-done.7.q11) | copy-start | bytes 2359300
  103.6 32.3 %collective-permute-start.2 = (bf16[256,1536]{1,0:T(8,128)(2,1)S(1)}, bf16[256,1536]{1,0:T(8,128)(2,1)S(1)}, u32[]{:S(2)}, u32[]{:S(2)}) collective-permute-start(bf16[256,1536]{1,0:T(8,128)(2,1)S(1)} %collective-permute-done.1.p0.q00), channel_id=1, source_target_pairs={{0,4},{4,8},{8,12},{12,0},{1,5},{5,9},{9,13},{13,1},{2,6},{6,10},{... | collective-permute-start | bytes 2359304 | tf_op jit(solution)/shard_map/ppermute | solution.py:172
  113.4 22.5 %copy-start.3 = (bf16[256,1536]{1,0:T(8,128)(2,1)}, bf16[256,1536]{1,0:T(8,128)(2,1)S(1)}, u32[]{:S(2)}) copy-start(bf16[256,1536]{1,0:T(8,128)(2,1)S(1)} %collective-permute-done.6.q10) | copy-start | bytes 2359300
  113.4 22.5 %copy-start.4 = (bf16[256,1536]{1,0:T(8,128)(2,1)}, bf16[256,1536]{1,0:T(8,128)(2,1)S(1)}, u32[]{:S(2)}) copy-start(bf16[256,1536]{1,0:T(8,128)(2,1)S(1)} %collective-permute-done.5.q01) | copy-start | bytes 2359300
  113.5 22.5 %copy-start.5 = (bf16[256,1536]{1,0:T(8,128)(2,1)}, bf16[256,1536]{1,0:T(8,128)(2,1)S(1)}, u32[]{:S(2)}) copy-start(bf16[256,1536]{1,0:T(8,128)(2,1)S(1)} %collective-permute-done.4.p3) | copy-start | bytes 2359300
  119.1 16.8 %copy-start.6 = (bf16[256,1536]{1,0:T(8,128)(2,1)}, bf16[256,1536]{1,0:T(8,128)(2,1)S(1)}, u32[]{:S(2)}) copy-start(bf16[256,1536]{1,0:T(8,128)(2,1)S(1)} %collective-permute-done.3.p2) | copy-start | bytes 2359300
  135.9 0.9 copy-start.7
  234.6 7.8 %collective-permute-start.8 = (f32[8,16,256]{2,1,0:T(8,128)}, f32[8,16,256]{2,1,0:T(8,128)S(1)}, u32[]{:S(2)}, u32[]{:S(2)}) collective-permute-start(f32[8,16,256]{2,1,0:T(8,128)} %shard_map.75.mine), channel_id=1, source_target_pairs={{0,1},{1,0},{2,3},{3,2},{4,5},{5,4},{6,7},{7,6},{8,9},{9,8},{10,11... | collective-permute-start | bytes 393224 | tf_op jit(solution)/shard_map/ppermute | solution.py:178
  242.4 0.7 copy-start
Sparse Core Ops, SparseCore 0:
  149.8 59.5 reduce-scatter.1

commit v2 on v1

v2 whole, which is shorter than its diff:
```python
import jax
import jax.numpy as jnp
from jax import lax
from jax.experimental import pallas as pl
from jax.experimental.pallas import tpu as pltpu
from jax.sharding import Mesh
from jax.sharding import PartitionSpec as P

AXES = ("z", "ylo", "x", "core", "yhi")
Y_RING = ("ylo", "core", "yhi")
VMEM_LIMIT = 56 * 1024 * 1024
CHUNKS = 1
SCALE = 5e5
FLIPS = ((0, 0), (0, 1), (1, 0), (1, 1))


def lookup(table, indices):
    positions = jnp.arange(table.shape[0], dtype=jnp.int32)
    hits = indices[:, None] == positions[None, :]
    return jnp.sum(jnp.where(hits, table[None, :], jnp.float32(0.0)), axis=1)


def pack_kernel(src, *dst):
    width = dst[0].shape[2]
    for w in range(src.shape[0]):
        for half in range(2):
            for chunk in range(len(dst)):
                start = (half * len(dst) + chunk) * width
                dst[chunk][2 * w + half] = src[w, :, start : start + width]


def pack(factors):
    orbitals, rows, virt = factors.shape
    whole = pl.BlockSpec(memory_space=pltpu.VMEM)
    shape = jax.ShapeDtypeStruct((2 * orbitals, rows, virt // (2 * CHUNKS)), factors.dtype)
    return pl.pallas_call(
        pack_kernel,
        in_specs=[whole],
        out_specs=[whole] * CHUNKS,
        out_shape=[shape] * CHUNKS,
    )(factors)


def product_kernel(place, weight, p0, p1, p3, p2_low, p2_high, *refs):
    q_blocks = refs[:4]
    keep, send, left, right = refs[4:]
    step = pl.program_id(0)
    x, ylo, yhi, core = place[0], place[1], place[2], place[3]
    planes, depth = left.shape[0], left.shape[3]

    @pl.when(step == 0)
    def _():
        for shift, block, low, high in (
            (0, p0, 0, planes),
            (1, p1, 0, planes),
            (3, p3, 0, planes),
            (2, p2_low, 0, planes // 2),
            (2, p2_high, planes // 2, planes),
        ):
            at = lax.rem(x + 4 - shift, 4)

            def scale(r, carry, block=block, at=at, low=low):
                chunk = block[pl.ds(pl.multiple_of((r - low) * 16, 16), 16), :]
                left[r, at] = (chunk.astype(jnp.float32) * weight[...]).astype(jnp.bfloat16)
                return carry

            lax.fori_loop(low, high, scale, 0)
        for (s, t), block in zip(FLIPS, q_blocks):
            at = (ylo ^ t) * 2 + (yhi ^ s)

            def move(r, carry, block=block, at=at):
                right[r, at] = block[pl.ds(pl.multiple_of(r * 16, 16), 16), :]
                return carry

            lax.fori_loop(0, planes, move, 0)

    columns = right[pl.ds(step * 4, 4)].reshape(256, depth)
    low = lax.broadcasted_iota(jnp.int32, (32, 128), 1) < 64
    total = lax.dot_general(
        left[...].reshape(planes * 64, depth),
        columns,
        (((1,), (1,)), ((), ())),
        preferred_element_type=jnp.float32,
    )
    for r in range(planes):
        for pair in range(2):
            lanes = slice(pair * 128, pair * 128 + 128)
            top = total[r * 64 : r * 64 + 32, lanes]
            bottom = total[r * 64 + 32 : r * 64 + 64, lanes]
            even = jnp.where(low, top, pltpu.roll(bottom, 64, 1))
            odd = jnp.where(low, pltpu.roll(top, 64, 1), bottom)
            for at, both in ((2 * pair, even), (2 * pair + 1, odd)):
                keep[r, at] = jnp.where(core == 0, both[:16], both[16:])
                send[r, at] = jnp.where(core == 0, both[16:], both[:16])


def product(place, weight, p_blocks, q_blocks):
    rows, depth = p_blocks[0].shape
    whole = pl.BlockSpec(memory_space=pltpu.VMEM)
    part = pl.BlockSpec((16, 4, 16, 128), lambda n: (0, n, 0, 0))
    return pl.pallas_call(
        product_kernel,
        grid=(4,),
        in_specs=[pl.BlockSpec(memory_space=pltpu.SMEM)] + [whole] * 10,
        out_specs=[part] * 2,
        out_shape=[jax.ShapeDtypeStruct((16, 16, 16, 128), jnp.float32)] * 2,
        scratch_shapes=[pltpu.VMEM((rows // 16, 4, 16, depth), jnp.bfloat16)] * 2,
        compiler_params=pltpu.CompilerParams(vmem_limit_bytes=VMEM_LIMIT),
        cost_estimate=pl.CostEstimate(
            flops=2 * 1024 * 1024 * depth, bytes_accessed=10 * 1024 * 1024, transcendentals=0
        ),
    )(place, weight, *p_blocks, *q_blocks)


def collect_kernel(parts, out):
    lane = lax.broadcasted_iota(jnp.int32, (16, 128), 1) // 32
    for ylo in range(2):
        for core in range(2):
            for high in range(2):
                for column in range(2):
                    start = high * 64 + column * 32
                    total = jnp.zeros((16, 128), jnp.float32)
                    for x in range(4):
                        shift = (x * 32 - start) % 128
                        part = parts[ylo * 8 + x * 2 + core]
                        total = jnp.where(lane == x, pltpu.roll(part, shift, 1) if shift else part, total)
                    out[ylo * 4 + high * 2 + core, :, column * 128 : column * 128 + 128] = total


def collect(parts):
    return pl.pallas_call(
        collect_kernel, out_shape=jax.ShapeDtypeStruct((8, 16, 256), jnp.float32)
    )(parts)


def merge_kernel(place, mine, other, out):
    yhi = place[2]
    for group in range(8):
        a, b = mine[group], other[group]
        out[pl.ds(group * 32, 16), :] = jnp.where(yhi == 0, a, b)
        out[pl.ds(group * 32 + 16, 16), :] = jnp.where(yhi == 0, b, a)


def merge(place, mine, other):
    whole = pl.BlockSpec(memory_space=pltpu.VMEM)
    return pl.pallas_call(
        merge_kernel,
        in_specs=[pl.BlockSpec(memory_space=pltpu.SMEM), whole, whole],
        out_specs=whole,
        out_shape=jax.ShapeDtypeStruct((256, 256), jnp.float32),
    )(place, mine, other)


def ring_permutation(s, t):
    index = lambda ylo, core, yhi: (ylo * 2 + core) * 2 + yhi
    return [
        (index(ylo, core, yhi), index(ylo ^ t, yhi, core ^ s))
        for ylo in range(2)
        for core in range(2)
        for yhi in range(2)
    ]


def body(factors, occ_energies, virt_energies, freq_grid, occ_index, virt_index, freq_index):
    z, ylo, x, core, yhi = (lax.axis_index(a) for a in AXES)
    place = jnp.stack([x, ylo, yhi, core]).astype(jnp.int32)
    own_index = lax.ppermute(occ_index, Y_RING, ring_permutation(0, 0))
    chunks = [
        lax.all_to_all(chunk, "z", split_axis=0, concat_axis=0, tiled=True) for chunk in pack(factors)
    ]
    depth = chunks[0].shape[2]
    half = depth * CHUNKS

    own_virtual = lax.dynamic_slice_in_dim(virt_index, (z % 2) * half, half)
    own_occupied = lax.dynamic_slice_in_dim(own_index, z // 2, 1)
    excitation = lookup(virt_energies, own_virtual) - lookup(occ_energies, own_occupied)
    frequency = lookup(freq_grid, freq_index)[0]
    weight = -4.0 * excitation / (excitation * excitation + frequency * frequency)

    rows = chunks[0].reshape(-1, depth)
    q_blocks = [lax.ppermute(rows, Y_RING, ring_permutation(s, t)) for s, t in FLIPS]
    own = q_blocks[0]
    up = lambda block: lax.ppermute(block, "x", [(i, (i + 1) % 4) for i in range(4)])
    down = lambda block: lax.ppermute(block, "x", [(i, (i + 3) % 4) for i in range(4)])
    below, above = up(own), down(own)
    middle = own.shape[0] // 2
    p_blocks = [own, below, above, up(below[:middle]), down(above[middle:])]
    keep, send = product(place, weight[None, :], p_blocks, q_blocks)
    total = keep + lax.ppermute(send, "core", [(0, 1), (1, 0)])
    root = jnp.sqrt(jnp.abs(total) * SCALE)
    coded = jnp.where(total < 0, -root, root).astype(jnp.float16)
    terms = lax.all_to_all(
        coded.reshape(256, 16, 128), ("z", "ylo", "x", "core"), split_axis=0, concat_axis=0, tiled=True
    )
    terms = terms.reshape(16, 16, 16, 128).astype(jnp.float32)
    parts = jnp.sum(terms * jnp.abs(terms), axis=0) * (1.0 / SCALE)
    mine = collect(parts)
    other = lax.ppermute(mine, "yhi", [(0, 1), (1, 0)])
    return merge(place, mine, other)


def solution(mesh):
    fine = Mesh(mesh.devices.reshape(16, 2, 4, 2, 2), AXES)
    columns = ("ylo", "x", "core")
    return jax.shard_map(
        body,
        mesh=fine,
        in_specs=(P("yhi", ("z",) + columns, None), P(), P(), P(), P("yhi"), P(), P()),
        out_specs=P("z", columns),
        check_vma=False,
    )
```

time: 253 us -> 219 us (0.87)
  waiting for transfers between devices: 90.6 us -> 22.5 us
  blocking collectives: 74.1 us -> 117 us
  between operations: 15.5 us -> 2.22 us
  starting transfers between devices: 38.9 us -> 47.5 us
  Pallas kernels: 21.4 us -> 15.2 us
    reduce_scatter x1 -> x0, waiting for transfers between devices: 59.7 us -> none  [body(): plane = lax.psum_scatter(partial, 'z', scatter_dimension=0, tiled=True)[0]]
    all_to_all x2, blocking collectives: 74.1 us -> 117 us  [the longest x1 66.7 us: body(): lax.all_to_all(coded.reshape(256, 16, 128), ('z', 'ylo', 'x', 'core'), sp...]
    ppermute x3 -> x5, waiting for transfers between devices: 22.4 us -> 5.99 us  [the longest x1 4.34 us: body(): total = keep + lax.ppermute(send, 'core', [(0, 1), (1, 0)])]
    ppermute x4, waiting for transfers between devices: 2.82 us -> 12.4 us  [body(): lax.ppermute(rows, Y_RING, ring_permutation(s, t))]
    ppermute x3 -> x5, starting transfers between devices: 11.8 us -> 15.7 us  [the longest x2 9.23 us: body(): lax.ppermute(block, 'x', [(i, (i + 3) % 4) for i in range(4)])]
    pallas_call x1, Pallas kernels: 12.9 us -> 9.64 us  [product(): pl.pallas_call(product_kernel, grid=(4,), in_specs=[pl.BlockSpec(memory_s...]
    pallas_call x1, Pallas kernels: 5.04 us -> 2.14 us  [pack(): pl.pallas_call(pack_kernel, in_specs=[whole], out_specs=[whole] * CHUNKS,...]
    convert_element_type x0 -> x1, other arithmetic: none -> 2.62 us  [body(): coded = jnp.where(total < 0, -root, root).astype(jnp.float16)]
  transfers between devices with their start and end apart: 10 -> 11, of which waited for: 6 -> 6; matrix products, arithmetic and copies ran while one was open for 4% -> 3% of each run, Pallas kernels for 0% -> 0%
where the time goes in v2:
time: 219 us; the launch traced here: 217 us
  blocking collectives  117 us (53%)
  starting transfers between devices  47.5 us (22%)
  waiting for transfers between devices  22.5 us (10%)
  Pallas kernels  15.2 us (7%)
  other arithmetic  9.25 us (4%)
  local copies, waits for them, and re-layouts  2.79 us (1%)
  between operations  2.22 us (1%)
    all_to_all x1, blocking collectives, body(): lax.all_to_all(coded.reshape(256, 16, 128), ('z', 'ylo', 'x', 'core'), sp...  66.7 us
    all_to_all x1, blocking collectives, body(): lax.all_to_all(chunk, 'z', split_axis=0, concat_axis=0, tiled=True)  50.7 us
    ppermute x4, starting transfers between devices, body(): lax.ppermute(rows, Y_RING, ring_permutation(s, t))  21.5 us
    ppermute x4, waiting for transfers between devices, body(): lax.ppermute(rows, Y_RING, ring_permutation(s, t))  12.4 us
    pallas_call x1, Pallas kernels, product(): pl.pallas_call(product_kernel, grid=(4,), in_specs=[pl.BlockSpec(memory_s...  9.64 us
    ppermute x2, starting transfers between devices, body(): lax.ppermute(block, 'x', [(i, (i + 3) % 4) for i in range(4)])  9.23 us
    ppermute x1, starting transfers between devices, body(): other = lax.ppermute(mine, 'yhi', [(0, 1), (1, 0)])  6.45 us
    ppermute x2, starting transfers between devices, body(): lax.ppermute(block, 'x', [(i, (i + 1) % 4) for i in range(4)])  4.6 us
  transfers between devices with their start and end apart: 11, of which 6 were waited for; matrix products, arithmetic and copies ran while one was open for 3% of the time, Pallas kernels for 0%

profile of v2, /device:TPU:1, one launch (start us, length us, event | category | flops | bytes accessed | tf_op | source)
XLA Modules:
  0.0 216.9 jit_solution(3419732511553030050)
XLA Ops:
  0.0 2.1 shard_map.73
  2.2 50.7 %all_to_all.10 = bf16[16,16,1536]{2,1,0:T(8,128)(2,1)S(1)} all-to-all(bf16[16,16,1536]{2,1,0:T(8,128)(2,1)} %shard_map.73), channel_id=1, replica_groups=mesh['z'=16,'ylo'=2,'x'=4,'core'=2,'yhi'=2] {'z'}, dimensions={0} | all-to-all | bytes 1572864 | tf_op jit(solution)/shard_map/all_to_all | solution.py:169
  52.8 12.1 %collective-permute-start.1 = (bf16[256,1536]{1,0:T(8,128)(2,1)S(1)}, bf16[256,1536]{1,0:T(8,128)(2,1)S(1)}, u32[]{:S(2)}, u32[]{:S(2)}) collective-permute-start(bf16[256,1536]{1,0:T(8,128)(2,1)S(1)} %bitcast.13), channel_id=1, source_target_pairs={{0,0},{1,2},{2,1},{3,3},{16,16},{17,18},{18,17},{19,19},{4,4},{5,6... | collective-permute-start | bytes 2359304 | tf_op jit(solution)/shard_map/ppermute | solution.py:181
  64.9 9.7 %collective-permute-done.1.p0.refs_0_ = bf16[256,1536]{1,0:T(8,128)(2,1)S(1)} collective-permute-done((bf16[256,1536]{1,0:T(8,128)(2,1)S(1)}, bf16[256,1536]{1,0:T(8,128)(2,1)S(1)}, u32[]{:S(2)}, u32[]{:S(2)}) %collective-permute-start.1) | collective-permute-done | bytes 786464 | tf_op jit(solution)/shard_map/ppermute | solution.py:181
  74.6 4.4 %collective-permute-start.3 = (bf16[256,1536]{1,0:T(8,128)(2,1)S(1)}, bf16[256,1536]{1,0:T(8,128)(2,1)S(1)}, u32[]{:S(2)}, u32[]{:S(2)}) collective-permute-start(bf16[256,1536]{1,0:T(8,128)(2,1)S(1)} %collective-permute-done.1.p0.refs_0_), channel_id=1, source_target_pairs={{0,12},{4,0},{8,4},{12,8},{1,13},{5,1},{9,5},{13,9},{2,14},{6,2},{... | collective-permute-start | bytes 2359304 | tf_op jit(solution)/shard_map/ppermute | solution.py:184
  79.0 1.9 collective-permute-start.2
  81.6 0.6 fusion.2
  83.6 1.9 collective-permute-start.8
  85.5 5.6 %collective-permute-start.7 = (bf16[256,1536]{1,0:T(8,128)(2,1)S(1)}, bf16[256,1536]{1,0:T(8,128)(2,1)S(1)}, u32[]{:S(2)}, u32[]{:S(2)}) collective-permute-start(bf16[256,1536]{1,0:T(8,128)(2,1)S(1)} %bitcast.15), channel_id=1, source_target_pairs={{0,1},{1,3},{2,0},{3,2},{16,17},{17,19},{18,16},{19,18},{4,5},{5,7... | collective-permute-start | bytes 2359304 | tf_op jit(solution)/shard_map/ppermute | solution.py:181
  91.1 1.9 collective-permute-start.6
  93.1 2.6 %select_reduce_fusion = f32[1536]{0:T(1024)S(1)} fusion(f32[3072]{0:T(1024)S(1)} %copy-done.11, s32[1536]{0:T(1024)S(1)} %dynamic_slice.6), kind=kLoop, calls=%fused_computation | loop fusion | flops 14154240 | bytes 24576 | tf_op jit(solution)/shard_map/reduce_sum | solution.py:20
  95.6 3.8 %collective-permute-start = (s32[8]{0:T(128)S(1)}, s32[8]{0:T(128)S(1)}, u32[]{:S(2)}, u32[]{:S(2)}) collective-permute-start(s32[8]{0:T(128)S(1)} %copy-done.13), channel_id=1, source_target_pairs={{0,0},{1,2},{2,1},{3,3},{16,16},{17,18},{18,17},{19,19},{4,4},{5,6... | collective-permute-start | bytes 104 | tf_op jit(solution)/shard_map/ppermute | solution.py:167
  99.5 4.9 %collective-permute-start.5 = (bf16[128,1536]{1,0:T(8,128)(2,1)S(1)}, bf16[128,1536]{1,0:T(8,128)(2,1)S(1)}, u32[]{:S(2)}, u32[]{:S(2)}) collective-permute-start(bf16[128,1536]{1,0:T(8,128)(2,1)S(1)} %slice.9), channel_id=1, source_target_pairs={{0,12},{4,0},{8,4},{12,8},{1,13},{5,1},{9,5},{13,9},{2,14},{6,2},{... | collective-permute-start | bytes 1179656 | tf_op jit(solution)/shard_map/ppermute | solution.py:184
  104.4 1.6 collective-permute-done
  106.0 2.7 %collective-permute-start.4 = (bf16[128,1536]{1,0:T(8,128)(2,1)S(1)}, bf16[128,1536]{1,0:T(8,128)(2,1)S(1)}, u32[]{:S(2)}, u32[]{:S(2)}) collective-permute-start(bf16[128,1536]{1,0:T(8,128)(2,1)S(1)} %slice.8), channel_id=1, source_target_pairs={{0,4},{4,8},{8,12},{12,0},{1,5},{5,9},{9,13},{13,1},{2,6},{6,10},{... | collective-permute-start | bytes 1179656 | tf_op jit(solution)/shard_map/ppermute | solution.py:183
  108.7 0.6 pad_add_fusion.place
  109.9 1.3 select_reduce_fusion.1
  111.1 0.6 add_divide_fusion
  112.4 2.8 %collective-permute-done.6.refs_1_ = bf16[256,1536]{1,0:T(8,128)(2,1)S(1)} collective-permute-done((bf16[256,1536]{1,0:T(8,128)(2,1)S(1)}, bf16[256,1536]{1,0:T(8,128)(2,1)S(1)}, u32[]{:S(2)}, u32[]{:S(2)}) %collective-permute-start.6) | collective-permute-done | bytes 786464 | tf_op jit(solution)/shard_map/ppermute | solution.py:181
  115.2 1.6 collective-permute-done.4.p2_low
  116.9 0.8 copy-done.10
  117.7 9.6 %shard_map.74 = (f32[16,16,16,128]{3,2,1,0:T(8,128)}, f32[16,16,16,128]{3,2,1,0:T(8,128)}) custom-call(s32[4]{0:T(128)} %pad_add_fusion.place, f32[1,1536]{1,0:T(1,128)} %div.25.weight, bf16[256,1536]{1,0:T(8,128)(2,1)} %copy-done.5, bf16[256,1536]{1,0:T(8,128)(2,1)} %copy-done.1, bf16[256,1536]{1,0:T(8,128)(2,1)} %copy-done, bf16[128,1536]{1,0:T(8,128)(2,1)} %copy-done.10, ...), custom_call_target="tpu_custom_call" | custom-call | flops 3221225472 | bytes 10485760 | tf_op jit(solution)/shard_map/pallas_call | solution.py:101
  127.3 1.9 collective-permute-start.9
  129.2 4.3 %collective-permute-done.9 = f32[16,16,16,128]{3,2,1,0:T(8,128)S(1)} collective-permute-done((f32[16,16,16,128]{3,2,1,0:T(8,128)}, f32[16,16,16,128]{3,2,1,0:T(8,128)S(1)}, u32[]{:S(2)}, u32[]{:S(2)}) %collective-permute-start.9) | collective-permute-done | bytes 2097184 | tf_op jit(solution)/shard_map/ppermute | solution.py:189
  133.5 2.6 %fusion = f16[16,16,16,128]{3,2,1,0:T(8,128)(2,1)S(1)} fusion(f32[16,16,16,128]{3,2,1,0:T(8,128)} %get-tuple-element.7, f32[16,16,16,128]{3,2,1,0:T(8,128)S(1)} %collective-permute-done.9), kind=kLoop, calls=%fused_computation.4 | loop fusion | flops 3670016 | bytes 5242880 | tf_op jit(solution)/shard_map/convert_element_type | solution.py:191
  136.2 66.7 %all_to_all.11 = f16[256,16,128]{2,1,0:T(8,128)(2,1)S(1)} all-to-all(f16[256,16,128]{2,1,0:T(8,128)(2,1)S(1)} %bitcast.11), channel_id=1, replica_groups=mesh['z'=16,'ylo'=2,'x'=4,'core'=2,'yhi'=2] {'z','ylo','x','core'}, dimensions={0} | all-to-all | bytes 2097152 | tf_op jit(solution)/shard_map/all_to_all | solution.py:192
  203.1 0.7 broadcast_multiply_fusion.parts
  203.8 1.7 shard_map.75.mine
  205.5 6.5 %collective-permute-start.10 = (f32[8,16,256]{2,1,0:T(8,128)}, f32[8,16,256]{2,1,0:T(8,128)S(1)}, u32[]{:S(2)}, u32[]{:S(2)}) collective-permute-start(f32[8,16,256]{2,1,0:T(8,128)} %shard_map.75.mine), channel_id=1, source_target_pairs={{0,1},{1,0},{2,3},{3,2},{4,5},{5,4},{6,7},{7,6},{8,9},{9,8},{10,11... | collective-permute-start | bytes 393224 | tf_op jit(solution)/shard_map/ppermute | solution.py:198
  212.0 2.6 %collective-permute-done.10.other = f32[8,16,256]{2,1,0:T(8,128)S(1)} collective-permute-done((f32[8,16,256]{2,1,0:T(8,128)}, f32[8,16,256]{2,1,0:T(8,128)S(1)}, u32[]{:S(2)}, u32[]{:S(2)}) %collective-permute-start.10) | collective-permute-done | bytes 131104 | tf_op jit(solution)/shard_map/ppermute | solution.py:198
  214.5 0.6 copy-done.2
  215.2 1.7 shard_map.76
  (37 shorter events, 1.7 us)
Async XLA Ops:
  0.0 81.6 %copy-start.12 = (f32[32]{0:T(128)S(1)}, f32[32]{0:T(128)}, u32[]{:S(2)}) copy-start(f32[32]{0:T(128)} %param.10) | copy-start | bytes 388
  0.0 83.5 %copy-start.3 = (s32[3072]{0:T(1024)S(1)}, s32[3072]{0:T(1024)}, u32[]{:S(2)}) copy-start(s32[3072]{0:T(1024)} %param.12) | copy-start | bytes 36868
  0.0 93.1 %copy-start.11 = (f32[3072]{0:T(1024)S(1)}, f32[3072]{0:T(1024)}, u32[]{:S(2)}) copy-start(f32[3072]{0:T(1024)} %param.9) | copy-start | bytes 36868
  0.0 95.6 %copy-start.13 = (s32[8]{0:T(128)S(1)}, s32[8]{0:T(128)}, u32[]{:S(2)}) copy-start(s32[8]{0:T(128)} %param.11) | copy-start | bytes 100
  0.0 109.9 %copy-start.4 = (f32[300]{0:T(512)S(1)}, f32[300]{0:T(512)}, u32[]{:S(2)}) copy-start(f32[300]{0:T(512)} %param.8) | copy-start | bytes 3604
  52.8 21.7 %collective-permute-start.1 = (bf16[256,1536]{1,0:T(8,128)(2,1)S(1)}, bf16[256,1536]{1,0:T(8,128)(2,1)S(1)}, u32[]{:S(2)}, u32[]{:S(2)}) collective-permute-start(bf16[256,1536]{1,0:T(8,128)(2,1)S(1)} %bitcast.13), channel_id=1, source_target_pairs={{0,0},{1,2},{2,1},{3,3},{16,16},{17,18},{18,17},{19,19},{4,4},{5,6... | collective-permute-start | bytes 2359304 | tf_op jit(solution)/shard_map/ppermute | solution.py:181
  74.6 42.2 %copy-start.5 = (bf16[256,1536]{1,0:T(8,128)(2,1)}, bf16[256,1536]{1,0:T(8,128)(2,1)S(1)}, u32[]{:S(2)}) copy-start(bf16[256,1536]{1,0:T(8,128)(2,1)S(1)} %collective-permute-done.1.p0.refs_0_) | copy-start | bytes 2359300
  74.6 21.0 %collective-permute-start.3 = (bf16[256,1536]{1,0:T(8,128)(2,1)S(1)}, bf16[256,1536]{1,0:T(8,128)(2,1)S(1)}, u32[]{:S(2)}, u32[]{:S(2)}) collective-permute-start(bf16[256,1536]{1,0:T(8,128)(2,1)S(1)} %collective-permute-done.1.p0.refs_0_), channel_id=1, source_target_pairs={{0,12},{4,0},{8,4},{12,8},{1,13},{5,1},{9,5},{13,9},{2,14},{6,2},{... | collective-permute-start | bytes 2359304 | tf_op jit(solution)/shard_map/ppermute | solution.py:184
  79.0 20.6 %collective-permute-start.2 = (bf16[256,1536]{1,0:T(8,128)(2,1)S(1)}, bf16[256,1536]{1,0:T(8,128)(2,1)S(1)}, u32[]{:S(2)}, u32[]{:S(2)}) collective-permute-start(bf16[256,1536]{1,0:T(8,128)(2,1)S(1)} %collective-permute-done.1.p0.refs_0_), channel_id=1, source_target_pairs={{0,4},{4,8},{8,12},{12,0},{1,5},{5,9},{9,13},{13,1},{2,6},{6,10},{... | collective-permute-start | bytes 2359304 | tf_op jit(solution)/shard_map/ppermute | solution.py:183
  83.6 28.8 %collective-permute-start.8 = (bf16[256,1536]{1,0:T(8,128)(2,1)S(1)}, bf16[256,1536]{1,0:T(8,128)(2,1)S(1)}, u32[]{:S(2)}, u32[]{:S(2)}) collective-permute-start(bf16[256,1536]{1,0:T(8,128)(2,1)S(1)} %bitcast.14), channel_id=1, source_target_pairs={{0,17},{1,19},{2,16},{3,18},{16,1},{17,3},{18,0},{19,2},{4,21},{5,... | collective-permute-start | bytes 2359304 | tf_op jit(solution)/shard_map/ppermute | solution.py:181
  85.5 26.9 %collective-permute-start.7 = (bf16[256,1536]{1,0:T(8,128)(2,1)S(1)}, bf16[256,1536]{1,0:T(8,128)(2,1)S(1)}, u32[]{:S(2)}, u32[]{:S(2)}) collective-permute-start(bf16[256,1536]{1,0:T(8,128)(2,1)S(1)} %bitcast.15), channel_id=1, source_target_pairs={{0,1},{1,3},{2,0},{3,2},{16,17},{17,19},{18,16},{19,18},{4,5},{5,7... | collective-permute-start | bytes 2359304 | tf_op jit(solution)/shard_map/ppermute | solution.py:181
  91.1 24.0 %collective-permute-start.6 = (bf16[256,1536]{1,0:T(8,128)(2,1)S(1)}, bf16[256,1536]{1,0:T(8,128)(2,1)S(1)}, u32[]{:S(2)}, u32[]{:S(2)}) collective-permute-start(bf16[256,1536]{1,0:T(8,128)(2,1)S(1)} %bitcast.16), channel_id=1, source_target_pairs={{0,16},{1,18},{2,17},{3,19},{16,0},{17,2},{18,1},{19,3},{4,20},{5,... | collective-permute-start | bytes 2359304 | tf_op jit(solution)/shard_map/ppermute | solution.py:181
  95.6 21.2 %copy-start = (bf16[256,1536]{1,0:T(8,128)(2,1)}, bf16[256,1536]{1,0:T(8,128)(2,1)S(1)}, u32[]{:S(2)}) copy-start(bf16[256,1536]{1,0:T(8,128)(2,1)S(1)} %collective-permute-done.3.p3) | copy-start | bytes 2359300
  95.6 10.3 %collective-permute-start = (s32[8]{0:T(128)S(1)}, s32[8]{0:T(128)S(1)}, u32[]{:S(2)}, u32[]{:S(2)}) collective-permute-start(s32[8]{0:T(128)S(1)} %copy-done.13), channel_id=1, source_target_pairs={{0,0},{1,2},{2,1},{3,3},{16,16},{17,18},{18,17},{19,19},{4,4},{5,6... | collective-permute-start | bytes 104 | tf_op jit(solution)/shard_map/ppermute | solution.py:167
  99.5 17.3 %copy-start.1 = (bf16[256,1536]{1,0:T(8,128)(2,1)}, bf16[256,1536]{1,0:T(8,128)(2,1)S(1)}, u32[]{:S(2)}) copy-start(bf16[256,1536]{1,0:T(8,128)(2,1)S(1)} %collective-permute-done.2.p1) | copy-start | bytes 2359300
  99.5 15.6 %collective-permute-start.5 = (bf16[128,1536]{1,0:T(8,128)(2,1)S(1)}, bf16[128,1536]{1,0:T(8,128)(2,1)S(1)}, u32[]{:S(2)}, u32[]{:S(2)}) collective-permute-start(bf16[128,1536]{1,0:T(8,128)(2,1)S(1)} %slice.9), channel_id=1, source_target_pairs={{0,12},{4,0},{8,4},{12,8},{1,13},{5,1},{9,5},{13,9},{2,14},{6,2},{... | collective-permute-start | bytes 1179656 | tf_op jit(solution)/shard_map/ppermute | solution.py:184
  106.0 10.8 %collective-permute-start.4 = (bf16[128,1536]{1,0:T(8,128)(2,1)S(1)}, bf16[128,1536]{1,0:T(8,128)(2,1)S(1)}, u32[]{:S(2)}, u32[]{:S(2)}) collective-permute-start(bf16[128,1536]{1,0:T(8,128)(2,1)S(1)} %slice.8), channel_id=1, source_target_pairs={{0,4},{4,8},{8,12},{12,0},{1,5},{5,9},{9,13},{13,1},{2,6},{6,10},{... | collective-permute-start | bytes 1179656 | tf_op jit(solution)/shard_map/ppermute | solution.py:183
  112.4 4.5 %copy-start.6 = (bf16[256,1536]{1,0:T(8,128)(2,1)}, bf16[256,1536]{1,0:T(8,128)(2,1)S(1)}, u32[]{:S(2)}) copy-start(bf16[256,1536]{1,0:T(8,128)(2,1)S(1)} %collective-permute-done.8.refs_3_) | copy-start | bytes 2359300
  112.4 4.5 %copy-start.7 = (bf16[256,1536]{1,0:T(8,128)(2,1)}, bf16[256,1536]{1,0:T(8,128)(2,1)S(1)}, u32[]{:S(2)}) copy-start(bf16[256,1536]{1,0:T(8,128)(2,1)S(1)} %collective-permute-done.7.refs_2_) | copy-start | bytes 2359300
  115.2 1.7 copy-start.8
  115.2 1.7 copy-start.9
  116.9 0.8 copy-start.10
  127.3 6.3 %collective-permute-start.9 = (f32[16,16,16,128]{3,2,1,0:T(8,128)}, f32[16,16,16,128]{3,2,1,0:T(8,128)S(1)}, u32[]{:S(2)}, u32[]{:S(2)}) collective-permute-start(f32[16,16,16,128]{3,2,1,0:T(8,128)} %get-tuple-element.8), channel_id=1, source_target_pairs={{0,2},{2,0},{1,3},{3,1},{4,6},{6,4},{5,7},{7,5},{8,10},{10,8},{9,1... | collective-permute-start | bytes 6291464 | tf_op jit(solution)/shard_map/ppermute | solution.py:189
  205.5 9.0 %collective-permute-start.10 = (f32[8,16,256]{2,1,0:T(8,128)}, f32[8,16,256]{2,1,0:T(8,128)S(1)}, u32[]{:S(2)}, u32[]{:S(2)}) collective-permute-start(f32[8,16,256]{2,1,0:T(8,128)} %shard_map.75.mine), channel_id=1, source_target_pairs={{0,1},{1,0},{2,3},{3,2},{4,5},{5,4},{6,7},{7,6},{8,9},{9,8},{10,11... | collective-permute-start | bytes 393224 | tf_op jit(solution)/shard_map/ppermute | solution.py:198
  214.5 0.6 copy-start.2

commit v3 on v0

v3 whole, which is shorter than its diff:
```python
import jax
import jax.numpy as jnp
from jax import lax
from jax.experimental import pallas as pl
from jax.experimental.pallas import tpu as pltpu
from jax.sharding import Mesh
from jax.sharding import PartitionSpec as P

AXES = ("z", "ylo", "x", "core", "yhi")
Y_RING = ("ylo", "core", "yhi")
VMEM_LIMIT = 32 * 1024 * 1024
SHIFTS = 3
SCALE = 5e5
FLIPS = ((0, 0), (0, 1), (1, 0), (1, 1))


def lookup(table, indices):
    positions = jnp.arange(table.shape[0], dtype=jnp.int32)
    hits = indices[:, None] == positions[None, :]
    return jnp.sum(jnp.where(hits, table[None, :], jnp.float32(0.0)), axis=1)


def pack_kernel(src, dst):
    width = dst.shape[2]
    for w in range(src.shape[0]):
        for half in range(2):
            dst[2 * w + half] = src[w, :, half * width : half * width + width]


def pack(factors):
    orbitals, rows, virt = factors.shape
    whole = pl.BlockSpec(memory_space=pltpu.VMEM)
    return pl.pallas_call(
        pack_kernel,
        in_specs=[whole],
        out_specs=whole,
        out_shape=jax.ShapeDtypeStruct((2 * orbitals, rows, virt // 2), factors.dtype),
    )(factors)


def product_kernel(place, weight, p0, p1, p2, q00, q01, q10, q11, keep, send, left, right):
    ylo, yhi, core = place[0], place[1], place[2]
    planes, _, _, depth = right.shape

    for shift, block in enumerate((p0, p1, p2)):

        def scale(r, carry, block=block, shift=shift):
            chunk = block[pl.ds(pl.multiple_of(r * 16, 16), 16), :]
            left[r, shift] = (chunk.astype(jnp.float32) * weight[...]).astype(jnp.bfloat16)
            return carry

        lax.fori_loop(0, planes, scale, 0)
    for (s, t), block in zip(FLIPS, (q00, q01, q10, q11)):
        at = (ylo ^ t) * 2 + (yhi ^ s)

        def move(r, carry, block=block, at=at):
            right[r, at] = block[pl.ds(pl.multiple_of(r * 16, 16), 16), :]
            return carry

        lax.fori_loop(0, planes, move, 0)

    low = lax.broadcasted_iota(jnp.int32, (8, 128), 1) < 64

    def columns(step, carry):
        total = lax.dot_general(
            left[...].reshape(planes * SHIFTS * 16, depth),
            right[pl.ds(step * 4, 4)].reshape(256, depth),
            (((1,), (1,)), ((), ())),
            preferred_element_type=jnp.float32,
        )
        for r in range(planes):
            for pair in range(2):
                for shift in range(SHIFTS):
                    start = (r * SHIFTS + shift) * 16
                    tiles = total[start : start + 16, pair * 128 : pair * 128 + 128]
                    for ref, tile in (
                        (keep, jnp.where(core == 0, tiles[:8], tiles[8:])),
                        (send, jnp.where(core == 0, tiles[8:], tiles[:8])),
                    ):
                        turned = pltpu.roll(tile, 64, 1)
                        even = jnp.where(low, tile, pltpu.roll(turned, 4, 0))
                        odd = jnp.where(low, turned, pltpu.roll(tile, 4, 0))
                        lanes = slice(shift * 128, shift * 128 + 128)
                        ref[r, step * 4 + pair * 2, :, lanes] = even[:4]
                        ref[r, step * 4 + pair * 2 + 1, :, lanes] = odd[:4]
        return carry

    lax.fori_loop(0, 4, columns, 0)


def product(place, weight, p_blocks, q_blocks):
    rows, depth = p_blocks[0].shape
    planes = rows // 16
    whole = pl.BlockSpec(memory_space=pltpu.VMEM)
    return pl.pallas_call(
        product_kernel,
        in_specs=[pl.BlockSpec(memory_space=pltpu.SMEM)] + [whole] * 8,
        out_specs=[whole] * 2,
        out_shape=[jax.ShapeDtypeStruct((planes, planes, 4, SHIFTS * 128), jnp.float32)] * 2,
        scratch_shapes=[
            pltpu.VMEM((planes, SHIFTS, 16, depth), jnp.bfloat16),
            pltpu.VMEM((planes, 4, 16, depth), jnp.bfloat16),
        ],
        compiler_params=pltpu.CompilerParams(vmem_limit_bytes=VMEM_LIMIT),
        cost_estimate=pl.CostEstimate(
            flops=2 * SHIFTS * 256 * 1024 * depth, bytes_accessed=8 * 1024 * 1024, transcendentals=0
        ),
    )(place, weight, *p_blocks, *q_blocks)


def assemble_kernel(place, mine, other, mirror_mine, mirror_other, out, mirror):
    first = place[1] == 0
    lane = lax.broadcasted_iota(jnp.int32, (4, 128), 1) // 32

    def fill(target, pair, shifts, offset):
        for a in range(2):
            for ylo in range(2):
                for row_x in range(4):
                    for core in range(2):
                        for half in range(2):
                            for column in range(2):
                                start = half * 64 + column * 32
                                total = jnp.zeros((4, 128), jnp.float32)
                                for shift in shifts:
                                    x = (row_x + shift) % 4
                                    lanes = slice((shift - offset) * 128, (shift - offset) * 128 + 128)
                                    at = ylo * 8 + x * 2 + core
                                    part = jnp.where(first == (a == 0), pair[0][at, :, lanes], pair[1][at, :, lanes])
                                    turn = (x * 32 - start) % 128
                                    part = pltpu.roll(part, turn, 1) if turn else part
                                    total = jnp.where(lane == x, part, total)
                                row = (ylo * 8 + row_x * 2 + a) * 16 + core * 8 + half * 4
                                target[pl.ds(row, 4), column * 128 : column * 128 + 128] = total

    fill(out, (mine, other), (0, 1, 2), 0)
    fill(mirror, (mirror_mine, mirror_other), (1,), 1)
    x_of = lambda axis: (lax.broadcasted_iota(jnp.int32, out.shape, axis) // 32) % 4
    mirrored = (x_of(1) - x_of(0) + 4) % 4 == 3
    out[...] = jnp.where(mirrored, mirror[...].T, out[...])


def assemble(place, *parts):
    whole = pl.BlockSpec(memory_space=pltpu.VMEM)
    return pl.pallas_call(
        assemble_kernel,
        in_specs=[pl.BlockSpec(memory_space=pltpu.SMEM)] + [whole] * 4,
        out_specs=whole,
        out_shape=jax.ShapeDtypeStruct((256, 256), jnp.float32),
        scratch_shapes=[pltpu.VMEM((256, 256), jnp.float32)],
    )(place, *parts)


def ring_permutation(s, t):
    index = lambda ylo, core, yhi: (ylo * 2 + core) * 2 + yhi
    return [
        (index(ylo, core, yhi), index(ylo ^ t, yhi, core ^ s))
        for ylo in range(2)
        for core in range(2)
        for yhi in range(2)
    ]


def transposed(yhi_flip):
    index = lambda z, c, yhi: (z * 16 + c) * 2 + yhi
    return [
        (index(z, c, yhi), index(c, z, yhi ^ yhi_flip))
        for z in range(16)
        for c in range(16)
        for yhi in range(2)
    ]


def body(factors, occ_energies, virt_energies, freq_grid, occ_index, virt_index, freq_index):
    z, ylo, x, core, yhi = (lax.axis_index(a) for a in AXES)
    place = jnp.stack([ylo, yhi, core]).astype(jnp.int32)
    own_index = lax.ppermute(occ_index, Y_RING, ring_permutation(0, 0))
    planes = lax.all_to_all(pack(factors), "z", split_axis=0, concat_axis=0, tiled=True)
    depth = planes.shape[2]
    rows = planes.reshape(-1, depth)

    own_virtual = lax.dynamic_slice_in_dim(virt_index, (z % 2) * depth, depth)
    own_occupied = lax.dynamic_slice_in_dim(own_index, z // 2, 1)
    excitation = lookup(virt_energies, own_virtual) - lookup(occ_energies, own_occupied)
    frequency = lookup(freq_grid, freq_index)[0]
    weight = -4.0 * excitation / (excitation * excitation + frequency * frequency)

    q_blocks = [lax.ppermute(rows, Y_RING, ring_permutation(s, t)) for s, t in FLIPS]
    own = q_blocks[0]
    p_blocks = [own] + [
        lax.ppermute(own, "x", [(i, (i + shift) % 4) for i in range(4)]) for shift in range(1, SHIFTS)
    ]
    keep, send = product(place, weight[None, :], p_blocks, q_blocks)
    total = keep + lax.ppermute(send, "core", [(0, 1), (1, 0)])
    root = jnp.sqrt(jnp.abs(total) * SCALE)
    coded = jnp.where(total < 0, -root, root).astype(jnp.float16)
    coded = coded.reshape(256, 4, SHIFTS * 128)
    terms = lax.all_to_all(coded, ("z", "ylo", "x", "core"), split_axis=0, concat_axis=0, tiled=True)
    terms = terms.reshape(16, 16, 4, SHIFTS * 128).astype(jnp.float32)
    mine = jnp.sum(terms * jnp.abs(terms), axis=0) * (1.0 / SCALE)
    first_shift = mine[:, :, 128:256]
    other = lax.ppermute(mine, "yhi", [(0, 1), (1, 0)])
    mirror_mine = lax.ppermute(first_shift, AXES, transposed(0))
    mirror_other = lax.ppermute(first_shift, AXES, transposed(1))
    return assemble(place, mine, other, mirror_mine, mirror_other)


def solution(mesh):
    fine = Mesh(mesh.devices.reshape(16, 2, 4, 2, 2), AXES)
    columns = ("ylo", "x", "core")
    return jax.shard_map(
        body,
        mesh=fine,
        in_specs=(P("yhi", ("z",) + columns, None), P(), P(), P(), P("yhi"), P(), P()),
        out_specs=P("z", columns),
        check_vma=False,
    )
```

time: 364 us -> 213 us (0.59)
  the two profiles are of different devices: /device:TPU:1 before, /device:TPU:7 now
where the time goes in v3:
time: 213 us
  blocking collectives  105 us (49%)
  starting transfers between devices  52.2 us (25%)
  waiting for transfers between devices  34.7 us (16%)
  Pallas kernels  9.5 us (4%)
  other arithmetic  7.23 us (3%)
    all_to_all x1, blocking collectives, body(): lax.all_to_all(coded, ('z', 'ylo', 'x', 'core'), split_axis=0, concat_axi...  55.3 us
    all_to_all x1, blocking collectives, body(): lax.all_to_all(pack(factors), 'z', split_axis=0, concat_axis=0, tiled=True)  49.8 us
    ppermute x4, starting transfers between devices, body(): lax.ppermute(rows, Y_RING, ring_permutation(s, t))  21.3 us
    ppermute x2, waiting for transfers between devices, body(): lax.ppermute(own, 'x', [(i, (i + shift) % 4) for i in range(4)])  14.4 us
    ppermute x4, waiting for transfers between devices, body(): lax.ppermute(rows, Y_RING, ring_permutation(s, t))  10.2 us
    ppermute x1, starting transfers between devices, body(): mirror_other = lax.ppermute(first_shift, AXES, transposed(1))  8.72 us
    ppermute x1, starting transfers between devices, body(): mirror_mine = lax.ppermute(first_shift, AXES, transposed(0))  6.89 us
    ppermute x2, starting transfers between devices, body(): lax.ppermute(own, 'x', [(i, (i + shift) % 4) for i in range(4)])  6.76 us
  transfers between devices with their start and end apart: 11, of which 6 were waited for; matrix products, arithmetic and copies ran while one was open for 3% of the time, Pallas kernels for 0%

profile of v3, /device:TPU:7, one launch (start us, length us, event | category | flops | bytes accessed | tf_op | source)
XLA Modules:
  0.0 212.7 jit_solution(5413411093515442575)
XLA Ops:
  0.0 2.1 shard_map.73
  2.1 49.8 %all_to_all.10 = bf16[16,16,1536]{2,1,0:T(8,128)(2,1)S(1)} all-to-all(bf16[16,16,1536]{2,1,0:T(8,128)(2,1)} %shard_map.73), channel_id=1, replica_groups=mesh['z'=16,'ylo'=2,'x'=4,'core'=2,'yhi'=2] {'z'}, dimensions={0} | all-to-all | bytes 1572864 | tf_op jit(solution)/shard_map/all_to_all | solution.py:177
  52.0 12.1 %collective-permute-start.1 = (bf16[256,1536]{1,0:T(8,128)(2,1)S(1)}, bf16[256,1536]{1,0:T(8,128)(2,1)S(1)}, u32[]{:S(2)}, u32[]{:S(2)}) collective-permute-start(bf16[256,1536]{1,0:T(8,128)(2,1)S(1)} %bitcast.12), channel_id=1, source_target_pairs={{0,0},{1,2},{2,1},{3,3},{16,16},{17,18},{18,17},{19,19},{4,4},{5,6... | collective-permute-start | bytes 2359304 | tf_op jit(solution)/shard_map/ppermute | solution.py:187
  64.1 1.9 collective-permute-start
  66.7 0.6 fusion.2
  68.4 0.1 dynamic_slice.6
  68.6 1.9 collective-permute-start.6
  70.5 5.3 %collective-permute-start.5 = (bf16[256,1536]{1,0:T(8,128)(2,1)S(1)}, bf16[256,1536]{1,0:T(8,128)(2,1)S(1)}, u32[]{:S(2)}, u32[]{:S(2)}) collective-permute-start(bf16[256,1536]{1,0:T(8,128)(2,1)S(1)} %bitcast.14), channel_id=1, source_target_pairs={{0,1},{1,3},{2,0},{3,2},{16,17},{17,19},{18,16},{19,18},{4,5},{5,7... | collective-permute-start | bytes 2359304 | tf_op jit(solution)/shard_map/ppermute | solution.py:187
  75.9 1.9 collective-permute-start.4
  77.8 3.0 %collective-permute-start.3 = (bf16[256,1536]{1,0:T(8,128)(2,1)S(1)}, bf16[256,1536]{1,0:T(8,128)(2,1)S(1)}, u32[]{:S(2)}, u32[]{:S(2)}) collective-permute-start(bf16[256,1536]{1,0:T(8,128)(2,1)S(1)} %collective-permute-done.1.p0.q00), channel_id=1, source_target_pairs={{0,8},{4,12},{8,0},{12,4},{1,9},{5,13},{9,1},{13,5},{2,10},{6,14},... | collective-permute-start | bytes 2359304 | tf_op jit(solution)/shard_map/ppermute | solution.py:190
  80.8 3.7 %collective-permute-start.2 = (bf16[256,1536]{1,0:T(8,128)(2,1)S(1)}, bf16[256,1536]{1,0:T(8,128)(2,1)S(1)}, u32[]{:S(2)}, u32[]{:S(2)}) collective-permute-start(bf16[256,1536]{1,0:T(8,128)(2,1)S(1)} %collective-permute-done.1.p0.q00), channel_id=1, source_target_pairs={{0,4},{4,8},{8,12},{12,0},{1,5},{5,9},{9,13},{13,1},{2,6},{6,10},{... | collective-permute-start | bytes 2359304 | tf_op jit(solution)/shard_map/ppermute | solution.py:190
  84.6 2.6 %select_reduce_fusion = f32[1536]{0:T(1024)S(1)} fusion(f32[3072]{0:T(1024)S(1)} %copy-done.7, s32[1536]{0:T(1024)S(1)} %dynamic_slice.6), kind=kLoop, calls=%fused_computation | loop fusion | flops 14154240 | bytes 24576 | tf_op jit(solution)/shard_map/reduce_sum | solution.py:20
  87.1 0.6 dynamic_slice.7
  87.7 1.3 select_reduce_fusion.1
  89.0 0.6 add_divide_fusion
  89.7 4.9 %collective-permute-done.6.q11 = bf16[256,1536]{1,0:T(8,128)(2,1)S(1)} collective-permute-done((bf16[256,1536]{1,0:T(8,128)(2,1)S(1)}, bf16[256,1536]{1,0:T(8,128)(2,1)S(1)}, u32[]{:S(2)}, u32[]{:S(2)}) %collective-permute-start.6) | collective-permute-done | bytes 786464 | tf_op jit(solution)/shard_map/ppermute | solution.py:187
  94.5 5.4 %collective-permute-done.4.q01 = bf16[256,1536]{1,0:T(8,128)(2,1)S(1)} collective-permute-done((bf16[256,1536]{1,0:T(8,128)(2,1)S(1)}, bf16[256,1536]{1,0:T(8,128)(2,1)S(1)}, u32[]{:S(2)}, u32[]{:S(2)}) %collective-permute-start.4) | collective-permute-done | bytes 786464 | tf_op jit(solution)/shard_map/ppermute | solution.py:187
  99.9 14.4 %collective-permute-done.2.p1 = bf16[256,1536]{1,0:T(8,128)(2,1)S(1)} collective-permute-done((bf16[256,1536]{1,0:T(8,128)(2,1)S(1)}, bf16[256,1536]{1,0:T(8,128)(2,1)S(1)}, u32[]{:S(2)}, u32[]{:S(2)}) %collective-permute-start.2) | collective-permute-done | bytes 786464 | tf_op jit(solution)/shard_map/ppermute | solution.py:190
  114.3 5.1 %shard_map.74 = (f32[16,16,4,384]{3,2,1,0:T(4,128)S(1)}, f32[16,16,4,384]{3,2,1,0:T(4,128)S(1)}) custom-call(s32[3]{0:T(128)S(1)} %pad_add_fusion.place, f32[1,1536]{1,0:T(1,128)S(1)} %div.25.weight, bf16[256,1536]{1,0:T(8,128)(2,1)S(1)} %collective-permute-done.1.p0.q00, bf16[256,1536]{1,0:T(8,128)(2,1)S(1)} %collective-permute-done.2.p1, ...), custom_call_target="tpu_custom_call" | custom-call | flops 2415919104 | bytes 8388608 | tf_op jit(solution)/shard_map/pallas_call | solution.py:95
  119.5 3.4 %collective-permute-start.7 = (f32[16,16,4,384]{3,2,1,0:T(4,128)S(1)}, f32[16,16,4,384]{3,2,1,0:T(4,128)S(1)}, u32[]{:S(2)}, u32[]{:S(2)}) collective-permute-start(f32[16,16,4,384]{3,2,1,0:T(4,128)S(1)} %get-tuple-element.8), channel_id=1, source_target_pairs={{0,2},{2,0},{1,3},{3,1},{4,6},{6,4},{5,7},{7,5},{8,10},{10,8},{9,1... | collective-permute-start | bytes 4718600 | tf_op jit(solution)/shard_map/ppermute | solution.py:193
  122.9 3.0 %collective-permute-done.7 = f32[16,16,4,384]{3,2,1,0:T(4,128)S(1)} collective-permute-done((f32[16,16,4,384]{3,2,1,0:T(4,128)S(1)}, f32[16,16,4,384]{3,2,1,0:T(4,128)S(1)}, u32[]{:S(2)}, u32[]{:S(2)}) %collective-permute-start.7) | collective-permute-done | bytes 1572896 | tf_op jit(solution)/shard_map/ppermute | solution.py:193
  125.9 1.5 fusion
  127.4 55.3 %all_to_all.11 = f16[256,4,384]{2,1,0:T(4,128)(2,1)S(1)} all-to-all(f16[256,4,384]{2,1,0:T(4,128)(2,1)S(1)} %bitcast.11), channel_id=1, replica_groups=mesh['z'=16,'ylo'=2,'x'=4,'core'=2,'yhi'=2] {'z','ylo','x','core'}, dimensions={0} | all-to-all | bytes 1572864 | tf_op jit(solution)/shard_map/all_to_all | solution.py:197
  182.7 0.5 fusion.1
  183.3 3.3 %collective-permute-start.8 = (f32[16,4,384]{2,1,0:T(4,128)S(1)}, f32[16,4,384]{2,1,0:T(4,128)S(1)}, u32[]{:S(2)}, u32[]{:S(2)}) collective-permute-start(f32[16,4,384]{2,1,0:T(4,128)S(1)} %broadcast_multiply_fusion.mine), channel_id=1, source_target_pairs={{0,1},{1,0},{2,3},{3,2},{4,5},{5,4},{6,7},{7,6},{8,9},{9,8},{10,11... | collective-permute-start | bytes 294920 | tf_op jit(solution)/shard_map/ppermute | solution.py:201
  186.6 8.7 %collective-permute-start.10 = (f32[16,4,128]{2,1,0:T(4,128)S(1)}, f32[16,4,128]{2,1,0:T(4,128)S(1)}, u32[]{:S(2)}, u32[]{:S(2)}) collective-permute-start(f32[16,4,128]{2,1,0:T(4,128)S(1)} %slice.4), channel_id=1, source_target_pairs={{0,1},{1,0},{2,33},{3,32},{4,65},{5,64},{6,97},{7,96},{8,129},{9,1... | collective-permute-start | bytes 98312 | tf_op jit(solution)/shard_map/ppermute | solution.py:203
  195.3 6.9 %collective-permute-start.9 = (f32[16,4,128]{2,1,0:T(4,128)S(1)}, f32[16,4,128]{2,1,0:T(4,128)S(1)}, u32[]{:S(2)}, u32[]{:S(2)}) collective-permute-start(f32[16,4,128]{2,1,0:T(4,128)S(1)} %slice.4), channel_id=1, source_target_pairs={{0,0},{1,1},{2,32},{3,33},{4,64},{5,65},{6,96},{7,97},{8,128},{9,1... | collective-permute-start | bytes 98312 | tf_op jit(solution)/shard_map/ppermute | solution.py:202
  202.2 1.2 collective-permute-done.10.mirror_other
  203.4 5.9 %collective-permute-done.9.mirror_mine = f32[16,4,128]{2,1,0:T(4,128)S(1)} collective-permute-done((f32[16,4,128]{2,1,0:T(4,128)S(1)}, f32[16,4,128]{2,1,0:T(4,128)S(1)}, u32[]{:S(2)}, u32[]{:S(2)}) %collective-permute-start.9) | collective-permute-done | bytes 32800 | tf_op jit(solution)/shard_map/ppermute | solution.py:202
  209.3 0.6 copy-done.4
  209.9 0.6 copy-done.2
  210.5 2.3 %shard_map.75 = f32[256,256]{1,0:T(8,128)} custom-call(s32[3]{0:T(128)} %copy-done, f32[16,4,384]{2,1,0:T(4,128)} %copy-done.1, f32[16,4,384]{2,1,0:T(4,128)} %copy-done.2, f32[16,4,128]{2,1,0:T(4,128)} %copy-done.4, f32[16,4,128]{2,1,0:T(4,128)} %copy-done.3), custom_call_target="tpu_custom_call" | custom-call | tf_op jit(solution)/shard_map/pallas_call | solution.py:144
  (27 shorter events, 0.2 us)
Async XLA Ops:
  0.0 64.0 %copy-start.9 = (s32[8]{0:T(128)S(1)}, s32[8]{0:T(128)}, u32[]{:S(2)}) copy-start(s32[8]{0:T(128)} %param.11) | copy-start | bytes 100
  0.0 66.7 %copy-start.8 = (f32[32]{0:T(128)S(1)}, f32[32]{0:T(128)}, u32[]{:S(2)}) copy-start(f32[32]{0:T(128)} %param.10) | copy-start | bytes 388
  0.0 68.4 %copy-start.5 = (s32[3072]{0:T(1024)S(1)}, s32[3072]{0:T(1024)}, u32[]{:S(2)}) copy-start(s32[3072]{0:T(1024)} %param.12) | copy-start | bytes 36868
  0.0 84.6 %copy-start.7 = (f32[3072]{0:T(1024)S(1)}, f32[3072]{0:T(1024)}, u32[]{:S(2)}) copy-start(f32[3072]{0:T(1024)} %param.9) | copy-start | bytes 36868
  0.0 87.7 %copy-start.6 = (f32[300]{0:T(512)S(1)}, f32[300]{0:T(512)}, u32[]{:S(2)}) copy-start(f32[300]{0:T(512)} %param.8) | copy-start | bytes 3604
  52.0 25.8 %collective-permute-start.1 = (bf16[256,1536]{1,0:T(8,128)(2,1)S(1)}, bf16[256,1536]{1,0:T(8,128)(2,1)S(1)}, u32[]{:S(2)}, u32[]{:S(2)}) collective-permute-start(bf16[256,1536]{1,0:T(8,128)(2,1)S(1)} %bitcast.12), channel_id=1, source_target_pairs={{0,0},{1,2},{2,1},{3,3},{16,16},{17,18},{18,17},{19,19},{4,4},{5,6... | collective-permute-start | bytes 2359304 | tf_op jit(solution)/shard_map/ppermute | solution.py:187
  64.1 16.8 %collective-permute-start = (s32[8]{0:T(128)S(1)}, s32[8]{0:T(128)S(1)}, u32[]{:S(2)}, u32[]{:S(2)}) collective-permute-start(s32[8]{0:T(128)S(1)} %copy-done.9), channel_id=1, source_target_pairs={{0,0},{1,2},{2,1},{3,3},{16,16},{17,18},{18,17},{19,19},{4,4},{5,6... | collective-permute-start | bytes 104 | tf_op jit(solution)/shard_map/ppermute | solution.py:176
  68.6 50.9 %copy-start = (s32[3]{0:T(128)}, s32[3]{0:T(128)S(1)}, u32[]{:S(2)}) copy-start(s32[3]{0:T(128)S(1)} %pad_add_fusion.place) | copy-start | bytes 40
  68.6 25.9 %collective-permute-start.6 = (bf16[256,1536]{1,0:T(8,128)(2,1)S(1)}, bf16[256,1536]{1,0:T(8,128)(2,1)S(1)}, u32[]{:S(2)}, u32[]{:S(2)}) collective-permute-start(bf16[256,1536]{1,0:T(8,128)(2,1)S(1)} %bitcast.13), channel_id=1, source_target_pairs={{0,17},{1,19},{2,16},{3,18},{16,1},{17,3},{18,0},{19,2},{4,21},{5,... | collective-permute-start | bytes 2359304 | tf_op jit(solution)/shard_map/ppermute | solution.py:187
  70.5 24.0 %collective-permute-start.5 = (bf16[256,1536]{1,0:T(8,128)(2,1)S(1)}, bf16[256,1536]{1,0:T(8,128)(2,1)S(1)}, u32[]{:S(2)}, u32[]{:S(2)}) collective-permute-start(bf16[256,1536]{1,0:T(8,128)(2,1)S(1)} %bitcast.14), channel_id=1, source_target_pairs={{0,1},{1,3},{2,0},{3,2},{16,17},{17,19},{18,16},{19,18},{4,5},{5,7... | collective-permute-start | bytes 2359304 | tf_op jit(solution)/shard_map/ppermute | solution.py:187
  75.9 24.0 %collective-permute-start.4 = (bf16[256,1536]{1,0:T(8,128)(2,1)S(1)}, bf16[256,1536]{1,0:T(8,128)(2,1)S(1)}, u32[]{:S(2)}, u32[]{:S(2)}) collective-permute-start(bf16[256,1536]{1,0:T(8,128)(2,1)S(1)} %bitcast.15), channel_id=1, source_target_pairs={{0,16},{1,18},{2,17},{3,19},{16,0},{17,2},{18,1},{19,3},{4,20},{5,... | collective-permute-start | bytes 2359304 | tf_op jit(solution)/shard_map/ppermute | solution.py:187
  77.8 22.1 %collective-permute-start.3 = (bf16[256,1536]{1,0:T(8,128)(2,1)S(1)}, bf16[256,1536]{1,0:T(8,128)(2,1)S(1)}, u32[]{:S(2)}, u32[]{:S(2)}) collective-permute-start(bf16[256,1536]{1,0:T(8,128)(2,1)S(1)} %collective-permute-done.1.p0.q00), channel_id=1, source_target_pairs={{0,8},{4,12},{8,0},{12,4},{1,9},{5,13},{9,1},{13,5},{2,10},{6,14},... | collective-permute-start | bytes 2359304 | tf_op jit(solution)/shard_map/ppermute | solution.py:190
  80.8 33.4 %collective-permute-start.2 = (bf16[256,1536]{1,0:T(8,128)(2,1)S(1)}, bf16[256,1536]{1,0:T(8,128)(2,1)S(1)}, u32[]{:S(2)}, u32[]{:S(2)}) collective-permute-start(bf16[256,1536]{1,0:T(8,128)(2,1)S(1)} %collective-permute-done.1.p0.q00), channel_id=1, source_target_pairs={{0,4},{4,8},{8,12},{12,0},{1,5},{5,9},{9,13},{13,1},{2,6},{6,10},{... | collective-permute-start | bytes 2359304 | tf_op jit(solution)/shard_map/ppermute | solution.py:190
  119.5 6.5 %collective-permute-start.7 = (f32[16,16,4,384]{3,2,1,0:T(4,128)S(1)}, f32[16,16,4,384]{3,2,1,0:T(4,128)S(1)}, u32[]{:S(2)}, u32[]{:S(2)}) collective-permute-start(f32[16,16,4,384]{3,2,1,0:T(4,128)S(1)} %get-tuple-element.8), channel_id=1, source_target_pairs={{0,2},{2,0},{1,3},{3,1},{4,6},{6,4},{5,7},{7,5},{8,10},{10,8},{9,1... | collective-permute-start | bytes 4718600 | tf_op jit(solution)/shard_map/ppermute | solution.py:193
  183.3 26.0 %copy-start.1 = (f32[16,4,384]{2,1,0:T(4,128)}, f32[16,4,384]{2,1,0:T(4,128)S(1)}, u32[]{:S(2)}) copy-start(f32[16,4,384]{2,1,0:T(4,128)S(1)} %broadcast_multiply_fusion.mine) | copy-start | bytes 294916
  183.3 26.0 %collective-permute-start.8 = (f32[16,4,384]{2,1,0:T(4,128)S(1)}, f32[16,4,384]{2,1,0:T(4,128)S(1)}, u32[]{:S(2)}, u32[]{:S(2)}) collective-permute-start(f32[16,4,384]{2,1,0:T(4,128)S(1)} %broadcast_multiply_fusion.mine), channel_id=1, source_target_pairs={{0,1},{1,0},{2,3},{3,2},{4,5},{5,4},{6,7},{7,6},{8,9},{9,8},{10,11... | collective-permute-start | bytes 294920 | tf_op jit(solution)/shard_map/ppermute | solution.py:201
  186.6 16.8 %collective-permute-start.10 = (f32[16,4,128]{2,1,0:T(4,128)S(1)}, f32[16,4,128]{2,1,0:T(4,128)S(1)}, u32[]{:S(2)}, u32[]{:S(2)}) collective-permute-start(f32[16,4,128]{2,1,0:T(4,128)S(1)} %slice.4), channel_id=1, source_target_pairs={{0,1},{1,0},{2,33},{3,32},{4,65},{5,64},{6,97},{7,96},{8,129},{9,1... | collective-permute-start | bytes 98312 | tf_op jit(solution)/shard_map/ppermute | solution.py:203
  195.3 13.9 %collective-permute-start.9 = (f32[16,4,128]{2,1,0:T(4,128)S(1)}, f32[16,4,128]{2,1,0:T(4,128)S(1)}, u32[]{:S(2)}, u32[]{:S(2)}) collective-permute-start(f32[16,4,128]{2,1,0:T(4,128)S(1)} %slice.4), channel_id=1, source_target_pairs={{0,0},{1,1},{2,32},{3,33},{4,64},{5,65},{6,96},{7,97},{8,128},{9,1... | collective-permute-start | bytes 98312 | tf_op jit(solution)/shard_map/ppermute | solution.py:202
  203.4 5.9 %copy-start.3 = (f32[16,4,128]{2,1,0:T(4,128)}, f32[16,4,128]{2,1,0:T(4,128)S(1)}, u32[]{:S(2)}) copy-start(f32[16,4,128]{2,1,0:T(4,128)S(1)} %collective-permute-done.10.mirror_other) | copy-start | bytes 98308
  209.2 0.6 copy-start.4
  209.9 0.6 copy-start.2

commit v4 on v0

v4 whole, which is shorter than its diff:
```python
import jax
import jax.numpy as jnp
from jax import lax
from jax.experimental import pallas as pl
from jax.experimental.pallas import tpu as pltpu
from jax.sharding import Mesh
from jax.sharding import PartitionSpec as P

AXES = ("z", "ylo", "x", "core", "yhi")
Y_RING = ("ylo", "core", "yhi")
VMEM_LIMIT = 32 * 1024 * 1024
SMALL_VMEM = 8 * 1024 * 1024
SHIFT_TILES = (0, 1, 3, 2)
SCALE = 5e5
FLIPS = ((0, 0), (0, 1), (1, 0), (1, 1))


def weight_kernel(occ_index, occ, freq, freq_index, virt, index, after, out):
    del after
    z = lax.axis_index("z")
    hits = index[...]
    lanes, groups = hits & 127, hits >> 7
    level = jnp.zeros(hits.shape, jnp.float32)
    for group in range(virt.shape[0]):
        table = jnp.broadcast_to(virt[group : group + 1, :], hits.shape)
        found = jnp.take_along_axis(table, lanes, axis=1, mode="promise_in_bounds")
        level = jnp.where(groups == group, found, level)
    excitation = level - occ[occ_index[z // 2]]
    frequency = freq[freq_index[0]]
    weight = -4.0 * excitation / (excitation * excitation + frequency * frequency)
    half = hits.shape[0] // 2
    weight = jnp.where(z % 2 == 0, weight[:half], weight[half:])
    for group in range(half):
        out[:, group * 128 : group * 128 + 128] = weight[group : group + 1]


def weights(occ_index, occ, freq, freq_index, virt, index, after):
    scalar, whole = pl.BlockSpec(memory_space=pltpu.SMEM), pl.BlockSpec(memory_space=pltpu.VMEM)
    return pl.pallas_call(
        weight_kernel,
        in_specs=[scalar] * 4 + [whole] * 3,
        out_specs=whole,
        out_shape=jax.ShapeDtypeStruct((1, index.shape[0] // 2), jnp.float32),
        compiler_params=pltpu.CompilerParams(vmem_limit_bytes=SMALL_VMEM),
        cost_estimate=pl.CostEstimate(flops=1, bytes_accessed=1, transcendentals=0),
    )(occ_index, occ, freq, freq_index, virt.reshape(-1, 128), index.reshape(-1, 128), after)


def pack_kernel(src, dst):
    width = dst.shape[2]
    for w in range(src.shape[0]):
        for half in range(2):
            dst[2 * w + half] = src[w, :, half * width : half * width + width]


def pack(factors):
    orbitals, rows, virt = factors.shape
    whole = pl.BlockSpec(memory_space=pltpu.VMEM)
    return pl.pallas_call(
        pack_kernel,
        in_specs=[whole],
        out_specs=whole,
        out_shape=jax.ShapeDtypeStruct((2 * orbitals, rows, virt // 2), factors.dtype),
        compiler_params=pltpu.CompilerParams(vmem_limit_bytes=SMALL_VMEM),
    )(factors)


def scaled_rows(left, shift, weight, blocks):
    first = 0
    for block in blocks:

        def scale(r, carry, block=block, first=first):
            chunk = block[pl.ds(pl.multiple_of(r * 16, 16), 16), :]
            left[first + r, shift] = (chunk.astype(jnp.float32) * weight[...]).astype(jnp.bfloat16)
            return carry

        count = block.shape[0] // 16
        lax.fori_loop(0, count, scale, 0)
        first += count


def multiply(left, right, keep, send, first):
    core = lax.axis_index("core")
    planes, shifts, _, depth = left.shape
    low = lax.broadcasted_iota(jnp.int32, (8, 128), 1) < 64

    def columns(step, carry):
        total = lax.dot_general(
            left[...].reshape(planes * shifts * 16, depth),
            right[pl.ds(step * 4, 4)].reshape(256, depth),
            (((1,), (1,)), ((), ())),
            preferred_element_type=jnp.float32,
        )
        for r in range(planes):
            for pair in range(2):
                for shift in range(shifts):
                    start = (r * shifts + shift) * 16
                    tiles = total[start : start + 16, pair * 128 : pair * 128 + 128]
                    for ref, tile in (
                        (keep, jnp.where(core == 0, tiles[:8], tiles[8:])),
                        (send, jnp.where(core == 0, tiles[8:], tiles[:8])),
                    ):
                        turned = pltpu.roll(tile, 64, 1)
                        even = jnp.where(low, tile, pltpu.roll(turned, 4, 0))
                        odd = jnp.where(low, turned, pltpu.roll(tile, 4, 0))
                        lanes = slice((first + shift) * 128, (first + shift) * 128 + 128)
                        ref[r, step * 4 + pair * 2, :, lanes] = even[:4]
                        ref[r, step * 4 + pair * 2 + 1, :, lanes] = odd[:4]
        return carry

    lax.fori_loop(0, 4, columns, 0)


def early_kernel(weight, p0, p1, p3, q00, q01, q10, q11, keep, send, right, left):
    ylo, yhi = lax.axis_index("ylo"), lax.axis_index("yhi")
    planes = right.shape[0]
    for (s, t), block in zip(FLIPS, (q00, q01, q10, q11)):
        at = (ylo ^ t) * 2 + (yhi ^ s)

        def move(r, carry, block=block, at=at):
            right[r, at] = block[pl.ds(pl.multiple_of(r * 16, 16), 16), :]
            return carry

        lax.fori_loop(0, planes, move, 0)
    for shift, block in enumerate((p0, p1, p3)):
        scaled_rows(left, shift, weight, (block,))
    multiply(left, right, keep, send, 0)


def late_kernel(weight, p2, right, keep_in, send_in, keep, send, left):
    del keep_in, send_in
    scaled_rows(left, 0, weight, (p2,))
    multiply(left, right, keep, send, 3)


def product(kernel, shifts, weight, *blocks):
    depth = blocks[0].shape[1]
    planes = 16
    whole = pl.BlockSpec(memory_space=pltpu.VMEM)
    packed = jax.ShapeDtypeStruct((planes, 4, 16, depth), jnp.bfloat16)
    results = [jax.ShapeDtypeStruct((planes, planes, 4, 512), jnp.float32)] * 2
    aliases = {}
    if kernel is early_kernel:
        results.append(packed)
    else:
        aliases = {len(blocks) - 1: 0, len(blocks): 1}
    return pl.pallas_call(
        kernel,
        in_specs=[whole] * (1 + len(blocks)),
        out_specs=[whole] * len(results),
        out_shape=results,
        scratch_shapes=[pltpu.VMEM((planes, shifts, 16, depth), jnp.bfloat16)],
        input_output_aliases=aliases,
        compiler_params=pltpu.CompilerParams(vmem_limit_bytes=VMEM_LIMIT),
        cost_estimate=pl.CostEstimate(
            flops=1, bytes_accessed=1, transcendentals=0
        ),
    )(weight, *blocks)


def assemble_kernel(mine, other, out):
    first = lax.axis_index("yhi") == 0
    lane = lax.broadcasted_iota(jnp.int32, (4, 128), 1) // 32
    for a in range(2):
        for ylo in range(2):
            for row_x in range(4):
                for core in range(2):
                    for half in range(2):
                        for column in range(2):
                            start = half * 64 + column * 32
                            total = jnp.zeros((4, 128), jnp.float32)
                            for x in range(4):
                                shift = (x - row_x) % 4
                                tile = SHIFT_TILES[shift]
                                lanes = slice(tile * 128, tile * 128 + 128)
                                at = ylo * 8 + x * 2 + core
                                part = jnp.where(first == (a == 0), mine[at, :, lanes], other[at, :, lanes])
                                turn = (x * 32 - start) % 128
                                part = pltpu.roll(part, turn, 1) if turn else part
                                total = jnp.where(lane == x, part, total)
                            row = (ylo * 8 + row_x * 2 + a) * 16 + core * 8 + half * 4
                            out[pl.ds(row, 4), column * 128 : column * 128 + 128] = total


def assemble(mine, other):
    whole = pl.BlockSpec(memory_space=pltpu.VMEM)
    return pl.pallas_call(
        assemble_kernel,
        in_specs=[whole] * 2,
        out_specs=whole,
        out_shape=jax.ShapeDtypeStruct((256, 256), jnp.float32),
        compiler_params=pltpu.CompilerParams(vmem_limit_bytes=SMALL_VMEM),
    )(mine, other)


def ring_permutation(s, t):
    index = lambda ylo, core, yhi: (ylo * 2 + core) * 2 + yhi
    return [
        (index(ylo, core, yhi), index(ylo ^ t, yhi, core ^ s))
        for ylo in range(2)
        for core in range(2)
        for yhi in range(2)
    ]


def flip_permutation(s, t):
    index = lambda ylo, core, yhi: (ylo * 2 + core) * 2 + yhi
    return [
        (index(ylo, core, yhi), index(ylo ^ t, core, yhi ^ s))
        for ylo in range(2)
        for core in range(2)
        for yhi in range(2)
    ]


def body(factors, occ_energies, virt_energies, freq_grid, occ_index, virt_index, freq_index):
    planes = lax.all_to_all(pack(factors), "z", split_axis=0, concat_axis=0, tiled=True)
    rows = planes.reshape(-1, planes.shape[2])

    own = lax.ppermute(rows, Y_RING, ring_permutation(0, 0))
    up = lambda block: lax.ppermute(block, "x", [(i, (i + 1) % 4) for i in range(4)])
    down = lambda block: lax.ppermute(block, "x", [(i, (i + 3) % 4) for i in range(4)])
    below, above = up(own), down(own)
    opposite = [lax.ppermute(own, "x", [(i, (i + 2) % 4) for i in range(4)])]
    q_blocks = [
        own,
        lax.ppermute(own, Y_RING, flip_permutation(0, 1)),
        lax.ppermute(rows, Y_RING, ring_permutation(1, 0)),
        lax.ppermute(own, Y_RING, flip_permutation(1, 1)),
    ]
    weight = weights(occ_index, occ_energies, freq_grid, freq_index, virt_energies, virt_index, rows)
    weight = lax.ppermute(weight, Y_RING, ring_permutation(0, 0))

    keep, send, right = product(early_kernel, 3, weight, own, below, above, *q_blocks)
    keep, send = product(late_kernel, 1, weight, *opposite, right, keep, send)
    total = keep + lax.ppermute(send, "core", [(0, 1), (1, 0)])
    root = jnp.sqrt(jnp.abs(total) * SCALE)
    coded = jnp.where(total < 0, -root, root).astype(jnp.float16)
    coded = coded.reshape(256, 4, 512)
    terms = lax.all_to_all(coded, ("z", "ylo", "x", "core"), split_axis=0, concat_axis=0, tiled=True)
    terms = terms.reshape(16, 16, 4, 512).astype(jnp.float32)
    mine = jnp.sum(terms * jnp.abs(terms), axis=0) * (1.0 / SCALE)
    other = lax.ppermute(mine, "yhi", [(0, 1), (1, 0)])
    return assemble(mine, other)


def solution(mesh):
    fine = Mesh(mesh.devices.reshape(16, 2, 4, 2, 2), AXES)
    columns = ("ylo", "x", "core")
    return jax.shard_map(
        body,
        mesh=fine,
        in_specs=(P("yhi", ("z",) + columns, None), P(), P(), P(), P("yhi"), P(), P()),
        out_specs=P("z", columns),
        check_vma=False,
    )
```

time: 364 us -> 207 us (0.57)
  waiting for transfers between devices: 284 us -> 30.4 us
  blocking collectives: 22.2 us -> 120 us
  starting transfers between devices: 0.09 us -> 41.8 us
  local copies, waits for them, and re-layouts: 31.3 us -> 1.15 us
  between operations: 15.1 us -> 0.86 us
  matrix products: 9.62 us -> 0 us
  Pallas kernels: 0 us -> 8.8 us
    all_gather x1 -> x0, waiting for transfers between devices: 158 us -> none  [body(): lax.all_gather(regrouped, 'arow', axis=1, tiled=True)]
    all_to_all x1 -> x2, blocking collectives: 22.2 us -> 120 us  [the longest x1 69.1 us: body(): lax.all_to_all(coded, ('z', 'ylo', 'x', 'core'), split_axis=0, concat_axi...]
    reduce_scatter x1 -> x0, waiting for transfers between devices: 75.4 us -> none  [body(): lax.psum_scatter(partial_rows, 'acol', scatter_dimension=1, tiled=True)]
    psum x1 -> x0, waiting for transfers between devices: 50.7 us -> none  [body(): return lax.psum(block, 'occ')]
    ppermute x0 -> x10, starting transfers between devices: none -> 41.8 us  [the longest x1 12.1 us: body(): own = lax.ppermute(rows, Y_RING, ring_permutation(0, 0))]
    ppermute x0 -> x10, waiting for transfers between devices: none -> 30.4 us  [the longest x1 9.38 us: body(): own = lax.ppermute(rows, Y_RING, ring_permutation(0, 0))]
    unnamed x12, local copies, waits for them, and re-layouts: 22.7 us -> 1.15 us
    dot_general x1 -> x0, matrix products: 9.62 us -> none  [body(): jnp.einsum('wpa,wqa->pq', scaled, lax.all_gather(regrouped, 'arow', axis=...]
  transfers between devices with their start and end apart: 3 -> 10, of which waited for: 3 -> 6; matrix products, arithmetic and copies ran while one was open for 1% -> 0% of each run, Pallas kernels for 0% -> 3%
where the time goes in v4:
time: 207 us; the launch traced here: 205 us
  blocking collectives  120 us (58%)
  starting transfers between devices  41.8 us (20%)
  waiting for transfers between devices  30.4 us (15%)
  Pallas kernels  8.8 us (4%)
  other arithmetic  2.79 us (1%)
    all_to_all x1, blocking collectives, body(): lax.all_to_all(coded, ('z', 'ylo', 'x', 'core'), split_axis=0, concat_axi...  69.1 us
    all_to_all x1, blocking collectives, body(): lax.all_to_all(pack(factors), 'z', split_axis=0, concat_axis=0, tiled=True)  50.5 us
    ppermute x1, starting transfers between devices, body(): own = lax.ppermute(rows, Y_RING, ring_permutation(0, 0))  12.1 us
    ppermute x1, waiting for transfers between devices, body(): own = lax.ppermute(rows, Y_RING, ring_permutation(0, 0))  9.38 us
    ppermute x1, waiting for transfers between devices, body(): lax.ppermute(own, Y_RING, flip_permutation(1, 1))  8.46 us
    ppermute x1, starting transfers between devices, body(): other = lax.ppermute(mine, 'yhi', [(0, 1), (1, 0)])  7.06 us
    pallas_call x2, Pallas kernels, product(): pl.pallas_call(kernel, in_specs=[whole] * (1 + len(blocks)), out_specs=[w...  6.74 us
    ppermute x1, waiting for transfers between devices, body(): lax.ppermute(own, Y_RING, flip_permutation(0, 1))  4.77 us
  transfers between devices with their start and end apart: 10, of which 6 were waited for; matrix products, arithmetic and copies ran while one was open for 0% of the time, Pallas kernels for 3%

profile of v4, /device:TPU:1, one launch (start us, length us, event | category | flops | bytes accessed | tf_op | source)
XLA Modules:
  0.0 205.3 jit_solution(6401001327405649881)
XLA Ops:
  0.0 1.1 copy-done
  1.2 0.1 shard_map.73
  1.2 50.5 %all_to_all.10 = bf16[16,16,1536]{2,1,0:T(8,128)(2,1)S(1)} all-to-all(bf16[16,16,1536]{2,1,0:T(8,128)(2,1)S(1)} %shard_map.73), channel_id=1, replica_groups=mesh['z'=16,'ylo'=2,'x'=4,'core'=2,'yhi'=2] {'z'}, dimensions={0} | all-to-all | bytes 1572864 | tf_op jit(solution)/shard_map/all_to_all | solution.py:217
  51.7 12.1 %collective-permute-start.1 = (bf16[256,1536]{1,0:T(8,128)(2,1)S(1)}, bf16[256,1536]{1,0:T(8,128)(2,1)S(1)}, u32[]{:S(2)}, u32[]{:S(2)}) collective-permute-start(bf16[256,1536]{1,0:T(8,128)(2,1)S(1)} %bitcast.6), channel_id=1, source_target_pairs={{0,0},{1,2},{2,1},{3,3},{16,16},{17,18},{18,17},{19,19},{4,4},{5,6... | collective-permute-start | bytes 2359304 | tf_op jit(solution)/shard_map/ppermute | solution.py:220
  63.8 1.9 collective-permute-start.6
  66.3 0.0 copy-done.1
  66.3 0.0 copy-done.2
  66.4 0.8 shard_map.74
  67.2 1.9 collective-permute-start
  69.1 9.4 %collective-permute-done.1.p0.q00 = bf16[256,1536]{1,0:T(8,128)(2,1)S(1)} collective-permute-done((bf16[256,1536]{1,0:T(8,128)(2,1)S(1)}, bf16[256,1536]{1,0:T(8,128)(2,1)S(1)}, u32[]{:S(2)}, u32[]{:S(2)}) %collective-permute-start.1) | collective-permute-done | bytes 786464 | tf_op jit(solution)/shard_map/ppermute | solution.py:220
  78.5 3.1 %collective-permute-start.3 = (bf16[256,1536]{1,0:T(8,128)(2,1)S(1)}, bf16[256,1536]{1,0:T(8,128)(2,1)S(1)}, u32[]{:S(2)}, u32[]{:S(2)}) collective-permute-start(bf16[256,1536]{1,0:T(8,128)(2,1)S(1)} %collective-permute-done.1.p0.q00), channel_id=1, source_target_pairs={{0,4},{4,8},{8,12},{12,0},{1,5},{5,9},{9,13},{13,1},{2,6},{6,10},{... | collective-permute-start | bytes 2359304 | tf_op jit(solution)/shard_map/ppermute | solution.py:221
  81.6 3.4 %collective-permute-start.4 = (bf16[256,1536]{1,0:T(8,128)(2,1)S(1)}, bf16[256,1536]{1,0:T(8,128)(2,1)S(1)}, u32[]{:S(2)}, u32[]{:S(2)}) collective-permute-start(bf16[256,1536]{1,0:T(8,128)(2,1)S(1)} %collective-permute-done.1.p0.q00), channel_id=1, source_target_pairs={{0,12},{4,0},{8,4},{12,8},{1,13},{5,1},{9,5},{13,9},{2,14},{6,2},{... | collective-permute-start | bytes 2359304 | tf_op jit(solution)/shard_map/ppermute | solution.py:222
  85.0 2.3 %collective-permute-start.5 = (bf16[256,1536]{1,0:T(8,128)(2,1)S(1)}, bf16[256,1536]{1,0:T(8,128)(2,1)S(1)}, u32[]{:S(2)}, u32[]{:S(2)}) collective-permute-start(bf16[256,1536]{1,0:T(8,128)(2,1)S(1)} %collective-permute-done.1.p0.q00), channel_id=1, source_target_pairs={{0,16},{1,17},{2,18},{3,19},{16,0},{17,1},{18,2},{19,3},{4,20},{5,... | collective-permute-start | bytes 2359304 | tf_op jit(solution)/shard_map/ppermute | solution.py:227
  87.3 0.0 collective-permute-done.weight
  87.3 1.9 collective-permute-start.7
  89.3 0.0 collective-permute-done.6.q10
  89.3 3.4 %collective-permute-start.2 = (bf16[256,1536]{1,0:T(8,128)(2,1)S(1)}, bf16[256,1536]{1,0:T(8,128)(2,1)S(1)}, u32[]{:S(2)}, u32[]{:S(2)}) collective-permute-start(bf16[256,1536]{1,0:T(8,128)(2,1)S(1)} %collective-permute-done.1.p0.q00), channel_id=1, source_target_pairs={{0,8},{4,12},{8,0},{12,4},{1,9},{5,13},{9,1},{13,5},{2,10},{6,14},... | collective-permute-start | bytes 2359304 | tf_op jit(solution)/shard_map/ppermute | solution.py:224
  92.7 0.0 collective-permute-done.3.p1
  92.7 1.6 collective-permute-done.4.p3
  94.4 4.8 %collective-permute-done.5.q01 = bf16[256,1536]{1,0:T(8,128)(2,1)S(1)} collective-permute-done((bf16[256,1536]{1,0:T(8,128)(2,1)S(1)}, bf16[256,1536]{1,0:T(8,128)(2,1)S(1)}, u32[]{:S(2)}, u32[]{:S(2)}) %collective-permute-start.5) | collective-permute-done | bytes 786464 | tf_op jit(solution)/shard_map/ppermute | solution.py:227
  99.1 8.5 %collective-permute-done.7.q11 = bf16[256,1536]{1,0:T(8,128)(2,1)S(1)} collective-permute-done((bf16[256,1536]{1,0:T(8,128)(2,1)S(1)}, bf16[256,1536]{1,0:T(8,128)(2,1)S(1)}, u32[]{:S(2)}, u32[]{:S(2)}) %collective-permute-start.7) | collective-permute-done | bytes 786464 | tf_op jit(solution)/shard_map/ppermute | solution.py:229
  107.6 4.6 %shard_map.75 = (f32[16,16,4,512]{3,2,1,0:T(4,128)S(1)}, f32[16,16,4,512]{3,2,1,0:T(4,128)S(1)}, bf16[16,4,16,1536]{3,2,1,0:T(8,128)(2,1)S(1)}) custom-call(f32[1,1536]{1,0:T(1,128)S(1)} %collective-permute-done.weight, bf16[256,1536]{1,0:T(8,128)(2,1)S(1)} %collective-permute-done.1.p0.q00, bf16[256,1536]{1,0:T(8,128)(2,1)S(1)} %collective-permute-done.3.p1, ...), custom_call_target="tpu_custom_call" | custom-call | flops 1 | bytes 1 | tf_op jit(solution)/shard_map/pallas_call | solution.py:147
  112.2 0.0 collective-permute-done.2.p2
  112.2 2.1 %shard_map.76 = (f32[16,16,4,512]{3,2,1,0:T(4,128)S(1)}, f32[16,16,4,512]{3,2,1,0:T(4,128)S(1)}) custom-call(f32[1,1536]{1,0:T(1,128)S(1)} %collective-permute-done.weight, bf16[256,1536]{1,0:T(8,128)(2,1)S(1)} %collective-permute-done.2.p2, bf16[16,4,16,1536]{3,2,1,0:T(8,128)(2,1)S(1)} %get-tuple-element.10.right, ...), custom_call_target="tpu_custom_call", output_to_operand_aliasing={{0}: (3, {}), {1}: (4, {})} | custom-call | flops 1 | bytes 1 | tf_op jit(solution)/shard_map/pallas_call | solution.py:147
  114.4 4.7 %collective-permute-start.8 = (f32[16,16,4,512]{3,2,1,0:T(4,128)S(1)}, f32[16,16,4,512]{3,2,1,0:T(4,128)S(1)}, u32[]{:S(2)}, u32[]{:S(2)}) collective-permute-start(f32[16,16,4,512]{3,2,1,0:T(4,128)S(1)} %get-tuple-element.14), channel_id=1, source_target_pairs={{0,2},{2,0},{1,3},{3,1},{4,6},{6,4},{5,7},{7,5},{8,10},{10,8},{9,1... | collective-permute-start | bytes 6291464 | tf_op jit(solution)/shard_map/ppermute | solution.py:236
  119.1 3.8 %collective-permute-done.8 = f32[16,16,4,512]{3,2,1,0:T(4,128)S(1)} collective-permute-done((f32[16,16,4,512]{3,2,1,0:T(4,128)S(1)}, f32[16,16,4,512]{3,2,1,0:T(4,128)S(1)}, u32[]{:S(2)}, u32[]{:S(2)}) %collective-permute-start.8) | collective-permute-done | bytes 2097184 | tf_op jit(solution)/shard_map/ppermute | solution.py:236
  122.8 2.0 fusion
  124.9 69.1 %all_to_all.11 = f16[256,4,512]{2,1,0:T(4,128)(2,1)S(1)} all-to-all(f16[256,4,512]{2,1,0:T(4,128)(2,1)S(1)} %bitcast.11), channel_id=1, replica_groups=mesh['z'=16,'ylo'=2,'x'=4,'core'=2,'yhi'=2] {'z','ylo','x','core'}, dimensions={0} | all-to-all | bytes 2097152 | tf_op jit(solution)/shard_map/all_to_all | solution.py:240
  193.9 0.7 fusion.1
  194.7 7.1 %collective-permute-start.9 = (f32[16,4,512]{2,1,0:T(4,128)S(1)}, f32[16,4,512]{2,1,0:T(4,128)S(1)}, u32[]{:S(2)}, u32[]{:S(2)}) collective-permute-start(f32[16,4,512]{2,1,0:T(4,128)S(1)} %broadcast_multiply_fusion.mine), channel_id=1, source_target_pairs={{0,1},{1,0},{2,3},{3,2},{4,5},{5,4},{6,7},{7,6},{8,9},{9,8},{10,11... | collective-permute-start | bytes 393224 | tf_op jit(solution)/shard_map/ppermute | solution.py:243
  201.7 2.3 %collective-permute-done.9.other = f32[16,4,512]{2,1,0:T(4,128)S(1)} collective-permute-done((f32[16,4,512]{2,1,0:T(4,128)S(1)}, f32[16,4,512]{2,1,0:T(4,128)S(1)}, u32[]{:S(2)}, u32[]{:S(2)}) %collective-permute-start.9) | collective-permute-done | bytes 131104 | tf_op jit(solution)/shard_map/ppermute | solution.py:243
  204.1 1.2 shard_map.77
  (10 shorter events, 0.1 us)
Async XLA Ops:
  0.0 1.1 copy-start
  1.1 65.2 %copy-start.1 = (f32[3072]{0:T(1024)S(1)}, f32[3072]{0:T(1024)}, u32[]{:S(2)}) copy-start(f32[3072]{0:T(1024)} %param.9) | copy-start | bytes 36868
  1.1 65.2 %copy-start.2 = (s32[3072]{0:T(1024)S(1)}, s32[3072]{0:T(1024)}, u32[]{:S(2)}) copy-start(s32[3072]{0:T(1024)} %param.12) | copy-start | bytes 36868
  1.1 65.2 %copy-start.3 = (f32[300]{0:T(512)S(1)}, f32[300]{0:T(512)}, u32[]{:S(2)}) copy-start(f32[300]{0:T(512)} %occ.1) | copy-start | bytes 3604
  1.1 65.2 %copy-start.4 = (s32[8]{0:T(128)S(1)}, s32[8]{0:T(128)}, u32[]{:S(2)}) copy-start(s32[8]{0:T(128)} %occ_index.1) | copy-start | bytes 100
  1.1 65.2 %copy-start.5 = (f32[32]{0:T(128)S(1)}, f32[32]{0:T(128)}, u32[]{:S(2)}) copy-start(f32[32]{0:T(128)} %freq.1) | copy-start | bytes 388
  51.7 26.8 %collective-permute-start.1 = (bf16[256,1536]{1,0:T(8,128)(2,1)S(1)}, bf16[256,1536]{1,0:T(8,128)(2,1)S(1)}, u32[]{:S(2)}, u32[]{:S(2)}) collective-permute-start(bf16[256,1536]{1,0:T(8,128)(2,1)S(1)} %bitcast.6), channel_id=1, source_target_pairs={{0,0},{1,2},{2,1},{3,3},{16,16},{17,18},{18,17},{19,19},{4,4},{5,6... | collective-permute-start | bytes 2359304 | tf_op jit(solution)/shard_map/ppermute | solution.py:220
  63.8 25.5 %collective-permute-start.6 = (bf16[256,1536]{1,0:T(8,128)(2,1)S(1)}, bf16[256,1536]{1,0:T(8,128)(2,1)S(1)}, u32[]{:S(2)}, u32[]{:S(2)}) collective-permute-start(bf16[256,1536]{1,0:T(8,128)(2,1)S(1)} %bitcast.7), channel_id=1, source_target_pairs={{0,1},{1,3},{2,0},{3,2},{16,17},{17,19},{18,16},{19,18},{4,5},{5,7... | collective-permute-start | bytes 2359304 | tf_op jit(solution)/shard_map/ppermute | solution.py:228
  67.2 20.1 %collective-permute-start = (f32[1,1536]{1,0:T(1,128)S(1)}, f32[1,1536]{1,0:T(1,128)S(1)}, u32[]{:S(2)}, u32[]{:S(2)}) collective-permute-start(f32[1,1536]{1,0:T(1,128)S(1)} %shard_map.74), channel_id=1, source_target_pairs={{0,0},{1,2},{2,1},{3,3},{16,16},{17,18},{18,17},{19,19},{4,4},{5,6... | collective-permute-start | bytes 18440 | tf_op jit(solution)/shard_map/ppermute | solution.py:232
  78.5 14.2 %collective-permute-start.3 = (bf16[256,1536]{1,0:T(8,128)(2,1)S(1)}, bf16[256,1536]{1,0:T(8,128)(2,1)S(1)}, u32[]{:S(2)}, u32[]{:S(2)}) collective-permute-start(bf16[256,1536]{1,0:T(8,128)(2,1)S(1)} %collective-permute-done.1.p0.q00), channel_id=1, source_target_pairs={{0,4},{4,8},{8,12},{12,0},{1,5},{5,9},{9,13},{13,1},{2,6},{6,10},{... | collective-permute-start | bytes 2359304 | tf_op jit(solution)/shard_map/ppermute | solution.py:221
  81.6 12.7 %collective-permute-start.4 = (bf16[256,1536]{1,0:T(8,128)(2,1)S(1)}, bf16[256,1536]{1,0:T(8,128)(2,1)S(1)}, u32[]{:S(2)}, u32[]{:S(2)}) collective-permute-start(bf16[256,1536]{1,0:T(8,128)(2,1)S(1)} %collective-permute-done.1.p0.q00), channel_id=1, source_target_pairs={{0,12},{4,0},{8,4},{12,8},{1,13},{5,1},{9,5},{13,9},{2,14},{6,2},{... | collective-permute-start | bytes 2359304 | tf_op jit(solution)/shard_map/ppermute | solution.py:222
  85.0 14.1 %collective-permute-start.5 = (bf16[256,1536]{1,0:T(8,128)(2,1)S(1)}, bf16[256,1536]{1,0:T(8,128)(2,1)S(1)}, u32[]{:S(2)}, u32[]{:S(2)}) collective-permute-start(bf16[256,1536]{1,0:T(8,128)(2,1)S(1)} %collective-permute-done.1.p0.q00), channel_id=1, source_target_pairs={{0,16},{1,17},{2,18},{3,19},{16,0},{17,1},{18,2},{19,3},{4,20},{5,... | collective-permute-start | bytes 2359304 | tf_op jit(solution)/shard_map/ppermute | solution.py:227
  87.3 20.3 %collective-permute-start.7 = (bf16[256,1536]{1,0:T(8,128)(2,1)S(1)}, bf16[256,1536]{1,0:T(8,128)(2,1)S(1)}, u32[]{:S(2)}, u32[]{:S(2)}) collective-permute-start(bf16[256,1536]{1,0:T(8,128)(2,1)S(1)} %collective-permute-done.1.p0.q00), channel_id=1, source_target_pairs={{0,17},{1,16},{2,19},{3,18},{16,1},{17,0},{18,3},{19,2},{4,21},{5,... | collective-permute-start | bytes 2359304 | tf_op jit(solution)/shard_map/ppermute | solution.py:229
  89.3 22.9 %collective-permute-start.2 = (bf16[256,1536]{1,0:T(8,128)(2,1)S(1)}, bf16[256,1536]{1,0:T(8,128)(2,1)S(1)}, u32[]{:S(2)}, u32[]{:S(2)}) collective-permute-start(bf16[256,1536]{1,0:T(8,128)(2,1)S(1)} %collective-permute-done.1.p0.q00), channel_id=1, source_target_pairs={{0,8},{4,12},{8,0},{12,4},{1,9},{5,13},{9,1},{13,5},{2,10},{6,14},... | collective-permute-start | bytes 2359304 | tf_op jit(solution)/shard_map/ppermute | solution.py:224
  114.4 8.5 %collective-permute-start.8 = (f32[16,16,4,512]{3,2,1,0:T(4,128)S(1)}, f32[16,16,4,512]{3,2,1,0:T(4,128)S(1)}, u32[]{:S(2)}, u32[]{:S(2)}) collective-permute-start(f32[16,16,4,512]{3,2,1,0:T(4,128)S(1)} %get-tuple-element.14), channel_id=1, source_target_pairs={{0,2},{2,0},{1,3},{3,1},{4,6},{6,4},{5,7},{7,5},{8,10},{10,8},{9,1... | collective-permute-start | bytes 6291464 | tf_op jit(solution)/shard_map/ppermute | solution.py:236
  194.7 9.4 %collective-permute-start.9 = (f32[16,4,512]{2,1,0:T(4,128)S(1)}, f32[16,4,512]{2,1,0:T(4,128)S(1)}, u32[]{:S(2)}, u32[]{:S(2)}) collective-permute-start(f32[16,4,512]{2,1,0:T(4,128)S(1)} %broadcast_multiply_fusion.mine), channel_id=1, source_target_pairs={{0,1},{1,0},{2,3},{3,2},{4,5},{5,4},{6,7},{7,6},{8,9},{9,8},{10,11... | collective-permute-start | bytes 393224 | tf_op jit(solution)/shard_map/ppermute | solution.py:243

commit v5 on v4

--- a/solution.py
+++ b/solution.py
@@ -8,10 +8,10 @@
 
 AXES = ("z", "ylo", "x", "core", "yhi")
 Y_RING = ("ylo", "core", "yhi")
-VMEM_LIMIT = 32 * 1024 * 1024
+VMEM_LIMIT = 12 * 1024 * 1024
 SMALL_VMEM = 8 * 1024 * 1024
-SHIFT_TILES = (0, 1, 3, 2)
-SCALE = 5e5
+SHIFT_TILES = ((0, 0), (0, 1), (1, 1), (1, 0))
+SCALE = 2.5e5
 FLIPS = ((0, 0), (0, 1), (1, 0), (1, 1))
 
 
@@ -79,10 +79,12 @@
         first += count
 
 
-def multiply(left, right, keep, send, first):
+def multiply(left, right, keep, send, shares):
     core = lax.axis_index("core")
+    parity = lax.axis_index("z") % 2
     planes, shifts, _, depth = left.shape
     low = lax.broadcasted_iota(jnp.int32, (8, 128), 1) < 64
+    top = lax.broadcasted_iota(jnp.int32, (8, 128), 0) < 4
 
     def columns(step, carry):
         total = lax.dot_general(
@@ -91,21 +93,35 @@
             (((1,), (1,)), ((), ())),
             preferred_element_type=jnp.float32,
         )
+
+        def tile(r, shift, pair, half):
+            start = (r * shifts + shift) * 16
+            tiles = total[start : start + 16, pair * 128 : pair * 128 + 128]
+            return jnp.where(core == half, tiles[:8], tiles[8:])
+
         for r in range(planes):
             for pair in range(2):
-                for shift in range(shifts):
-                    start = (r * shifts + shift) * 16
-                    tiles = total[start : start + 16, pair * 128 : pair * 128 + 128]
-                    for ref, tile in (
-                        (keep, jnp.where(core == 0, tiles[:8], tiles[8:])),
-                        (send, jnp.where(core == 0, tiles[8:], tiles[:8])),
-                    ):
-                        turned = pltpu.roll(tile, 64, 1)
-                        even = jnp.where(low, tile, pltpu.roll(turned, 4, 0))
-                        odd = jnp.where(low, turned, pltpu.roll(tile, 4, 0))
-                        lanes = slice((first + shift) * 128, (first + shift) * 128 + 128)
-                        ref[r, step * 4 + pair * 2, :, lanes] = even[:4]
-                        ref[r, step * 4 + pair * 2 + 1, :, lanes] = odd[:4]
+                for share, (a, b) in shares.items():
+                    for half, ref in ((0, keep), (1, send)):
+                        if a is not None:
+                            first = tile(r, a, pair, half)
+                            first_turned = pltpu.roll(first, 64, 1)
+                            even = jnp.where(low, first, pltpu.roll(first_turned, 4, 0))
+                            odd = jnp.where(low, first_turned, pltpu.roll(first, 4, 0))
+                            rows = slice(0, 4)
+                        if b is not None:
+                            second = tile(r, b, pair, half)
+                            second_turned = pltpu.roll(second, 64, 1)
+                            even_b = jnp.where(low, pltpu.roll(second, 4, 0), second_turned)
+                            odd_b = jnp.where(low, pltpu.roll(second_turned, 4, 0), second)
+                            rows = slice(4, 8)
+                            if a is None:
+                                even, odd = even_b, odd_b
+                            else:
+                                even, odd = jnp.where(top, even, even_b), jnp.where(top, odd, odd_b)
+                                rows = slice(0, 8)
+                        ref[share ^ parity, r, step * 4 + pair * 2, rows, :] = even[rows]
+                        ref[share ^ parity, r, step * 4 + pair * 2 + 1, rows, :] = odd[rows]
         return carry
 
     lax.fori_loop(0, 4, columns, 0)
@@ -124,13 +140,13 @@
         lax.fori_loop(0, planes, move, 0)
     for shift, block in enumerate((p0, p1, p3)):
         scaled_rows(left, shift, weight, (block,))
-    multiply(left, right, keep, send, 0)
+    multiply(left, right, keep, send, {0: (0, 1), 1: (2, None)})
 
 
 def late_kernel(weight, p2, right, keep_in, send_in, keep, send, left):
     del keep_in, send_in
     scaled_rows(left, 0, weight, (p2,))
-    multiply(left, right, keep, send, 3)
+    multiply(left, right, keep, send, {1: (None, 0)})
 
 
 def product(kernel, shifts, weight, *blocks):
@@ -138,7 +154,7 @@
     planes = 16
     whole = pl.BlockSpec(memory_space=pltpu.VMEM)
     packed = jax.ShapeDtypeStruct((planes, 4, 16, depth), jnp.bfloat16)
-    results = [jax.ShapeDtypeStruct((planes, planes, 4, 512), jnp.float32)] * 2
+    results = [jax.ShapeDtypeStruct((2, planes, planes, 8, 128), jnp.float32)] * 2
     aliases = {}
     if kernel is early_kernel:
         results.append(packed)
@@ -171,10 +187,10 @@
                             total = jnp.zeros((4, 128), jnp.float32)
                             for x in range(4):
                                 shift = (x - row_x) % 4
-                                tile = SHIFT_TILES[shift]
-                                lanes = slice(tile * 128, tile * 128 + 128)
+                                share, tile = SHIFT_TILES[shift]
+                                rows = slice(tile * 4, tile * 4 + 4)
                                 at = ylo * 8 + x * 2 + core
-                                part = jnp.where(first == (a == 0), mine[at, :, lanes], other[at, :, lanes])
+                                part = jnp.where(first == (a == 0), mine[share, at, rows, :], other[share, at, rows, :])
                                 turn = (x * 32 - start) % 128
                                 part = pltpu.roll(part, turn, 1) if turn else part
                                 total = jnp.where(lane == x, part, total)
@@ -211,6 +227,16 @@
         for core in range(2)
         for yhi in range(2)
     ]
+
+
+def encode(terms):
+    root = jnp.sqrt(jnp.abs(terms) * SCALE)
+    return jnp.where(terms < 0, -root, root).astype(jnp.float16)
+
+
+def decode(codes):
+    root = codes.astype(jnp.float32)
+    return root * jnp.abs(root) * (1.0 / SCALE)
 
 
 def body(factors, occ_energies, virt_energies, freq_grid, occ_index, virt_index, freq_index):
@@ -233,13 +259,13 @@
 
     keep, send, right = product(early_kernel, 3, weight, own, below, above, *q_blocks)
     keep, send = product(late_kernel, 1, weight, *opposite, right, keep, send)
-    total = keep + lax.ppermute(send, "core", [(0, 1), (1, 0)])
-    root = jnp.sqrt(jnp.abs(total) * SCALE)
-    coded = jnp.where(total < 0, -root, root).astype(jnp.float16)
-    coded = coded.reshape(256, 4, 512)
-    terms = lax.all_to_all(coded, ("z", "ylo", "x", "core"), split_axis=0, concat_axis=0, tiled=True)
-    terms = terms.reshape(16, 16, 4, 512).astype(jnp.float32)
-    mine = jnp.sum(terms * jnp.abs(terms), axis=0) * (1.0 / SCALE)
+    got = lax.ppermute(send, "core", [(0, 1), (1, 0)])
+    passed = lax.ppermute(encode(keep[1] + got[1]), "z", [(i, i ^ 1) for i in range(16)])
+    pairs = encode(keep[0] + got[0] + decode(passed))
+    terms = lax.all_to_all(
+        pairs.reshape(256, 8, 128), ("z", "ylo", "x", "core"), split_axis=0, concat_axis=0, tiled=True
+    )
+    mine = jnp.sum(decode(terms).reshape(8, 2, 16, 8, 128), axis=0)
     other = lax.ppermute(mine, "yhi", [(0, 1), (1, 0)])
     return assemble(mine, other)
 

time: 207 us -> 200 us (0.966)
  blocking collectives: 120 us -> 97.5 us
  waiting for transfers between devices: 30.4 us -> 42.3 us
  starting transfers between devices: 41.8 us -> 45.3 us
    all_to_all x1, blocking collectives: 69.1 us -> 47.1 us  [body(): lax.all_to_all(pairs.reshape(256, 8, 128), ('z', 'ylo', 'x', 'core'), spl...]
    ppermute x1 -> x2, waiting for transfers between devices: 3.76 us -> 15.7 us  [the longest x1 12 us: body(): lax.ppermute(encode(keep[1] + got[1]), 'z', [(i, i ^ 1) for i in range(16)])]
    ppermute x1 -> x2, starting transfers between devices: 4.68 us -> 8.43 us  [the longest x1 4.71 us: body(): got = lax.ppermute(send, 'core', [(0, 1), (1, 0)])]
  transfers between devices with their start and end apart: 10 -> 11, of which waited for: 6 -> 7; matrix products, arithmetic and copies ran while one was open for 0% -> 0% of each run, Pallas kernels for 3% -> 3%
where the time goes in v5:
time: 200 us; the launch traced here: 197 us
  blocking collectives  97.5 us (49%)
  starting transfers between devices  45.3 us (23%)
  waiting for transfers between devices  42.3 us (21%)
  Pallas kernels  8.8 us (4%)
    all_to_all x1, blocking collectives, body(): lax.all_to_all(pack(factors), 'z', split_axis=0, concat_axis=0, tiled=True)  50.5 us
    all_to_all x1, blocking collectives, body(): lax.all_to_all(pairs.reshape(256, 8, 128), ('z', 'ylo', 'x', 'core'), spl...  47.1 us
    ppermute x1, starting transfers between devices, body(): own = lax.ppermute(rows, Y_RING, ring_permutation(0, 0))  12.1 us
    ppermute x1, waiting for transfers between devices, body(): lax.ppermute(encode(keep[1] + got[1]), 'z', [(i, i ^ 1) for i in range(16)])  12 us
    ppermute x1, waiting for transfers between devices, body(): own = lax.ppermute(rows, Y_RING, ring_permutation(0, 0))  9.38 us
    ppermute x1, waiting for transfers between devices, body(): lax.ppermute(own, Y_RING, flip_permutation(1, 1))  8.46 us
    ppermute x1, starting transfers between devices, body(): other = lax.ppermute(mine, 'yhi', [(0, 1), (1, 0)])  6.84 us
    pallas_call x2, Pallas kernels, product(): pl.pallas_call(kernel, in_specs=[whole] * (1 + len(blocks)), out_specs=[w...  6.74 us
  transfers between devices with their start and end apart: 11, of which 7 were waited for; matrix products, arithmetic and copies ran while one was open for 0% of the time, Pallas kernels for 3%

profile of v5, /device:TPU:1, one launch (start us, length us, event | category | flops | bytes accessed | tf_op | source)
XLA Modules:
  0.0 197.5 jit_solution(1951107142706146616)
XLA Ops:
  0.0 1.1 copy-done
  1.2 0.1 shard_map.73
  1.2 50.5 %all_to_all.10 = bf16[16,16,1536]{2,1,0:T(8,128)(2,1)S(1)} all-to-all(bf16[16,16,1536]{2,1,0:T(8,128)(2,1)S(1)} %shard_map.73), channel_id=1, replica_groups=mesh['z'=16,'ylo'=2,'x'=4,'core'=2,'yhi'=2] {'z'}, dimensions={0} | all-to-all | bytes 1572864 | tf_op jit(solution)/shard_map/all_to_all | solution.py:243
  51.7 12.1 %collective-permute-start.1 = (bf16[256,1536]{1,0:T(8,128)(2,1)S(1)}, bf16[256,1536]{1,0:T(8,128)(2,1)S(1)}, u32[]{:S(2)}, u32[]{:S(2)}) collective-permute-start(bf16[256,1536]{1,0:T(8,128)(2,1)S(1)} %bitcast.15), channel_id=1, source_target_pairs={{0,0},{1,2},{2,1},{3,3},{16,16},{17,18},{18,17},{19,19},{4,4},{5,6... | collective-permute-start | bytes 2359304 | tf_op jit(solution)/shard_map/ppermute | solution.py:246
  63.8 1.9 collective-permute-start.6
  66.4 0.8 shard_map.74
  67.2 1.9 collective-permute-start
  69.1 9.4 %collective-permute-done.1.p0.q00 = bf16[256,1536]{1,0:T(8,128)(2,1)S(1)} collective-permute-done((bf16[256,1536]{1,0:T(8,128)(2,1)S(1)}, bf16[256,1536]{1,0:T(8,128)(2,1)S(1)}, u32[]{:S(2)}, u32[]{:S(2)}) %collective-permute-start.1) | collective-permute-done | bytes 786464 | tf_op jit(solution)/shard_map/ppermute | solution.py:246
  78.5 3.1 %collective-permute-start.3 = (bf16[256,1536]{1,0:T(8,128)(2,1)S(1)}, bf16[256,1536]{1,0:T(8,128)(2,1)S(1)}, u32[]{:S(2)}, u32[]{:S(2)}) collective-permute-start(bf16[256,1536]{1,0:T(8,128)(2,1)S(1)} %collective-permute-done.1.p0.q00), channel_id=1, source_target_pairs={{0,4},{4,8},{8,12},{12,0},{1,5},{5,9},{9,13},{13,1},{2,6},{6,10},{... | collective-permute-start | bytes 2359304 | tf_op jit(solution)/shard_map/ppermute | solution.py:247
  81.6 3.4 %collective-permute-start.4 = (bf16[256,1536]{1,0:T(8,128)(2,1)S(1)}, bf16[256,1536]{1,0:T(8,128)(2,1)S(1)}, u32[]{:S(2)}, u32[]{:S(2)}) collective-permute-start(bf16[256,1536]{1,0:T(8,128)(2,1)S(1)} %collective-permute-done.1.p0.q00), channel_id=1, source_target_pairs={{0,12},{4,0},{8,4},{12,8},{1,13},{5,1},{9,5},{13,9},{2,14},{6,2},{... | collective-permute-start | bytes 2359304 | tf_op jit(solution)/shard_map/ppermute | solution.py:248
  85.0 2.3 %collective-permute-start.5 = (bf16[256,1536]{1,0:T(8,128)(2,1)S(1)}, bf16[256,1536]{1,0:T(8,128)(2,1)S(1)}, u32[]{:S(2)}, u32[]{:S(2)}) collective-permute-start(bf16[256,1536]{1,0:T(8,128)(2,1)S(1)} %collective-permute-done.1.p0.q00), channel_id=1, source_target_pairs={{0,16},{1,17},{2,18},{3,19},{16,0},{17,1},{18,2},{19,3},{4,20},{5,... | collective-permute-start | bytes 2359304 | tf_op jit(solution)/shard_map/ppermute | solution.py:253
  87.3 1.9 collective-permute-start.7
  89.3 0.0 collective-permute-done.6.q10
  89.3 3.4 %collective-permute-start.2 = (bf16[256,1536]{1,0:T(8,128)(2,1)S(1)}, bf16[256,1536]{1,0:T(8,128)(2,1)S(1)}, u32[]{:S(2)}, u32[]{:S(2)}) collective-permute-start(bf16[256,1536]{1,0:T(8,128)(2,1)S(1)} %collective-permute-done.1.p0.q00), channel_id=1, source_target_pairs={{0,8},{4,12},{8,0},{12,4},{1,9},{5,13},{9,1},{13,5},{2,10},{6,14},... | collective-permute-start | bytes 2359304 | tf_op jit(solution)/shard_map/ppermute | solution.py:250
  92.7 0.0 collective-permute-done.3.p1
  92.7 1.6 collective-permute-done.4.p3
  94.4 4.8 %collective-permute-done.5.q01 = bf16[256,1536]{1,0:T(8,128)(2,1)S(1)} collective-permute-done((bf16[256,1536]{1,0:T(8,128)(2,1)S(1)}, bf16[256,1536]{1,0:T(8,128)(2,1)S(1)}, u32[]{:S(2)}, u32[]{:S(2)}) %collective-permute-start.5) | collective-permute-done | bytes 786464 | tf_op jit(solution)/shard_map/ppermute | solution.py:253
  99.1 8.5 %collective-permute-done.7.q11 = bf16[256,1536]{1,0:T(8,128)(2,1)S(1)} collective-permute-done((bf16[256,1536]{1,0:T(8,128)(2,1)S(1)}, bf16[256,1536]{1,0:T(8,128)(2,1)S(1)}, u32[]{:S(2)}, u32[]{:S(2)}) %collective-permute-start.7) | collective-permute-done | bytes 786464 | tf_op jit(solution)/shard_map/ppermute | solution.py:255
  107.6 4.6 %shard_map.75 = (f32[2,16,16,8,128]{4,3,2,1,0:T(8,128)S(1)}, f32[2,16,16,8,128]{4,3,2,1,0:T(8,128)S(1)}, bf16[16,4,16,1536]{3,2,1,0:T(8,128)(2,1)S(1)}) custom-call(f32[1,1536]{1,0:T(1,128)S(1)} %collective-permute-done.weight, bf16[256,1536]{1,0:T(8,128)(2,1)S(1)} %collective-permute-done.1.p0.q00, bf16[256,1536]{1,0:T(8,128)(2,1)S(1)} %collective-permute-done.3.p1, ...), custom_call_target="tpu_custom_call" | custom-call | flops 1 | bytes 1 | tf_op jit(solution)/shard_map/pallas_call | solution.py:163
  112.2 2.2 %shard_map.76 = (f32[2,16,16,8,128]{4,3,2,1,0:T(8,128)S(1)}, f32[2,16,16,8,128]{4,3,2,1,0:T(8,128)S(1)}) custom-call(f32[1,1536]{1,0:T(1,128)S(1)} %collective-permute-done.weight, bf16[256,1536]{1,0:T(8,128)(2,1)S(1)} %collective-permute-done.2.p2, ...), custom_call_target="tpu_custom_call", output_to_operand_aliasing={{0}: (3, {}), {1}: (4, {})} | custom-call | flops 1 | bytes 1 | tf_op jit(solution)/shard_map/pallas_call | solution.py:163
  114.4 4.7 %collective-permute-start.8 = (f32[2,16,16,8,128]{4,3,2,1,0:T(8,128)S(1)}, f32[2,16,16,8,128]{4,3,2,1,0:T(8,128)S(1)}, u32[]{:S(2)}, u32[]{:S(2)}) collective-permute-start(f32[2,16,16,8,128]{4,3,2,1,0:T(8,128)S(1)} %get-tuple-element.14), channel_id=1, source_target_pairs={{0,2},{2,0},{1,3},{3,1},{4,6},{6,4},{5,7},{7,5},{8,10},{10,8},{9,1... | collective-permute-start | bytes 6291464 | tf_op jit(solution)/shard_map/ppermute | solution.py:262
  119.1 3.8 %collective-permute-done.8 = f32[2,16,16,8,128]{4,3,2,1,0:T(8,128)S(1)} collective-permute-done((f32[2,16,16,8,128]{4,3,2,1,0:T(8,128)S(1)}, f32[2,16,16,8,128]{4,3,2,1,0:T(8,128)S(1)}, u32[]{:S(2)}, u32[]{:S(2)}) %collective-permute-start.8) | collective-permute-done | bytes 2097184 | tf_op jit(solution)/shard_map/ppermute | solution.py:262
  122.9 0.5 fusion
  123.4 3.7 %collective-permute-start.9 = (f16[16,16,8,128]{3,2,1,0:T(8,128)(2,1)S(1)}, f16[16,16,8,128]{3,2,1,0:T(8,128)(2,1)S(1)}, u32[]{:S(2)}, u32[]{:S(2)}) collective-permute-start(f16[16,16,8,128]{3,2,1,0:T(8,128)(2,1)S(1)} %fusion), channel_id=1, source_target_pairs={{0,32},{32,0},{64,96},{96,64},{128,160},{160,128},{192,224},{224,1... | collective-permute-start | bytes 1572872 | tf_op jit(solution)/shard_map/ppermute | solution.py:263
  127.1 12.0 %collective-permute-done.9 = f16[16,16,8,128]{3,2,1,0:T(8,128)(2,1)S(1)} collective-permute-done((f16[16,16,8,128]{3,2,1,0:T(8,128)(2,1)S(1)}, f16[16,16,8,128]{3,2,1,0:T(8,128)(2,1)S(1)}, u32[]{:S(2)}, u32[]{:S(2)}) %collective-permute-start.9) | collective-permute-done | bytes 524320 | tf_op jit(solution)/shard_map/ppermute | solution.py:263
  139.1 0.7 fusion.3
  139.8 47.1 %all_to_all.11 = f16[256,8,128]{2,1,0:T(8,128)(2,1)S(1)} all-to-all(f16[256,8,128]{2,1,0:T(8,128)(2,1)S(1)} %bitcast.21), channel_id=1, replica_groups=mesh['z'=16,'ylo'=2,'x'=4,'core'=2,'yhi'=2] {'z','ylo','x','core'}, dimensions={0} | all-to-all | bytes 1048576 | tf_op jit(solution)/shard_map/all_to_all | solution.py:265
  186.9 0.2 fusion.4
  187.0 0.1 reduce_sum.9.mine
  187.1 6.8 %collective-permute-start.10 = (f32[2,16,8,128]{3,2,1,0:T(8,128)S(1)}, f32[2,16,8,128]{3,2,1,0:T(8,128)S(1)}, u32[]{:S(2)}, u32[]{:S(2)}) collective-permute-start(f32[2,16,8,128]{3,2,1,0:T(8,128)S(1)} %reduce_sum.9.mine), channel_id=1, source_target_pairs={{0,1},{1,0},{2,3},{3,2},{4,5},{5,4},{6,7},{7,6},{8,9},{9,8},{10,11... | collective-permute-start | bytes 393224 | tf_op jit(solution)/shard_map/ppermute | solution.py:269
  193.9 2.3 %collective-permute-done.10.other = f32[2,16,8,128]{3,2,1,0:T(8,128)S(1)} collective-permute-done((f32[2,16,8,128]{3,2,1,0:T(8,128)S(1)}, f32[2,16,8,128]{3,2,1,0:T(8,128)S(1)}, u32[]{:S(2)}, u32[]{:S(2)}) %collective-permute-start.10) | collective-permute-done | bytes 131104 | tf_op jit(solution)/shard_map/ppermute | solution.py:269
  196.3 1.2 shard_map.77
  (13 shorter events, 0.0 us)
Async XLA Ops:
  0.0 1.1 copy-start
  1.1 65.2 %copy-start.1 = (f32[3072]{0:T(1024)S(1)}, f32[3072]{0:T(1024)}, u32[]{:S(2)}) copy-start(f32[3072]{0:T(1024)} %param.9) | copy-start | bytes 36868
  1.1 65.2 %copy-start.2 = (s32[3072]{0:T(1024)S(1)}, s32[3072]{0:T(1024)}, u32[]{:S(2)}) copy-start(s32[3072]{0:T(1024)} %param.12) | copy-start | bytes 36868
  1.1 65.2 %copy-start.3 = (f32[300]{0:T(512)S(1)}, f32[300]{0:T(512)}, u32[]{:S(2)}) copy-start(f32[300]{0:T(512)} %occ.1) | copy-start | bytes 3604
  1.1 65.2 %copy-start.4 = (s32[8]{0:T(128)S(1)}, s32[8]{0:T(128)}, u32[]{:S(2)}) copy-start(s32[8]{0:T(128)} %occ_index.1) | copy-start | bytes 100
  1.1 65.2 %copy-start.5 = (f32[32]{0:T(128)S(1)}, f32[32]{0:T(128)}, u32[]{:S(2)}) copy-start(f32[32]{0:T(128)} %freq.1) | copy-start | bytes 388
  51.7 26.8 %collective-permute-start.1 = (bf16[256,1536]{1,0:T(8,128)(2,1)S(1)}, bf16[256,1536]{1,0:T(8,128)(2,1)S(1)}, u32[]{:S(2)}, u32[]{:S(2)}) collective-permute-start(bf16[256,1536]{1,0:T(8,128)(2,1)S(1)} %bitcast.15), channel_id=1, source_target_pairs={{0,0},{1,2},{2,1},{3,3},{16,16},{17,18},{18,17},{19,19},{4,4},{5,6... | collective-permute-start | bytes 2359304 | tf_op jit(solution)/shard_map/ppermute | solution.py:246
  63.8 25.5 %collective-permute-start.6 = (bf16[256,1536]{1,0:T(8,128)(2,1)S(1)}, bf16[256,1536]{1,0:T(8,128)(2,1)S(1)}, u32[]{:S(2)}, u32[]{:S(2)}) collective-permute-start(bf16[256,1536]{1,0:T(8,128)(2,1)S(1)} %bitcast.16), channel_id=1, source_target_pairs={{0,1},{1,3},{2,0},{3,2},{16,17},{17,19},{18,16},{19,18},{4,5},{5,7... | collective-permute-start | bytes 2359304 | tf_op jit(solution)/shard_map/ppermute | solution.py:254
  67.2 20.1 %collective-permute-start = (f32[1,1536]{1,0:T(1,128)S(1)}, f32[1,1536]{1,0:T(1,128)S(1)}, u32[]{:S(2)}, u32[]{:S(2)}) collective-permute-start(f32[1,1536]{1,0:T(1,128)S(1)} %shard_map.74), channel_id=1, source_target_pairs={{0,0},{1,2},{2,1},{3,3},{16,16},{17,18},{18,17},{19,19},{4,4},{5,6... | collective-permute-start | bytes 18440 | tf_op jit(solution)/shard_map/ppermute | solution.py:258
  78.5 14.2 %collective-permute-start.3 = (bf16[256,1536]{1,0:T(8,128)(2,1)S(1)}, bf16[256,1536]{1,0:T(8,128)(2,1)S(1)}, u32[]{:S(2)}, u32[]{:S(2)}) collective-permute-start(bf16[256,1536]{1,0:T(8,128)(2,1)S(1)} %collective-permute-done.1.p0.q00), channel_id=1, source_target_pairs={{0,4},{4,8},{8,12},{12,0},{1,5},{5,9},{9,13},{13,1},{2,6},{6,10},{... | collective-permute-start | bytes 2359304 | tf_op jit(solution)/shard_map/ppermute | solution.py:247
  81.6 12.7 %collective-permute-start.4 = (bf16[256,1536]{1,0:T(8,128)(2,1)S(1)}, bf16[256,1536]{1,0:T(8,128)(2,1)S(1)}, u32[]{:S(2)}, u32[]{:S(2)}) collective-permute-start(bf16[256,1536]{1,0:T(8,128)(2,1)S(1)} %collective-permute-done.1.p0.q00), channel_id=1, source_target_pairs={{0,12},{4,0},{8,4},{12,8},{1,13},{5,1},{9,5},{13,9},{2,14},{6,2},{... | collective-permute-start | bytes 2359304 | tf_op jit(solution)/shard_map/ppermute | solution.py:248
  85.0 14.1 %collective-permute-start.5 = (bf16[256,1536]{1,0:T(8,128)(2,1)S(1)}, bf16[256,1536]{1,0:T(8,128)(2,1)S(1)}, u32[]{:S(2)}, u32[]{:S(2)}) collective-permute-start(bf16[256,1536]{1,0:T(8,128)(2,1)S(1)} %collective-permute-done.1.p0.q00), channel_id=1, source_target_pairs={{0,16},{1,17},{2,18},{3,19},{16,0},{17,1},{18,2},{19,3},{4,20},{5,... | collective-permute-start | bytes 2359304 | tf_op jit(solution)/shard_map/ppermute | solution.py:253
  87.3 20.3 %collective-permute-start.7 = (bf16[256,1536]{1,0:T(8,128)(2,1)S(1)}, bf16[256,1536]{1,0:T(8,128)(2,1)S(1)}, u32[]{:S(2)}, u32[]{:S(2)}) collective-permute-start(bf16[256,1536]{1,0:T(8,128)(2,1)S(1)} %collective-permute-done.1.p0.q00), channel_id=1, source_target_pairs={{0,17},{1,16},{2,19},{3,18},{16,1},{17,0},{18,3},{19,2},{4,21},{5,... | collective-permute-start | bytes 2359304 | tf_op jit(solution)/shard_map/ppermute | solution.py:255
  89.3 22.9 %collective-permute-start.2 = (bf16[256,1536]{1,0:T(8,128)(2,1)S(1)}, bf16[256,1536]{1,0:T(8,128)(2,1)S(1)}, u32[]{:S(2)}, u32[]{:S(2)}) collective-permute-start(bf16[256,1536]{1,0:T(8,128)(2,1)S(1)} %collective-permute-done.1.p0.q00), channel_id=1, source_target_pairs={{0,8},{4,12},{8,0},{12,4},{1,9},{5,13},{9,1},{13,5},{2,10},{6,14},... | collective-permute-start | bytes 2359304 | tf_op jit(solution)/shard_map/ppermute | solution.py:250
  114.4 8.5 %collective-permute-start.8 = (f32[2,16,16,8,128]{4,3,2,1,0:T(8,128)S(1)}, f32[2,16,16,8,128]{4,3,2,1,0:T(8,128)S(1)}, u32[]{:S(2)}, u32[]{:S(2)}) collective-permute-start(f32[2,16,16,8,128]{4,3,2,1,0:T(8,128)S(1)} %get-tuple-element.14), channel_id=1, source_target_pairs={{0,2},{2,0},{1,3},{3,1},{4,6},{6,4},{5,7},{7,5},{8,10},{10,8},{9,1... | collective-permute-start | bytes 6291464 | tf_op jit(solution)/shard_map/ppermute | solution.py:262
  123.4 15.7 %collective-permute-start.9 = (f16[16,16,8,128]{3,2,1,0:T(8,128)(2,1)S(1)}, f16[16,16,8,128]{3,2,1,0:T(8,128)(2,1)S(1)}, u32[]{:S(2)}, u32[]{:S(2)}) collective-permute-start(f16[16,16,8,128]{3,2,1,0:T(8,128)(2,1)S(1)} %fusion), channel_id=1, source_target_pairs={{0,32},{32,0},{64,96},{96,64},{128,160},{160,128},{192,224},{224,1... | collective-permute-start | bytes 1572872 | tf_op jit(solution)/shard_map/ppermute | solution.py:263
  187.1 9.2 %collective-permute-start.10 = (f32[2,16,8,128]{3,2,1,0:T(8,128)S(1)}, f32[2,16,8,128]{3,2,1,0:T(8,128)S(1)}, u32[]{:S(2)}, u32[]{:S(2)}) collective-permute-start(f32[2,16,8,128]{3,2,1,0:T(8,128)S(1)} %reduce_sum.9.mine), channel_id=1, source_target_pairs={{0,1},{1,0},{2,3},{3,2},{4,5},{5,4},{6,7},{7,6},{8,9},{9,8},{10,11... | collective-permute-start | bytes 393224 | tf_op jit(solution)/shard_map/ppermute | solution.py:269

commit v6 on v5

--- a/solution.py
+++ b/solution.py
@@ -10,7 +10,7 @@
 Y_RING = ("ylo", "core", "yhi")
 VMEM_LIMIT = 12 * 1024 * 1024
 SMALL_VMEM = 8 * 1024 * 1024
-SHIFT_TILES = ((0, 0), (0, 1), (1, 1), (1, 0))
+SHIFT_TILES = ((0, 0), (0, 1), (1, 0), (1, 1))
 SCALE = 2.5e5
 FLIPS = ((0, 0), (0, 1), (1, 0), (1, 1))
 
@@ -127,7 +127,7 @@
     lax.fori_loop(0, 4, columns, 0)
 
 
-def early_kernel(weight, p0, p1, p3, q00, q01, q10, q11, keep, send, right, left):
+def early_kernel(weight, p0, p1, p2, q00, q01, q10, q11, keep, send, right, left):
     ylo, yhi = lax.axis_index("ylo"), lax.axis_index("yhi")
     planes = right.shape[0]
     for (s, t), block in zip(FLIPS, (q00, q01, q10, q11)):
@@ -138,14 +138,14 @@
             return carry
 
         lax.fori_loop(0, planes, move, 0)
-    for shift, block in enumerate((p0, p1, p3)):
+    for shift, block in enumerate((p0, p1, p2)):
         scaled_rows(left, shift, weight, (block,))
     multiply(left, right, keep, send, {0: (0, 1), 1: (2, None)})
 
 
-def late_kernel(weight, p2, right, keep_in, send_in, keep, send, left):
+def late_kernel(weight, p3, right, keep_in, send_in, keep, send, left):
     del keep_in, send_in
-    scaled_rows(left, 0, weight, (p2,))
+    scaled_rows(left, 0, weight, (p3,))
     multiply(left, right, keep, send, {1: (None, 0)})
 
 
@@ -229,6 +229,11 @@
     ]
 
 
+def neighbour_planes():
+    other = lambda z, core: ((z + core) ^ 1) - core
+    return [(z * 2 + core, other(z, core) % 16 * 2 + core) for z in range(16) for core in range(2)]
+
+
 def encode(terms):
     root = jnp.sqrt(jnp.abs(terms) * SCALE)
     return jnp.where(terms < 0, -root, root).astype(jnp.float16)
@@ -244,10 +249,9 @@
     rows = planes.reshape(-1, planes.shape[2])
 
     own = lax.ppermute(rows, Y_RING, ring_permutation(0, 0))
-    up = lambda block: lax.ppermute(block, "x", [(i, (i + 1) % 4) for i in range(4)])
-    down = lambda block: lax.ppermute(block, "x", [(i, (i + 3) % 4) for i in range(4)])
-    below, above = up(own), down(own)
-    opposite = [lax.ppermute(own, "x", [(i, (i + 2) % 4) for i in range(4)])]
+    step, opposite, back = [
+        lax.ppermute(own, "x", [(i, (i + shift) % 4) for i in range(4)]) for shift in (1, 2, 3)
+    ]
     q_blocks = [
         own,
         lax.ppermute(own, Y_RING, flip_permutation(0, 1)),
@@ -257,10 +261,10 @@
     weight = weights(occ_index, occ_energies, freq_grid, freq_index, virt_energies, virt_index, rows)
     weight = lax.ppermute(weight, Y_RING, ring_permutation(0, 0))
 
-    keep, send, right = product(early_kernel, 3, weight, own, below, above, *q_blocks)
-    keep, send = product(late_kernel, 1, weight, *opposite, right, keep, send)
+    keep, send, right = product(early_kernel, 3, weight, own, step, opposite, *q_blocks)
+    keep, send = product(late_kernel, 1, weight, back, right, keep, send)
     got = lax.ppermute(send, "core", [(0, 1), (1, 0)])
-    passed = lax.ppermute(encode(keep[1] + got[1]), "z", [(i, i ^ 1) for i in range(16)])
+    passed = lax.ppermute(encode(keep[1] + got[1]), ("z", "core"), neighbour_planes())
     pairs = encode(keep[0] + got[0] + decode(passed))
     terms = lax.all_to_all(
         pairs.reshape(256, 8, 128), ("z", "ylo", "x", "core"), split_axis=0, concat_axis=0, tiled=True

time: 200 us -> 191 us (0.955)
  waiting for transfers between devices: 42.3 us -> 38.1 us
  blocking collectives: 97.5 us -> 94.2 us
    ppermute x4, waiting for transfers between devices: 13.6 us -> 22.6 us  [the longest x3 15.6 us: body(): lax.ppermute(own, 'x', [(i, (i + shift) % 4) for i in range(4)])]
    ppermute x1, waiting for transfers between devices: 8.46 us -> 0.01 us  [body(): lax.ppermute(own, Y_RING, flip_permutation(1, 1))]
    ppermute x1, waiting for transfers between devices: 4.77 us -> 0.01 us  [body(): lax.ppermute(own, Y_RING, flip_permutation(0, 1))]
    all_to_all x1, blocking collectives: 47.1 us -> 43.7 us  [body(): lax.all_to_all(pairs.reshape(256, 8, 128), ('z', 'ylo', 'x', 'core'), spl...]
  transfers between devices with their start and end apart: 11 -> 11, of which waited for: 7 -> 6; matrix products, arithmetic and copies ran while one was open for 0% -> 0% of each run, Pallas kernels for 3% -> 3%
where the time goes in v6:
time: 191 us; the launch traced here: 189 us
  blocking collectives  94.2 us (49%)
  starting transfers between devices  44.2 us (23%)
  waiting for transfers between devices  38.1 us (20%)
  Pallas kernels  8.81 us (5%)
    all_to_all x1, blocking collectives, body(): lax.all_to_all(pack(factors), 'z', split_axis=0, concat_axis=0, tiled=True)  50.5 us
    all_to_all x1, blocking collectives, body(): lax.all_to_all(pairs.reshape(256, 8, 128), ('z', 'ylo', 'x', 'core'), spl...  43.7 us
    ppermute x3, waiting for transfers between devices, body(): lax.ppermute(own, 'x', [(i, (i + shift) % 4) for i in range(4)])  15.6 us
    ppermute x1, starting transfers between devices, body(): own = lax.ppermute(rows, Y_RING, ring_permutation(0, 0))  12.1 us
    ppermute x3, starting transfers between devices, body(): lax.ppermute(own, 'x', [(i, (i + shift) % 4) for i in range(4)])  10.5 us
    ppermute x1, waiting for transfers between devices, body(): own = lax.ppermute(rows, Y_RING, ring_permutation(0, 0))  9.38 us
    ppermute x1, waiting for transfers between devices, body(): lax.ppermute(encode(keep[1] + got[1]), ('z', 'core'), neighbour_planes())  6.95 us
    pallas_call x2, Pallas kernels, product(): pl.pallas_call(kernel, in_specs=[whole] * (1 + len(blocks)), out_specs=[w...  6.75 us
  transfers between devices with their start and end apart: 11, of which 6 were waited for; matrix products, arithmetic and copies ran while one was open for 0% of the time, Pallas kernels for 3%

profile of v6, /device:TPU:1, one launch (start us, length us, event | category | flops | bytes accessed | tf_op | source)
XLA Modules:
  0.0 188.7 jit_solution(18042152107025531979)
XLA Ops:
  0.0 1.1 copy-done
  1.2 0.1 shard_map.73
  1.2 50.5 %all_to_all.10 = bf16[16,16,1536]{2,1,0:T(8,128)(2,1)S(1)} all-to-all(bf16[16,16,1536]{2,1,0:T(8,128)(2,1)S(1)} %shard_map.73), channel_id=1, replica_groups=mesh['z'=16,'ylo'=2,'x'=4,'core'=2,'yhi'=2] {'z'}, dimensions={0} | all-to-all | bytes 1572864 | tf_op jit(solution)/shard_map/all_to_all | solution.py:248
  51.7 12.1 %collective-permute-start.1 = (bf16[256,1536]{1,0:T(8,128)(2,1)S(1)}, bf16[256,1536]{1,0:T(8,128)(2,1)S(1)}, u32[]{:S(2)}, u32[]{:S(2)}) collective-permute-start(bf16[256,1536]{1,0:T(8,128)(2,1)S(1)} %bitcast.15), channel_id=1, source_target_pairs={{0,0},{1,2},{2,1},{3,3},{16,16},{17,18},{18,17},{19,19},{4,4},{5,6... | collective-permute-start | bytes 2359304 | tf_op jit(solution)/shard_map/ppermute | solution.py:251
  63.8 1.9 %collective-permute-start.6 = (bf16[256,1536]{1,0:T(8,128)(2,1)S(1)}, bf16[256,1536]{1,0:T(8,128)(2,1)S(1)}, u32[]{:S(2)}, u32[]{:S(2)}) collective-permute-start(bf16[256,1536]{1,0:T(8,128)(2,1)S(1)} %bitcast.16), channel_id=1, source_target_pairs={{0,1},{1,3},{2,0},{3,2},{16,17},{17,19},{18,16},{19,18},{4,5},{5,7... | collective-permute-start | bytes 2359304 | tf_op jit(solution)/shard_map/ppermute | solution.py:258
  66.4 0.8 shard_map.74
  67.2 1.9 %collective-permute-start = (f32[1,1536]{1,0:T(1,128)S(1)}, f32[1,1536]{1,0:T(1,128)S(1)}, u32[]{:S(2)}, u32[]{:S(2)}) collective-permute-start(f32[1,1536]{1,0:T(1,128)S(1)} %shard_map.74), channel_id=1, source_target_pairs={{0,0},{1,2},{2,1},{3,3},{16,16},{17,18},{18,17},{19,19},{4,4},{5,6... | collective-permute-start | bytes 18440 | tf_op jit(solution)/shard_map/ppermute | solution.py:262
  69.1 9.4 %collective-permute-done.1.p0.q00 = bf16[256,1536]{1,0:T(8,128)(2,1)S(1)} collective-permute-done((bf16[256,1536]{1,0:T(8,128)(2,1)S(1)}, bf16[256,1536]{1,0:T(8,128)(2,1)S(1)}, u32[]{:S(2)}, u32[]{:S(2)}) %collective-permute-start.1) | collective-permute-done | bytes 786464 | tf_op jit(solution)/shard_map/ppermute | solution.py:251
  78.5 3.1 %collective-permute-start.3 = (bf16[256,1536]{1,0:T(8,128)(2,1)S(1)}, bf16[256,1536]{1,0:T(8,128)(2,1)S(1)}, u32[]{:S(2)}, u32[]{:S(2)}) collective-permute-start(bf16[256,1536]{1,0:T(8,128)(2,1)S(1)} %collective-permute-done.1.p0.q00), channel_id=1, source_target_pairs={{0,4},{4,8},{8,12},{12,0},{1,5},{5,9},{9,13},{13,1},{2,6},{6,10},{... | collective-permute-start | bytes 2359304 | tf_op jit(solution)/shard_map/ppermute | solution.py:253
  81.6 4.4 %collective-permute-start.4 = (bf16[256,1536]{1,0:T(8,128)(2,1)S(1)}, bf16[256,1536]{1,0:T(8,128)(2,1)S(1)}, u32[]{:S(2)}, u32[]{:S(2)}) collective-permute-start(bf16[256,1536]{1,0:T(8,128)(2,1)S(1)} %collective-permute-done.1.p0.q00), channel_id=1, source_target_pairs={{0,8},{4,12},{8,0},{12,4},{1,9},{5,13},{9,1},{13,5},{2,10},{6,14},... | collective-permute-start | bytes 2359304 | tf_op jit(solution)/shard_map/ppermute | solution.py:253
  86.0 2.3 %collective-permute-start.5 = (bf16[256,1536]{1,0:T(8,128)(2,1)S(1)}, bf16[256,1536]{1,0:T(8,128)(2,1)S(1)}, u32[]{:S(2)}, u32[]{:S(2)}) collective-permute-start(bf16[256,1536]{1,0:T(8,128)(2,1)S(1)} %collective-permute-done.1.p0.q00), channel_id=1, source_target_pairs={{0,16},{1,17},{2,18},{3,19},{16,0},{17,1},{18,2},{19,3},{4,20},{5,... | collective-permute-start | bytes 2359304 | tf_op jit(solution)/shard_map/ppermute | solution.py:257
  88.3 0.0 collective-permute-done.weight
  88.3 1.9 %collective-permute-start.7 = (bf16[256,1536]{1,0:T(8,128)(2,1)S(1)}, bf16[256,1536]{1,0:T(8,128)(2,1)S(1)}, u32[]{:S(2)}, u32[]{:S(2)}) collective-permute-start(bf16[256,1536]{1,0:T(8,128)(2,1)S(1)} %collective-permute-done.1.p0.q00), channel_id=1, source_target_pairs={{0,17},{1,16},{2,19},{3,18},{16,1},{17,0},{18,3},{19,2},{4,21},{5,... | collective-permute-start | bytes 2359304 | tf_op jit(solution)/shard_map/ppermute | solution.py:259
  90.3 3.1 %collective-permute-start.2 = (bf16[256,1536]{1,0:T(8,128)(2,1)S(1)}, bf16[256,1536]{1,0:T(8,128)(2,1)S(1)}, u32[]{:S(2)}, u32[]{:S(2)}) collective-permute-start(bf16[256,1536]{1,0:T(8,128)(2,1)S(1)} %collective-permute-done.1.p0.q00), channel_id=1, source_target_pairs={{0,12},{4,0},{8,4},{12,8},{1,13},{5,1},{9,5},{13,9},{2,14},{6,2},{... | collective-permute-start | bytes 2359304 | tf_op jit(solution)/shard_map/ppermute | solution.py:253
  93.3 7.5 %collective-permute-done.3.p1 = bf16[256,1536]{1,0:T(8,128)(2,1)S(1)} collective-permute-done((bf16[256,1536]{1,0:T(8,128)(2,1)S(1)}, bf16[256,1536]{1,0:T(8,128)(2,1)S(1)}, u32[]{:S(2)}, u32[]{:S(2)}) %collective-permute-start.3) | collective-permute-done | bytes 786464 | tf_op jit(solution)/shard_map/ppermute | solution.py:253
  100.8 8.1 %collective-permute-done.4.p2 = bf16[256,1536]{1,0:T(8,128)(2,1)S(1)} collective-permute-done((bf16[256,1536]{1,0:T(8,128)(2,1)S(1)}, bf16[256,1536]{1,0:T(8,128)(2,1)S(1)}, u32[]{:S(2)}, u32[]{:S(2)}) %collective-permute-start.4) | collective-permute-done | bytes 786464 | tf_op jit(solution)/shard_map/ppermute | solution.py:253
  109.0 0.0 collective-permute-done.5.q01
  109.0 0.0 collective-permute-done.7.q11
  109.0 4.6 %shard_map.75 = (f32[2,16,16,8,128]{4,3,2,1,0:T(8,128)S(1)}, f32[2,16,16,8,128]{4,3,2,1,0:T(8,128)S(1)}, bf16[16,4,16,1536]{3,2,1,0:T(8,128)(2,1)S(1)}) custom-call(f32[1,1536]{1,0:T(1,128)S(1)} %collective-permute-done.weight, bf16[256,1536]{1,0:T(8,128)(2,1)S(1)} %collective-permute-done.1.p0.q00, bf16[256,1536]{1,0:T(8,128)(2,1)S(1)} %collective-permute-done.3.p1, ...), custom_call_target="tpu_custom_call" | custom-call | flops 1 | bytes 1 | tf_op jit(solution)/shard_map/pallas_call | solution.py:163
  113.6 2.2 %shard_map.76 = (f32[2,16,16,8,128]{4,3,2,1,0:T(8,128)S(1)}, f32[2,16,16,8,128]{4,3,2,1,0:T(8,128)S(1)}) custom-call(f32[1,1536]{1,0:T(1,128)S(1)} %collective-permute-done.weight, bf16[256,1536]{1,0:T(8,128)(2,1)S(1)} %collective-permute-done.2.p3, ...), custom_call_target="tpu_custom_call", output_to_operand_aliasing={{0}: (3, {}), {1}: (4, {})} | custom-call | flops 1 | bytes 1 | tf_op jit(solution)/shard_map/pallas_call | solution.py:163
  115.7 4.3 %collective-permute-start.8 = (f32[2,16,16,8,128]{4,3,2,1,0:T(8,128)S(1)}, f32[2,16,16,8,128]{4,3,2,1,0:T(8,128)S(1)}, u32[]{:S(2)}, u32[]{:S(2)}) collective-permute-start(f32[2,16,16,8,128]{4,3,2,1,0:T(8,128)S(1)} %get-tuple-element.14), channel_id=1, source_target_pairs={{0,2},{2,0},{1,3},{3,1},{4,6},{6,4},{5,7},{7,5},{8,10},{10,8},{9,1... | collective-permute-start | bytes 6291464 | tf_op jit(solution)/shard_map/ppermute | solution.py:266
  120.1 3.8 %collective-permute-done.8 = f32[2,16,16,8,128]{4,3,2,1,0:T(8,128)S(1)} collective-permute-done((f32[2,16,16,8,128]{4,3,2,1,0:T(8,128)S(1)}, f32[2,16,16,8,128]{4,3,2,1,0:T(8,128)S(1)}, u32[]{:S(2)}, u32[]{:S(2)}) %collective-permute-start.8) | collective-permute-done | bytes 2097184 | tf_op jit(solution)/shard_map/ppermute | solution.py:266
  123.8 0.5 fusion
  124.4 4.2 %collective-permute-start.9 = (f16[16,16,8,128]{3,2,1,0:T(8,128)(2,1)S(1)}, f16[16,16,8,128]{3,2,1,0:T(8,128)(2,1)S(1)}, u32[]{:S(2)}, u32[]{:S(2)}) collective-permute-start(f16[16,16,8,128]{3,2,1,0:T(8,128)(2,1)S(1)} %fusion), channel_id=1, source_target_pairs={{0,32},{2,482},{32,0},{34,66},{64,96},{66,34},{96,64},{98,130},{12... | collective-permute-start | bytes 1572872 | tf_op jit(solution)/shard_map/ppermute | solution.py:267
  128.5 6.9 %collective-permute-done.9 = f16[16,16,8,128]{3,2,1,0:T(8,128)(2,1)S(1)} collective-permute-done((f16[16,16,8,128]{3,2,1,0:T(8,128)(2,1)S(1)}, f16[16,16,8,128]{3,2,1,0:T(8,128)(2,1)S(1)}, u32[]{:S(2)}, u32[]{:S(2)}) %collective-permute-start.9) | collective-permute-done | bytes 524320 | tf_op jit(solution)/shard_map/ppermute | solution.py:267
  135.5 0.7 fusion.3
  136.2 43.7 %all_to_all.11 = f16[256,8,128]{2,1,0:T(8,128)(2,1)S(1)} all-to-all(f16[256,8,128]{2,1,0:T(8,128)(2,1)S(1)} %bitcast.21), channel_id=1, replica_groups=mesh['z'=16,'ylo'=2,'x'=4,'core'=2,'yhi'=2] {'z','ylo','x','core'}, dimensions={0} | all-to-all | bytes 1048576 | tf_op jit(solution)/shard_map/all_to_all | solution.py:269
  179.9 0.2 fusion.4
  180.1 0.1 reduce_sum.9.mine
  180.2 5.0 %collective-permute-start.10 = (f32[2,16,8,128]{3,2,1,0:T(8,128)S(1)}, f32[2,16,8,128]{3,2,1,0:T(8,128)S(1)}, u32[]{:S(2)}, u32[]{:S(2)}) collective-permute-start(f32[2,16,8,128]{3,2,1,0:T(8,128)S(1)} %reduce_sum.9.mine), channel_id=1, source_target_pairs={{0,1},{1,0},{2,3},{3,2},{4,5},{5,4},{6,7},{7,6},{8,9},{9,8},{10,11... | collective-permute-start | bytes 393224 | tf_op jit(solution)/shard_map/ppermute | solution.py:273
  185.2 2.3 %collective-permute-done.10.other = f32[2,16,8,128]{3,2,1,0:T(8,128)S(1)} collective-permute-done((f32[2,16,8,128]{3,2,1,0:T(8,128)S(1)}, f32[2,16,8,128]{3,2,1,0:T(8,128)S(1)}, u32[]{:S(2)}, u32[]{:S(2)}) %collective-permute-start.10) | collective-permute-done | bytes 131104 | tf_op jit(solution)/shard_map/ppermute | solution.py:273
  187.5 1.2 shard_map.77
  (13 shorter events, 0.0 us)
Async XLA Ops:
  0.0 1.1 copy-start
  1.1 65.2 %copy-start.1 = (f32[3072]{0:T(1024)S(1)}, f32[3072]{0:T(1024)}, u32[]{:S(2)}) copy-start(f32[3072]{0:T(1024)} %param.9) | copy-start | bytes 36868
  1.1 65.2 %copy-start.2 = (s32[3072]{0:T(1024)S(1)}, s32[3072]{0:T(1024)}, u32[]{:S(2)}) copy-start(s32[3072]{0:T(1024)} %param.12) | copy-start | bytes 36868
  1.1 65.2 %copy-start.3 = (f32[300]{0:T(512)S(1)}, f32[300]{0:T(512)}, u32[]{:S(2)}) copy-start(f32[300]{0:T(512)} %occ.1) | copy-start | bytes 3604
  1.1 65.2 %copy-start.4 = (s32[8]{0:T(128)S(1)}, s32[8]{0:T(128)}, u32[]{:S(2)}) copy-start(s32[8]{0:T(128)} %occ_index.1) | copy-start | bytes 100
  1.1 65.2 %copy-start.5 = (f32[32]{0:T(128)S(1)}, f32[32]{0:T(128)}, u32[]{:S(2)}) copy-start(f32[32]{0:T(128)} %freq.1) | copy-start | bytes 388
  51.7 26.8 %collective-permute-start.1 = (bf16[256,1536]{1,0:T(8,128)(2,1)S(1)}, bf16[256,1536]{1,0:T(8,128)(2,1)S(1)}, u32[]{:S(2)}, u32[]{:S(2)}) collective-permute-start(bf16[256,1536]{1,0:T(8,128)(2,1)S(1)} %bitcast.15), channel_id=1, source_target_pairs={{0,0},{1,2},{2,1},{3,3},{16,16},{17,18},{18,17},{19,19},{4,4},{5,6... | collective-permute-start | bytes 2359304 | tf_op jit(solution)/shard_map/ppermute | solution.py:251
  63.8 26.5 %collective-permute-start.6 = (bf16[256,1536]{1,0:T(8,128)(2,1)S(1)}, bf16[256,1536]{1,0:T(8,128)(2,1)S(1)}, u32[]{:S(2)}, u32[]{:S(2)}) collective-permute-start(bf16[256,1536]{1,0:T(8,128)(2,1)S(1)} %bitcast.16), channel_id=1, source_target_pairs={{0,1},{1,3},{2,0},{3,2},{16,17},{17,19},{18,16},{19,18},{4,5},{5,7... | collective-permute-start | bytes 2359304 | tf_op jit(solution)/shard_map/ppermute | solution.py:258
  67.2 21.1 %collective-permute-start = (f32[1,1536]{1,0:T(1,128)S(1)}, f32[1,1536]{1,0:T(1,128)S(1)}, u32[]{:S(2)}, u32[]{:S(2)}) collective-permute-start(f32[1,1536]{1,0:T(1,128)S(1)} %shard_map.74), channel_id=1, source_target_pairs={{0,0},{1,2},{2,1},{3,3},{16,16},{17,18},{18,17},{19,19},{4,4},{5,6... | collective-permute-start | bytes 18440 | tf_op jit(solution)/shard_map/ppermute | solution.py:262
  78.5 22.3 %collective-permute-start.3 = (bf16[256,1536]{1,0:T(8,128)(2,1)S(1)}, bf16[256,1536]{1,0:T(8,128)(2,1)S(1)}, u32[]{:S(2)}, u32[]{:S(2)}) collective-permute-start(bf16[256,1536]{1,0:T(8,128)(2,1)S(1)} %collective-permute-done.1.p0.q00), channel_id=1, source_target_pairs={{0,4},{4,8},{8,12},{12,0},{1,5},{5,9},{9,13},{13,1},{2,6},{6,10},{... | collective-permute-start | bytes 2359304 | tf_op jit(solution)/shard_map/ppermute | solution.py:253
  81.6 27.3 %collective-permute-start.4 = (bf16[256,1536]{1,0:T(8,128)(2,1)S(1)}, bf16[256,1536]{1,0:T(8,128)(2,1)S(1)}, u32[]{:S(2)}, u32[]{:S(2)}) collective-permute-start(bf16[256,1536]{1,0:T(8,128)(2,1)S(1)} %collective-permute-done.1.p0.q00), channel_id=1, source_target_pairs={{0,8},{4,12},{8,0},{12,4},{1,9},{5,13},{9,1},{13,5},{2,10},{6,14},... | collective-permute-start | bytes 2359304 | tf_op jit(solution)/shard_map/ppermute | solution.py:253
  86.0 23.0 %collective-permute-start.5 = (bf16[256,1536]{1,0:T(8,128)(2,1)S(1)}, bf16[256,1536]{1,0:T(8,128)(2,1)S(1)}, u32[]{:S(2)}, u32[]{:S(2)}) collective-permute-start(bf16[256,1536]{1,0:T(8,128)(2,1)S(1)} %collective-permute-done.1.p0.q00), channel_id=1, source_target_pairs={{0,16},{1,17},{2,18},{3,19},{16,0},{17,1},{18,2},{19,3},{4,20},{5,... | collective-permute-start | bytes 2359304 | tf_op jit(solution)/shard_map/ppermute | solution.py:257
  88.3 20.6 %collective-permute-start.7 = (bf16[256,1536]{1,0:T(8,128)(2,1)S(1)}, bf16[256,1536]{1,0:T(8,128)(2,1)S(1)}, u32[]{:S(2)}, u32[]{:S(2)}) collective-permute-start(bf16[256,1536]{1,0:T(8,128)(2,1)S(1)} %collective-permute-done.1.p0.q00), channel_id=1, source_target_pairs={{0,17},{1,16},{2,19},{3,18},{16,1},{17,0},{18,3},{19,2},{4,21},{5,... | collective-permute-start | bytes 2359304 | tf_op jit(solution)/shard_map/ppermute | solution.py:259
  90.3 23.3 %collective-permute-start.2 = (bf16[256,1536]{1,0:T(8,128)(2,1)S(1)}, bf16[256,1536]{1,0:T(8,128)(2,1)S(1)}, u32[]{:S(2)}, u32[]{:S(2)}) collective-permute-start(bf16[256,1536]{1,0:T(8,128)(2,1)S(1)} %collective-permute-done.1.p0.q00), channel_id=1, source_target_pairs={{0,12},{4,0},{8,4},{12,8},{1,13},{5,1},{9,5},{13,9},{2,14},{6,2},{... | collective-permute-start | bytes 2359304 | tf_op jit(solution)/shard_map/ppermute | solution.py:253
  115.7 8.1 %collective-permute-start.8 = (f32[2,16,16,8,128]{4,3,2,1,0:T(8,128)S(1)}, f32[2,16,16,8,128]{4,3,2,1,0:T(8,128)S(1)}, u32[]{:S(2)}, u32[]{:S(2)}) collective-permute-start(f32[2,16,16,8,128]{4,3,2,1,0:T(8,128)S(1)} %get-tuple-element.14), channel_id=1, source_target_pairs={{0,2},{2,0},{1,3},{3,1},{4,6},{6,4},{5,7},{7,5},{8,10},{10,8},{9,1... | collective-permute-start | bytes 6291464 | tf_op jit(solution)/shard_map/ppermute | solution.py:266
  124.4 11.1 %collective-permute-start.9 = (f16[16,16,8,128]{3,2,1,0:T(8,128)(2,1)S(1)}, f16[16,16,8,128]{3,2,1,0:T(8,128)(2,1)S(1)}, u32[]{:S(2)}, u32[]{:S(2)}) collective-permute-start(f16[16,16,8,128]{3,2,1,0:T(8,128)(2,1)S(1)} %fusion), channel_id=1, source_target_pairs={{0,32},{2,482},{32,0},{34,66},{64,96},{66,34},{96,64},{98,130},{12... | collective-permute-start | bytes 1572872 | tf_op jit(solution)/shard_map/ppermute | solution.py:267
  180.2 7.4 %collective-permute-start.10 = (f32[2,16,8,128]{3,2,1,0:T(8,128)S(1)}, f32[2,16,8,128]{3,2,1,0:T(8,128)S(1)}, u32[]{:S(2)}, u32[]{:S(2)}) collective-permute-start(f32[2,16,8,128]{3,2,1,0:T(8,128)S(1)} %reduce_sum.9.mine), channel_id=1, source_target_pairs={{0,1},{1,0},{2,3},{3,2},{4,5},{5,4},{6,7},{7,6},{8,9},{9,8},{10,11... | collective-permute-start | bytes 393224 | tf_op jit(solution)/shard_map/ppermute | solution.py:273

commit v7 on v6

--- a/solution.py
+++ b/solution.py
@@ -8,7 +8,7 @@
 
 AXES = ("z", "ylo", "x", "core", "yhi")
 Y_RING = ("ylo", "core", "yhi")
-VMEM_LIMIT = 12 * 1024 * 1024
+VMEM_LIMIT = 20 * 1024 * 1024
 SMALL_VMEM = 8 * 1024 * 1024
 SHIFT_TILES = ((0, 0), (0, 1), (1, 0), (1, 1))
 SCALE = 2.5e5
@@ -120,14 +120,14 @@
                             else:
                                 even, odd = jnp.where(top, even, even_b), jnp.where(top, odd, odd_b)
                                 rows = slice(0, 8)
-                        ref[share ^ parity, r, step * 4 + pair * 2, rows, :] = even[rows]
-                        ref[share ^ parity, r, step * 4 + pair * 2 + 1, rows, :] = odd[rows]
+                        ref[share ^ parity ^ core, r, step * 4 + pair * 2, rows, :] = even[rows]
+                        ref[share ^ parity ^ core, r, step * 4 + pair * 2 + 1, rows, :] = odd[rows]
         return carry
 
     lax.fori_loop(0, 4, columns, 0)
 
 
-def early_kernel(weight, p0, p1, p2, q00, q01, q10, q11, keep, send, right, left):
+def product_kernel(weight, p0, p3, q11, q10, q01, q00, p2, p1, keep, send, right, left):
     ylo, yhi = lax.axis_index("ylo"), lax.axis_index("yhi")
     planes = right.shape[0]
     for (s, t), block in zip(FLIPS, (q00, q01, q10, q11)):
@@ -138,39 +138,23 @@
             return carry
 
         lax.fori_loop(0, planes, move, 0)
-    for shift, block in enumerate((p0, p1, p2)):
-        scaled_rows(left, shift, weight, (block,))
-    multiply(left, right, keep, send, {0: (0, 1), 1: (2, None)})
-
-
-def late_kernel(weight, p3, right, keep_in, send_in, keep, send, left):
-    del keep_in, send_in
-    scaled_rows(left, 0, weight, (p3,))
-    multiply(left, right, keep, send, {1: (None, 0)})
-
-
-def product(kernel, shifts, weight, *blocks):
+    core = lax.axis_index("core")
+    for slot, block in ((2 * core, p0), (1, p1), (2 - 2 * core, p2), (3, p3)):
+        scaled_rows(left, slot, weight, (block,))
+    multiply(left, right, keep, send, {0: (0, 1), 1: (2, 3)})
+
+
+def product(weight, *blocks):
     depth = blocks[0].shape[1]
-    planes = 16
     whole = pl.BlockSpec(memory_space=pltpu.VMEM)
-    packed = jax.ShapeDtypeStruct((planes, 4, 16, depth), jnp.bfloat16)
-    results = [jax.ShapeDtypeStruct((2, planes, planes, 8, 128), jnp.float32)] * 2
-    aliases = {}
-    if kernel is early_kernel:
-        results.append(packed)
-    else:
-        aliases = {len(blocks) - 1: 0, len(blocks): 1}
-    return pl.pallas_call(
-        kernel,
-        in_specs=[whole] * (1 + len(blocks)),
-        out_specs=[whole] * len(results),
-        out_shape=results,
-        scratch_shapes=[pltpu.VMEM((planes, shifts, 16, depth), jnp.bfloat16)],
-        input_output_aliases=aliases,
+    return pl.pallas_call(
+        product_kernel,
+        in_specs=[whole] * 9,
+        out_specs=[whole] * 2,
+        out_shape=[jax.ShapeDtypeStruct((2, 16, 16, 8, 128), jnp.float32)] * 2,
+        scratch_shapes=[pltpu.VMEM((16, 4, 16, depth), jnp.bfloat16)] * 2,
         compiler_params=pltpu.CompilerParams(vmem_limit_bytes=VMEM_LIMIT),
-        cost_estimate=pl.CostEstimate(
-            flops=1, bytes_accessed=1, transcendentals=0
-        ),
+        cost_estimate=pl.CostEstimate(flops=1, bytes_accessed=1, transcendentals=0),
     )(weight, *blocks)
 
 
@@ -229,6 +213,11 @@
     ]
 
 
+def ring_steps(shift):
+    sign = (1, -1)
+    return [(x * 2 + core, (x + sign[core] * shift) % 4 * 2 + core) for x in range(4) for core in range(2)]
+
+
 def neighbour_planes():
     other = lambda z, core: ((z + core) ^ 1) - core
     return [(z * 2 + core, other(z, core) % 16 * 2 + core) for z in range(16) for core in range(2)]
@@ -249,9 +238,7 @@
     rows = planes.reshape(-1, planes.shape[2])
 
     own = lax.ppermute(rows, Y_RING, ring_permutation(0, 0))
-    step, opposite, back = [
-        lax.ppermute(own, "x", [(i, (i + shift) % 4) for i in range(4)]) for shift in (1, 2, 3)
-    ]
+    step, opposite, back = [lax.ppermute(own, ("x", "core"), ring_steps(shift)) for shift in (1, 2, 3)]
     q_blocks = [
         own,
         lax.ppermute(own, Y_RING, flip_permutation(0, 1)),
@@ -261,8 +248,7 @@
     weight = weights(occ_index, occ_energies, freq_grid, freq_index, virt_energies, virt_index, rows)
     weight = lax.ppermute(weight, Y_RING, ring_permutation(0, 0))
 
-    keep, send, right = product(early_kernel, 3, weight, own, step, opposite, *q_blocks)
-    keep, send = product(late_kernel, 1, weight, back, right, keep, send)
+    keep, send = product(weight, own, back, *q_blocks[::-1], opposite, step)
     got = lax.ppermute(send, "core", [(0, 1), (1, 0)])
     passed = lax.ppermute(encode(keep[1] + got[1]), ("z", "core"), neighbour_planes())
     pairs = encode(keep[0] + got[0] + decode(passed))

time: 191 us -> 191 us (level)
  starting transfers between devices: 44.2 us -> 40.9 us
  waiting for transfers between devices: 38.1 us -> 41.3 us
  blocking collectives: 94.2 us -> 96.6 us
    ppermute x1, waiting for transfers between devices: 0.01 us -> 6.23 us  [body(): lax.ppermute(own, Y_RING, flip_permutation(1, 1))]
    ppermute x3, waiting for transfers between devices: 15.6 us -> 10.9 us  [body(): lax.ppermute(own, ('x', 'core'), ring_steps(shift))]
    all_to_all x1, blocking collectives: 43.7 us -> 46.1 us  [body(): lax.all_to_all(pairs.reshape(256, 8, 128), ('z', 'ylo', 'x', 'core'), spl...]
    pallas_call x2 -> x1, Pallas kernels: 6.75 us -> 5.62 us  [product(): pl.pallas_call(product_kernel, in_specs=[whole] * 9, out_specs=[whole] *...]
  transfers between devices with their start and end apart: 11 -> 11, of which waited for: 6 -> 7; matrix products, arithmetic and copies ran while one was open for 0% -> 0% of each run, Pallas kernels for 3% -> 0%
where the time goes in v7:
time: 191 us; the launch traced here: 190 us
  blocking collectives  96.6 us (51%)
  waiting for transfers between devices  41.3 us (22%)
  starting transfers between devices  40.9 us (21%)
  Pallas kernels  7.68 us (4%)
    all_to_all x1, blocking collectives, body(): lax.all_to_all(pack(factors), 'z', split_axis=0, concat_axis=0, tiled=True)  50.5 us
    all_to_all x1, blocking collectives, body(): lax.all_to_all(pairs.reshape(256, 8, 128), ('z', 'ylo', 'x', 'core'), spl...  46.1 us
    ppermute x1, starting transfers between devices, body(): own = lax.ppermute(rows, Y_RING, ring_permutation(0, 0))  12.1 us
    ppermute x3, waiting for transfers between devices, body(): lax.ppermute(own, ('x', 'core'), ring_steps(shift))  10.9 us
    ppermute x1, waiting for transfers between devices, body(): own = lax.ppermute(rows, Y_RING, ring_permutation(0, 0))  9.38 us
    ppermute x3, starting transfers between devices, body(): lax.ppermute(own, ('x', 'core'), ring_steps(shift))  9.32 us
    ppermute x1, waiting for transfers between devices, body(): lax.ppermute(encode(keep[1] + got[1]), ('z', 'core'), neighbour_planes())  6.95 us
    ppermute x1, waiting for transfers between devices, body(): lax.ppermute(own, Y_RING, flip_permutation(1, 1))  6.23 us
  transfers between devices with their start and end apart: 11, of which 7 were waited for; matrix products, arithmetic and copies ran while one was open for 0% of the time, Pallas kernels for 0%

profile of v7, /device:TPU:1, one launch (start us, length us, event | category | flops | bytes accessed | tf_op | source)
XLA Modules:
  0.0 189.9 jit_solution(5639426377541092510)
XLA Ops:
  0.0 1.1 copy-done
  1.2 0.1 shard_map.73
  1.2 50.5 %all_to_all.10 = bf16[16,16,1536]{2,1,0:T(8,128)(2,1)S(1)} all-to-all(bf16[16,16,1536]{2,1,0:T(8,128)(2,1)S(1)} %shard_map.73), channel_id=1, replica_groups=mesh['z'=16,'ylo'=2,'x'=4,'core'=2,'yhi'=2] {'z'}, dimensions={0} | all-to-all | bytes 1572864 | tf_op jit(solution)/shard_map/all_to_all | solution.py:237
  51.7 12.1 %collective-permute-start.1 = (bf16[256,1536]{1,0:T(8,128)(2,1)S(1)}, bf16[256,1536]{1,0:T(8,128)(2,1)S(1)}, u32[]{:S(2)}, u32[]{:S(2)}) collective-permute-start(bf16[256,1536]{1,0:T(8,128)(2,1)S(1)} %bitcast.15), channel_id=1, source_target_pairs={{0,0},{1,2},{2,1},{3,3},{16,16},{17,18},{18,17},{19,19},{4,4},{5,6... | collective-permute-start | bytes 2359304 | tf_op jit(solution)/shard_map/ppermute | solution.py:240
  63.8 1.9 %collective-permute-start.4 = (bf16[256,1536]{1,0:T(8,128)(2,1)S(1)}, bf16[256,1536]{1,0:T(8,128)(2,1)S(1)}, u32[]{:S(2)}, u32[]{:S(2)}) collective-permute-start(bf16[256,1536]{1,0:T(8,128)(2,1)S(1)} %bitcast.16), channel_id=1, source_target_pairs={{0,1},{1,3},{2,0},{3,2},{16,17},{17,19},{18,16},{19,18},{4,5},{5,7... | collective-permute-start | bytes 2359304 | tf_op jit(solution)/shard_map/ppermute | solution.py:245
  66.4 0.8 shard_map.74
  67.2 1.9 %collective-permute-start = (f32[1,1536]{1,0:T(1,128)S(1)}, f32[1,1536]{1,0:T(1,128)S(1)}, u32[]{:S(2)}, u32[]{:S(2)}) collective-permute-start(f32[1,1536]{1,0:T(1,128)S(1)} %shard_map.74), channel_id=1, source_target_pairs={{0,0},{1,2},{2,1},{3,3},{16,16},{17,18},{18,17},{19,19},{4,4},{5,6... | collective-permute-start | bytes 18440 | tf_op jit(solution)/shard_map/ppermute | solution.py:249
  69.1 9.4 %collective-permute-done.1.p0.q00 = bf16[256,1536]{1,0:T(8,128)(2,1)S(1)} collective-permute-done((bf16[256,1536]{1,0:T(8,128)(2,1)S(1)}, bf16[256,1536]{1,0:T(8,128)(2,1)S(1)}, u32[]{:S(2)}, u32[]{:S(2)}) %collective-permute-start.1) | collective-permute-done | bytes 786464 | tf_op jit(solution)/shard_map/ppermute | solution.py:240
  78.5 4.4 %collective-permute-start.7 = (bf16[256,1536]{1,0:T(8,128)(2,1)S(1)}, bf16[256,1536]{1,0:T(8,128)(2,1)S(1)}, u32[]{:S(2)}, u32[]{:S(2)}) collective-permute-start(bf16[256,1536]{1,0:T(8,128)(2,1)S(1)} %collective-permute-done.1.p0.q00), channel_id=1, source_target_pairs={{0,4},{2,14},{4,8},{6,2},{8,12},{10,6},{12,0},{14,10},{1,5},{3,15}... | collective-permute-start | bytes 2359304 | tf_op jit(solution)/shard_map/ppermute | solution.py:241
  82.9 2.4 %collective-permute-start.6 = (bf16[256,1536]{1,0:T(8,128)(2,1)S(1)}, bf16[256,1536]{1,0:T(8,128)(2,1)S(1)}, u32[]{:S(2)}, u32[]{:S(2)}) collective-permute-start(bf16[256,1536]{1,0:T(8,128)(2,1)S(1)} %collective-permute-done.1.p0.q00), channel_id=1, source_target_pairs={{0,8},{2,10},{4,12},{6,14},{8,0},{10,2},{12,4},{14,6},{1,9},{3,11}... | collective-permute-start | bytes 2359304 | tf_op jit(solution)/shard_map/ppermute | solution.py:241
  85.3 2.3 %collective-permute-start.5 = (bf16[256,1536]{1,0:T(8,128)(2,1)S(1)}, bf16[256,1536]{1,0:T(8,128)(2,1)S(1)}, u32[]{:S(2)}, u32[]{:S(2)}) collective-permute-start(bf16[256,1536]{1,0:T(8,128)(2,1)S(1)} %collective-permute-done.1.p0.q00), channel_id=1, source_target_pairs={{0,16},{1,17},{2,18},{3,19},{16,0},{17,1},{18,2},{19,3},{4,20},{5,... | collective-permute-start | bytes 2359304 | tf_op jit(solution)/shard_map/ppermute | solution.py:244
  87.7 0.0 collective-permute-done.weight
  87.7 1.9 %collective-permute-start.3 = (bf16[256,1536]{1,0:T(8,128)(2,1)S(1)}, bf16[256,1536]{1,0:T(8,128)(2,1)S(1)}, u32[]{:S(2)}, u32[]{:S(2)}) collective-permute-start(bf16[256,1536]{1,0:T(8,128)(2,1)S(1)} %collective-permute-done.1.p0.q00), channel_id=1, source_target_pairs={{0,17},{1,16},{2,19},{3,18},{16,1},{17,0},{18,3},{19,2},{4,21},{5,... | collective-permute-start | bytes 2359304 | tf_op jit(solution)/shard_map/ppermute | solution.py:246
  89.6 0.0 collective-permute-done.4.q10
  89.6 2.5 %collective-permute-start.2 = (bf16[256,1536]{1,0:T(8,128)(2,1)S(1)}, bf16[256,1536]{1,0:T(8,128)(2,1)S(1)}, u32[]{:S(2)}, u32[]{:S(2)}) collective-permute-start(bf16[256,1536]{1,0:T(8,128)(2,1)S(1)} %collective-permute-done.1.p0.q00), channel_id=1, source_target_pairs={{0,12},{2,6},{4,0},{6,10},{8,4},{10,14},{12,8},{14,2},{1,13},{3,7}... | collective-permute-start | bytes 2359304 | tf_op jit(solution)/shard_map/ppermute | solution.py:241
  92.1 8.9 %collective-permute-done.7.p1 = bf16[256,1536]{1,0:T(8,128)(2,1)S(1)} collective-permute-done((bf16[256,1536]{1,0:T(8,128)(2,1)S(1)}, bf16[256,1536]{1,0:T(8,128)(2,1)S(1)}, u32[]{:S(2)}, u32[]{:S(2)}) %collective-permute-start.7) | collective-permute-done | bytes 786464 | tf_op jit(solution)/shard_map/ppermute | solution.py:241
  101.0 0.0 collective-permute-done.6.p2
  101.0 6.2 %collective-permute-done.3.q11 = bf16[256,1536]{1,0:T(8,128)(2,1)S(1)} collective-permute-done((bf16[256,1536]{1,0:T(8,128)(2,1)S(1)}, bf16[256,1536]{1,0:T(8,128)(2,1)S(1)}, u32[]{:S(2)}, u32[]{:S(2)}) %collective-permute-start.3) | collective-permute-done | bytes 786464 | tf_op jit(solution)/shard_map/ppermute | solution.py:246
  107.3 2.0 %collective-permute-done.2.p3 = bf16[256,1536]{1,0:T(8,128)(2,1)S(1)} collective-permute-done((bf16[256,1536]{1,0:T(8,128)(2,1)S(1)}, bf16[256,1536]{1,0:T(8,128)(2,1)S(1)}, u32[]{:S(2)}, u32[]{:S(2)}) %collective-permute-start.2) | collective-permute-done | bytes 786464 | tf_op jit(solution)/shard_map/ppermute | solution.py:241
  109.3 5.6 %shard_map.75 = (f32[2,16,16,8,128]{4,3,2,1,0:T(8,128)S(1)}, f32[2,16,16,8,128]{4,3,2,1,0:T(8,128)S(1)}) custom-call(f32[1,1536]{1,0:T(1,128)S(1)} %collective-permute-done.weight, bf16[256,1536]{1,0:T(8,128)(2,1)S(1)} %collective-permute-done.1.p0.q00, bf16[256,1536]{1,0:T(8,128)(2,1)S(1)} %collective-permute-done.2.p3, ...), custom_call_target="tpu_custom_call" | custom-call | flops 1 | bytes 1 | tf_op jit(solution)/shard_map/pallas_call | solution.py:150
  114.9 4.1 %collective-permute-start.8 = (f32[2,16,16,8,128]{4,3,2,1,0:T(8,128)S(1)}, f32[2,16,16,8,128]{4,3,2,1,0:T(8,128)S(1)}, u32[]{:S(2)}, u32[]{:S(2)}) collective-permute-start(f32[2,16,16,8,128]{4,3,2,1,0:T(8,128)S(1)} %get-tuple-element.8), channel_id=1, source_target_pairs={{0,2},{2,0},{1,3},{3,1},{4,6},{6,4},{5,7},{7,5},{8,10},{10,8},{9,1... | collective-permute-start | bytes 6291464 | tf_op jit(solution)/shard_map/ppermute | solution.py:252
  119.0 3.8 %collective-permute-done.8 = f32[2,16,16,8,128]{4,3,2,1,0:T(8,128)S(1)} collective-permute-done((f32[2,16,16,8,128]{4,3,2,1,0:T(8,128)S(1)}, f32[2,16,16,8,128]{4,3,2,1,0:T(8,128)S(1)}, u32[]{:S(2)}, u32[]{:S(2)}) %collective-permute-start.8) | collective-permute-done | bytes 2097184 | tf_op jit(solution)/shard_map/ppermute | solution.py:252
  122.8 0.5 fusion
  123.3 4.2 %collective-permute-start.9 = (f16[16,16,8,128]{3,2,1,0:T(8,128)(2,1)S(1)}, f16[16,16,8,128]{3,2,1,0:T(8,128)(2,1)S(1)}, u32[]{:S(2)}, u32[]{:S(2)}) collective-permute-start(f16[16,16,8,128]{3,2,1,0:T(8,128)(2,1)S(1)} %fusion), channel_id=1, source_target_pairs={{0,32},{2,482},{32,0},{34,66},{64,96},{66,34},{96,64},{98,130},{12... | collective-permute-start | bytes 1572872 | tf_op jit(solution)/shard_map/ppermute | solution.py:253
  127.5 7.0 %collective-permute-done.9 = f16[16,16,8,128]{3,2,1,0:T(8,128)(2,1)S(1)} collective-permute-done((f16[16,16,8,128]{3,2,1,0:T(8,128)(2,1)S(1)}, f16[16,16,8,128]{3,2,1,0:T(8,128)(2,1)S(1)}, u32[]{:S(2)}, u32[]{:S(2)}) %collective-permute-start.9) | collective-permute-done | bytes 524320 | tf_op jit(solution)/shard_map/ppermute | solution.py:253
  134.4 0.7 fusion.3
  135.1 46.1 %all_to_all.11 = f16[256,8,128]{2,1,0:T(8,128)(2,1)S(1)} all-to-all(f16[256,8,128]{2,1,0:T(8,128)(2,1)S(1)} %bitcast.21), channel_id=1, replica_groups=mesh['z'=16,'ylo'=2,'x'=4,'core'=2,'yhi'=2] {'z','ylo','x','core'}, dimensions={0} | all-to-all | bytes 1048576 | tf_op jit(solution)/shard_map/all_to_all | solution.py:255
  181.3 0.2 fusion.4
  181.4 0.1 reduce_sum.9.mine
  181.5 3.1 %collective-permute-start.10 = (f32[2,16,8,128]{3,2,1,0:T(8,128)S(1)}, f32[2,16,8,128]{3,2,1,0:T(8,128)S(1)}, u32[]{:S(2)}, u32[]{:S(2)}) collective-permute-start(f32[2,16,8,128]{3,2,1,0:T(8,128)S(1)} %reduce_sum.9.mine), channel_id=1, source_target_pairs={{0,1},{1,0},{2,3},{3,2},{4,5},{5,4},{6,7},{7,6},{8,9},{9,8},{10,11... | collective-permute-start | bytes 393224 | tf_op jit(solution)/shard_map/ppermute | solution.py:259
  184.6 4.1 %collective-permute-done.10.other = f32[2,16,8,128]{3,2,1,0:T(8,128)S(1)} collective-permute-done((f32[2,16,8,128]{3,2,1,0:T(8,128)S(1)}, f32[2,16,8,128]{3,2,1,0:T(8,128)S(1)}, u32[]{:S(2)}, u32[]{:S(2)}) %collective-permute-start.10) | collective-permute-done | bytes 131104 | tf_op jit(solution)/shard_map/ppermute | solution.py:259
  188.7 1.2 shard_map.76
  (12 shorter events, 0.0 us)
Async XLA Ops:
  0.0 1.1 copy-start
  1.1 65.2 %copy-start.1 = (f32[3072]{0:T(1024)S(1)}, f32[3072]{0:T(1024)}, u32[]{:S(2)}) copy-start(f32[3072]{0:T(1024)} %param.9) | copy-start | bytes 36868
  1.1 65.2 %copy-start.2 = (s32[3072]{0:T(1024)S(1)}, s32[3072]{0:T(1024)}, u32[]{:S(2)}) copy-start(s32[3072]{0:T(1024)} %param.12) | copy-start | bytes 36868
  1.1 65.2 %copy-start.3 = (f32[300]{0:T(512)S(1)}, f32[300]{0:T(512)}, u32[]{:S(2)}) copy-start(f32[300]{0:T(512)} %occ.1) | copy-start | bytes 3604
  1.1 65.2 %copy-start.4 = (s32[8]{0:T(128)S(1)}, s32[8]{0:T(128)}, u32[]{:S(2)}) copy-start(s32[8]{0:T(128)} %occ_index.1) | copy-start | bytes 100
  1.1 65.2 %copy-start.5 = (f32[32]{0:T(128)S(1)}, f32[32]{0:T(128)}, u32[]{:S(2)}) copy-start(f32[32]{0:T(128)} %freq.1) | copy-start | bytes 388
  51.7 26.8 %collective-permute-start.1 = (bf16[256,1536]{1,0:T(8,128)(2,1)S(1)}, bf16[256,1536]{1,0:T(8,128)(2,1)S(1)}, u32[]{:S(2)}, u32[]{:S(2)}) collective-permute-start(bf16[256,1536]{1,0:T(8,128)(2,1)S(1)} %bitcast.15), channel_id=1, source_target_pairs={{0,0},{1,2},{2,1},{3,3},{16,16},{17,18},{18,17},{19,19},{4,4},{5,6... | collective-permute-start | bytes 2359304 | tf_op jit(solution)/shard_map/ppermute | solution.py:240
  63.8 25.8 %collective-permute-start.4 = (bf16[256,1536]{1,0:T(8,128)(2,1)S(1)}, bf16[256,1536]{1,0:T(8,128)(2,1)S(1)}, u32[]{:S(2)}, u32[]{:S(2)}) collective-permute-start(bf16[256,1536]{1,0:T(8,128)(2,1)S(1)} %bitcast.16), channel_id=1, source_target_pairs={{0,1},{1,3},{2,0},{3,2},{16,17},{17,19},{18,16},{19,18},{4,5},{5,7... | collective-permute-start | bytes 2359304 | tf_op jit(solution)/shard_map/ppermute | solution.py:245
  67.2 20.4 %collective-permute-start = (f32[1,1536]{1,0:T(1,128)S(1)}, f32[1,1536]{1,0:T(1,128)S(1)}, u32[]{:S(2)}, u32[]{:S(2)}) collective-permute-start(f32[1,1536]{1,0:T(1,128)S(1)} %shard_map.74), channel_id=1, source_target_pairs={{0,0},{1,2},{2,1},{3,3},{16,16},{17,18},{18,17},{19,19},{4,4},{5,6... | collective-permute-start | bytes 18440 | tf_op jit(solution)/shard_map/ppermute | solution.py:249
  78.5 22.5 %collective-permute-start.7 = (bf16[256,1536]{1,0:T(8,128)(2,1)S(1)}, bf16[256,1536]{1,0:T(8,128)(2,1)S(1)}, u32[]{:S(2)}, u32[]{:S(2)}) collective-permute-start(bf16[256,1536]{1,0:T(8,128)(2,1)S(1)} %collective-permute-done.1.p0.q00), channel_id=1, source_target_pairs={{0,4},{2,14},{4,8},{6,2},{8,12},{10,6},{12,0},{14,10},{1,5},{3,15}... | collective-permute-start | bytes 2359304 | tf_op jit(solution)/shard_map/ppermute | solution.py:241
  82.9 18.1 %collective-permute-start.6 = (bf16[256,1536]{1,0:T(8,128)(2,1)S(1)}, bf16[256,1536]{1,0:T(8,128)(2,1)S(1)}, u32[]{:S(2)}, u32[]{:S(2)}) collective-permute-start(bf16[256,1536]{1,0:T(8,128)(2,1)S(1)} %collective-permute-done.1.p0.q00), channel_id=1, source_target_pairs={{0,8},{2,10},{4,12},{6,14},{8,0},{10,2},{12,4},{14,6},{1,9},{3,11}... | collective-permute-start | bytes 2359304 | tf_op jit(solution)/shard_map/ppermute | solution.py:241
  85.3 15.7 %collective-permute-start.5 = (bf16[256,1536]{1,0:T(8,128)(2,1)S(1)}, bf16[256,1536]{1,0:T(8,128)(2,1)S(1)}, u32[]{:S(2)}, u32[]{:S(2)}) collective-permute-start(bf16[256,1536]{1,0:T(8,128)(2,1)S(1)} %collective-permute-done.1.p0.q00), channel_id=1, source_target_pairs={{0,16},{1,17},{2,18},{3,19},{16,0},{17,1},{18,2},{19,3},{4,20},{5,... | collective-permute-start | bytes 2359304 | tf_op jit(solution)/shard_map/ppermute | solution.py:244
  87.7 19.6 %collective-permute-start.3 = (bf16[256,1536]{1,0:T(8,128)(2,1)S(1)}, bf16[256,1536]{1,0:T(8,128)(2,1)S(1)}, u32[]{:S(2)}, u32[]{:S(2)}) collective-permute-start(bf16[256,1536]{1,0:T(8,128)(2,1)S(1)} %collective-permute-done.1.p0.q00), channel_id=1, source_target_pairs={{0,17},{1,16},{2,19},{3,18},{16,1},{17,0},{18,3},{19,2},{4,21},{5,... | collective-permute-start | bytes 2359304 | tf_op jit(solution)/shard_map/ppermute | solution.py:246
  89.6 19.6 %collective-permute-start.2 = (bf16[256,1536]{1,0:T(8,128)(2,1)S(1)}, bf16[256,1536]{1,0:T(8,128)(2,1)S(1)}, u32[]{:S(2)}, u32[]{:S(2)}) collective-permute-start(bf16[256,1536]{1,0:T(8,128)(2,1)S(1)} %collective-permute-done.1.p0.q00), channel_id=1, source_target_pairs={{0,12},{2,6},{4,0},{6,10},{8,4},{10,14},{12,8},{14,2},{1,13},{3,7}... | collective-permute-start | bytes 2359304 | tf_op jit(solution)/shard_map/ppermute | solution.py:241
  114.9 7.9 %collective-permute-start.8 = (f32[2,16,16,8,128]{4,3,2,1,0:T(8,128)S(1)}, f32[2,16,16,8,128]{4,3,2,1,0:T(8,128)S(1)}, u32[]{:S(2)}, u32[]{:S(2)}) collective-permute-start(f32[2,16,16,8,128]{4,3,2,1,0:T(8,128)S(1)} %get-tuple-element.8), channel_id=1, source_target_pairs={{0,2},{2,0},{1,3},{3,1},{4,6},{6,4},{5,7},{7,5},{8,10},{10,8},{9,1... | collective-permute-start | bytes 6291464 | tf_op jit(solution)/shard_map/ppermute | solution.py:252
  123.3 11.1 %collective-permute-start.9 = (f16[16,16,8,128]{3,2,1,0:T(8,128)(2,1)S(1)}, f16[16,16,8,128]{3,2,1,0:T(8,128)(2,1)S(1)}, u32[]{:S(2)}, u32[]{:S(2)}) collective-permute-start(f16[16,16,8,128]{3,2,1,0:T(8,128)(2,1)S(1)} %fusion), channel_id=1, source_target_pairs={{0,32},{2,482},{32,0},{34,66},{64,96},{66,34},{96,64},{98,130},{12... | collective-permute-start | bytes 1572872 | tf_op jit(solution)/shard_map/ppermute | solution.py:253
  181.5 7.2 %collective-permute-start.10 = (f32[2,16,8,128]{3,2,1,0:T(8,128)S(1)}, f32[2,16,8,128]{3,2,1,0:T(8,128)S(1)}, u32[]{:S(2)}, u32[]{:S(2)}) collective-permute-start(f32[2,16,8,128]{3,2,1,0:T(8,128)S(1)} %reduce_sum.9.mine), channel_id=1, source_target_pairs={{0,1},{1,0},{2,3},{3,2},{4,5},{5,4},{6,7},{7,6},{8,9},{9,8},{10,11... | collective-permute-start | bytes 393224 | tf_op jit(solution)/shard_map/ppermute | solution.py:259
